TPU v7x, 256 devices: a whole 4x4x8 slice. The times are simulated.
256 devices in a mesh: rad: 4 (over y), az: 64 (over x, z, core).
Axes of the slice: x: 4, y: 4, z: 8, core: 2. Of those that a mesh axis runs over, the one named last changes fastest.
Arguments:
- fields: float32 [2, 1, 1024, 8192], P(None, None, 'rad', 'az'), may hold values from -6 to 6
- whole_shift: int32 [1024], P('rad'), may hold values from -2048 to 2047
- frac_shift: float32 [1024], P('rad'), may hold values from -0.5 to 0.5
- inv_spacing: float32 [1024], P('rad'), may hold values from 0.5 to 2
Outputs:
- remapped: float32 [2, 1, 1024, 8192], P(None, None, 'rad', 'az')
- radial_derivative: float32 [2, 1, 1024, 8192], P(None, None, 'rad', 'az')
All inputs are finite; a program needn't handle non-finite values.
Results may differ from a plain program's by a relative error of at most 0.0001.
Values sent between devices are 32-bit elements; how exact they have to be, the bound alone decides.
No kernel may reach another device: no remote copies, remote signals or barrier semaphores. Data moves between devices by JAX's collectives and lax.ppermute only.
A program may use at most 256 MiB of HBM per device.

v0:
```python
import math

import jax
import jax.numpy as jnp
from jax import lax
from jax.sharding import PartitionSpec as P

BLOCK = 128


HIGHEST = lax.Precision.HIGHEST


def partner_2(x, axis, apart):
    return lax.ppermute(x, axis, [(i, i ^ 1 << apart) for i in range(lax.axis_size(axis))])


def extended(cells, sides, width):
    for axis, dim in sides:
        count = lax.axis_size(axis)
        ends = count - 1
        head = lax.slice_in_dim(cells, 0, width, axis=dim)
        tail = lax.slice_in_dim(cells, cells.shape[dim] - width, cells.shape[dim], axis=dim)
        cells = jnp.concatenate(
            [
                lax.ppermute(tail, axis, [(i, (i + 1) % count) for i in range(ends)]),
                cells,
                lax.ppermute(head, axis, [((i + 1) % count, i) for i in range(ends)]),
            ],
            axis=dim,
        )
    return cells


def compact_inverse(size):
    identity = jnp.eye(size, dtype=jnp.float32)
    offdiag = 0.25 * (
        jnp.eye(size, k=1, dtype=jnp.float32) + jnp.eye(size, k=-1, dtype=jnp.float32)
    )
    inverse = identity - offdiag
    power = offdiag
    for square_step in range(5):
        power = jnp.dot(power, power, precision=HIGHEST)
        inverse = jnp.dot(inverse, identity + power, precision=HIGHEST)
    return inverse


def reverse_bits(number, nbits):
    result = 0
    for bit_place in range(nbits):
        result = result + ((number >> bit_place & 1) << nbits - 1 - bit_place)
    return result


def rotate(signal, turn_angle):
    cosine = jnp.cos(turn_angle)
    sine = jnp.sin(turn_angle)
    return jnp.stack([signal[0] * cosine - signal[1] * sine, signal[0] * sine + signal[1] * cosine])


def local_transform(signal, cosine_table, sine_table):
    real_cos = jnp.einsum("fzxj,jm->fzxm", signal[0], cosine_table, precision=HIGHEST)
    real_sin = jnp.einsum("fzxj,jm->fzxm", signal[0], sine_table, precision=HIGHEST)
    imag_cos = jnp.einsum("fzxj,jm->fzxm", signal[1], cosine_table, precision=HIGHEST)
    imag_sin = jnp.einsum("fzxj,jm->fzxm", signal[1], sine_table, precision=HIGHEST)
    return jnp.stack([real_cos - imag_sin, real_sin + imag_cos])


def forward_across(fields):
    groups = lax.axis_size("az")
    position = lax.axis_index("az")
    nbits = groups.bit_length() - 1
    signal = jnp.stack([fields, jnp.zeros_like(fields)])
    for section_bit in reversed(range(nbits)):
        half_span = 1 << section_bit
        partner = partner_2(signal, "az", section_bit)
        is_upper = position >> section_bit & 1 == 1
        offset = (position & half_span - 1).astype(jnp.float32)
        twisted = rotate(partner - signal, -2.0 * math.pi * offset / (2 * half_span))
        signal = jnp.where(is_upper, twisted, signal + partner)
    return signal


def inverse_across(signal):
    groups = lax.axis_size("az")
    position = lax.axis_index("az")
    nbits = groups.bit_length() - 1
    for section_bit in range(nbits):
        half_span = 1 << section_bit
        is_upper = position >> section_bit & 1 == 1
        offset = (position & half_span - 1).astype(jnp.float32)
        sent = jnp.where(is_upper, rotate(signal, 2.0 * math.pi * offset / (2 * half_span)), signal)
        partner = partner_2(sent, "az", section_bit)
        signal = 0.5 * jnp.where(is_upper, partner - sent, sent + partner)
    return signal[0]


def shear_phase(signal, signed, total, shift_whole, shift_frac):
    phase_turns = jnp.mod(signed * shift_whole, total).astype(jnp.float32)
    phase_turns = phase_turns + signed.astype(jnp.float32) * shift_frac
    return rotate(signal, -(2.0 * math.pi / total) * phase_turns)


def on_device(fields, whole_shift, frac_shift, inv_spacing):
    groups = lax.axis_size("az")
    position = lax.axis_index("az")
    nbits = groups.bit_length() - 1
    field_count, plane_count, row_count, width = fields.shape
    total = width * groups
    flipped = reverse_bits(position, nbits)
    signal = forward_across(fields)
    column = jnp.arange(width, dtype=jnp.int32)
    twist = 2.0 * math.pi / total * jnp.mod(column * flipped, total).astype(jnp.float32)
    signal = rotate(signal, -twist)
    grid_angle = (
        2.0
        * math.pi
        / width
        * jnp.mod(column[:, None] * column[None, :], width).astype(jnp.float32)
    )
    cosine_table = jnp.cos(grid_angle)
    sine_table = jnp.sin(grid_angle)
    signal = local_transform(signal, cosine_table, -sine_table)
    wavenumber = flipped + groups * column
    signed = jnp.where(wavenumber < total // 2, wavenumber, wavenumber - total)
    signal = shear_phase(signal, signed[None, :], total, whole_shift[:, None], frac_shift[:, None])
    signal = local_transform(signal, cosine_table, sine_table) / width
    signal = rotate(signal, twist)
    remapped = inverse_across(signal)
    padded = extended(remapped, (("rad", 2),), 1)
    right_side = 0.75 * (padded[:, :, 2:] - padded[:, :, :-2]) * inv_spacing[:, None]
    blocks = right_side.reshape(field_count, plane_count, row_count // BLOCK, BLOCK, width)
    radial_derivative = jnp.einsum(
        "ab,fzgbl->fzgal", compact_inverse(BLOCK), blocks, precision=HIGHEST
    )
    return (remapped, radial_derivative.reshape(field_count, plane_count, row_count, width))


def solution(mesh):
    return jax.shard_map(
        on_device,
        mesh=mesh,
        in_specs=(P(None, None, "rad", "az"), P("rad"), P("rad"), P("rad")),
        out_specs=(P(None, None, "rad", "az"), P(None, None, "rad", "az")),
        check_vma=False,
    )
```

profile of v0, /device:TPU:1, one launch (start us, length us, event | category | flops | bytes accessed | tf_op | source)
XLA Modules:
  0.0 209.9 jit_solution(1132531095542716954)
XLA Ops:
  0.6 1.0 stack.37
  1.7 3.7 %collective-permute-start = (f32[2,2,1,256,128]{4,3,1,2,0:T(8,128)S(1)}, f32[2,2,1,256,128]{4,3,1,2,0:T(8,128)S(1)}, u32[]{:S(2)}, u32[]{:S(2)}) collective-permute-start(f32[2,2,1,256,128]{4,3,1,2,0:T(8,128)S(1)} %stack.37), channel_id=1, source_target_pairs={{0,32},{1,33},{2,34},{3,35},{4,36},{5,37},{6,38},{7,39},{8,40},{9,... | collective-permute-start | bytes 1572872 | tf_op jit(solution)/shard_map/ppermute | solution.py:15
  5.5 10.4 %collective-permute-done = f32[2,2,1,256,128]{4,3,1,2,0:T(8,128)S(1)} collective-permute-done((f32[2,2,1,256,128]{4,3,1,2,0:T(8,128)S(1)}, f32[2,2,1,256,128]{4,3,1,2,0:T(8,128)S(1)}, u32[]{:S(2)}, u32[]{:S(2)}) %collective-permute-start) | collective-permute-done | bytes 524320 | tf_op jit(solution)/shard_map/ppermute | solution.py:15
  16.1 2.3 %collective-permute-start.1 = (f32[2,2,1,256,128]{4,3,1,2,0:T(8,128)S(1)}, f32[2,2,1,256,128]{4,3,1,2,0:T(8,128)S(1)}, u32[]{:S(2)}, u32[]{:S(2)}) collective-permute-start(f32[2,2,1,256,128]{4,3,1,2,0:T(8,128)S(1)} %maximum_select_fusion), channel_id=1, source_target_pairs={{0,16},{1,17},{2,18},{3,19},{4,20},{5,21},{6,22},{7,23},{8,24},{9,... | collective-permute-start | bytes 1572872 | tf_op jit(solution)/shard_map/ppermute | solution.py:15
  18.6 10.2 %collective-permute-done.1 = f32[2,2,1,256,128]{4,3,1,2,0:T(8,128)S(1)} collective-permute-done((f32[2,2,1,256,128]{4,3,1,2,0:T(8,128)S(1)}, f32[2,2,1,256,128]{4,3,1,2,0:T(8,128)S(1)}, u32[]{:S(2)}, u32[]{:S(2)}) %collective-permute-start.1) | collective-permute-done | bytes 524320 | tf_op jit(solution)/shard_map/ppermute | solution.py:15
  29.1 7.3 %collective-permute-start.2 = (f32[2,2,1,256,128]{4,3,1,2,0:T(8,128)S(1)}, f32[2,2,1,256,128]{4,3,1,2,0:T(8,128)S(1)}, u32[]{:S(2)}, u32[]{:S(2)}) collective-permute-start(f32[2,2,1,256,128]{4,3,1,2,0:T(8,128)S(1)} %maximum_select_fusion.1), channel_id=1, source_target_pairs={{0,8},{1,9},{2,10},{3,11},{4,12},{5,13},{6,14},{7,15},{8,0},{9,1},... | collective-permute-start | bytes 1572872 | tf_op jit(solution)/shard_map/ppermute | solution.py:15
  36.5 11.7 %collective-permute-done.2 = f32[2,2,1,256,128]{4,3,1,2,0:T(8,128)S(1)} collective-permute-done((f32[2,2,1,256,128]{4,3,1,2,0:T(8,128)S(1)}, f32[2,2,1,256,128]{4,3,1,2,0:T(8,128)S(1)}, u32[]{:S(2)}, u32[]{:S(2)}) %collective-permute-start.2) | collective-permute-done | bytes 524320 | tf_op jit(solution)/shard_map/ppermute | solution.py:15
  48.4 12.6 %collective-permute-start.3 = (f32[2,2,1,256,128]{4,3,1,2,0:T(8,128)S(1)}, f32[2,2,1,256,128]{4,3,1,2,0:T(8,128)S(1)}, u32[]{:S(2)}, u32[]{:S(2)}) collective-permute-start(f32[2,2,1,256,128]{4,3,1,2,0:T(8,128)S(1)} %maximum_select_fusion.2), channel_id=1, source_target_pairs={{0,4},{1,5},{2,6},{3,7},{4,0},{5,1},{6,2},{7,3},{8,12},{9,13},{10,... | collective-permute-start | bytes 1572872 | tf_op jit(solution)/shard_map/ppermute | solution.py:15
  61.2 23.4 %collective-permute-done.3 = f32[2,2,1,256,128]{4,3,1,2,0:T(8,128)S(1)} collective-permute-done((f32[2,2,1,256,128]{4,3,1,2,0:T(8,128)S(1)}, f32[2,2,1,256,128]{4,3,1,2,0:T(8,128)S(1)}, u32[]{:S(2)}, u32[]{:S(2)}) %collective-permute-start.3) | collective-permute-done | bytes 524320 | tf_op jit(solution)/shard_map/ppermute | solution.py:15
  85.0 12.8 %collective-permute-done.4 = f32[2,2,1,256,128]{4,3,1,2,0:T(8,128)S(1)} collective-permute-done((f32[2,2,1,256,128]{4,3,1,2,0:T(8,128)S(1)}, f32[2,2,1,256,128]{4,3,1,2,0:T(8,128)S(1)}, u32[]{:S(2)}, u32[]{:S(2)}) %collective-permute-start.4) | collective-permute-done | bytes 524320 | tf_op jit(solution)/shard_map/ppermute | solution.py:15
  98.1 1.4 collective-permute-start.5
  107.1 1.4 collective-permute-done.6
  109.1 13.0 %collective-permute-done.7 = f32[2,2,1,256,128]{4,3,1,2,0:T(8,128)S(1)} collective-permute-done((f32[2,2,1,256,128]{4,3,1,2,0:T(8,128)S(1)}, f32[2,2,1,256,128]{4,3,1,2,0:T(8,128)S(1)}, u32[]{:S(2)}, u32[]{:S(2)}) %collective-permute-start.7) | collective-permute-done | bytes 524320 | tf_op jit(solution)/shard_map/ppermute | solution.py:15
  122.9 25.2 %collective-permute-done.8 = f32[2,2,1,256,128]{4,3,1,2,0:T(8,128)S(1)} collective-permute-done((f32[2,2,1,256,128]{4,3,1,2,0:T(8,128)S(1)}, f32[2,2,1,256,128]{4,3,1,2,0:T(8,128)S(1)}, u32[]{:S(2)}, u32[]{:S(2)}) %collective-permute-start.8) | collective-permute-done | bytes 524320 | tf_op jit(solution)/shard_map/ppermute | solution.py:15
  148.4 4.0 %collective-permute-start.9 = (f32[2,2,1,256,128]{4,3,1,2,0:T(8,128)S(1)}, f32[2,2,1,256,128]{4,3,1,2,0:T(8,128)S(1)}, u32[]{:S(2)}, u32[]{:S(2)}) collective-permute-start(f32[2,2,1,256,128]{4,3,1,2,0:T(8,128)S(1)} %maximum_select_fusion.9), channel_id=1, source_target_pairs={{0,8},{1,9},{2,10},{3,11},{4,12},{5,13},{6,14},{7,15},{8,0},{9,1},... | collective-permute-start | bytes 1572872 | tf_op jit(solution)/shard_map/ppermute | solution.py:15
  153.2 23.4 %collective-permute-done.9 = f32[2,2,1,256,128]{4,3,1,2,0:T(8,128)S(1)} collective-permute-done((f32[2,2,1,256,128]{4,3,1,2,0:T(8,128)S(1)}, f32[2,2,1,256,128]{4,3,1,2,0:T(8,128)S(1)}, u32[]{:S(2)}, u32[]{:S(2)}) %collective-permute-start.9) | collective-permute-done | bytes 524320 | tf_op jit(solution)/shard_map/ppermute | solution.py:15
  176.8 1.3 collective-permute-start.10
  178.9 10.0 %collective-permute-done.10 = f32[2,2,1,256,128]{4,3,1,2,0:T(8,128)S(1)} collective-permute-done((f32[2,2,1,256,128]{4,3,1,2,0:T(8,128)S(1)}, f32[2,2,1,256,128]{4,3,1,2,0:T(8,128)S(1)}, u32[]{:S(2)}, u32[]{:S(2)}) %collective-permute-start.10) | collective-permute-done | bytes 524320 | tf_op jit(solution)/shard_map/ppermute | solution.py:15
  189.2 2.9 %collective-permute-start.11 = (f32[2,2,1,256,128]{4,3,1,2,0:T(8,128)S(1)}, f32[2,2,1,256,128]{4,3,1,2,0:T(8,128)S(1)}, u32[]{:S(2)}, u32[]{:S(2)}) collective-permute-start(f32[2,2,1,256,128]{4,3,1,2,0:T(8,128)S(1)} %maximum_select_fusion.11), channel_id=1, source_target_pairs={{0,32},{1,33},{2,34},{3,35},{4,36},{5,37},{6,38},{7,39},{8,40},{9,... | collective-permute-start | bytes 1572872 | tf_op jit(solution)/shard_map/ppermute | solution.py:15
  192.5 9.4 %collective-permute-done.11 = f32[2,2,1,256,128]{4,3,1,2,0:T(8,128)S(1)} collective-permute-done((f32[2,2,1,256,128]{4,3,1,2,0:T(8,128)S(1)}, f32[2,2,1,256,128]{4,3,1,2,0:T(8,128)S(1)}, u32[]{:S(2)}, u32[]{:S(2)}) %collective-permute-start.11) | collective-permute-done | bytes 524320 | tf_op jit(solution)/shard_map/ppermute | solution.py:15
  202.0 0.7 fusion.35
  202.7 1.3 collective-permute-start.12
  204.0 4.0 %collective-permute-start.13 = (f32[2,1,1,128]{3,2,0,1:T(1,128)S(1)}, f32[2,1,1,128]{3,2,0,1:T(1,128)S(1)}, u32[]{:S(2)}, u32[]{:S(2)}) collective-permute-start(f32[2,1,1,128]{3,2,0,1:T(1,128)S(1)} %get-tuple-element.32), channel_id=1, source_target_pairs={{0,64},{64,128},{128,192},{1,65},{65,129},{129,193},{2,66},{66,130... | collective-permute-start | bytes 3080 | tf_op jit(solution)/shard_map/ppermute | solution.py:26
  208.8 1.1 fusion.97
  (78 shorter events, 12.6 us)
Async XLA Ops:
  0.6 15.3 %copy-start = (f32[2,1,256,128]{3,2,1,0:T(8,128)S(1)}, f32[2,1,256,128]{3,2,1,0:T(8,128)}, u32[]{:S(2)}) copy-start(f32[2,1,256,128]{3,2,1,0:T(8,128)} %param.4) | copy-start | bytes 786436
  1.7 14.3 %collective-permute-start = (f32[2,2,1,256,128]{4,3,1,2,0:T(8,128)S(1)}, f32[2,2,1,256,128]{4,3,1,2,0:T(8,128)S(1)}, u32[]{:S(2)}, u32[]{:S(2)}) collective-permute-start(f32[2,2,1,256,128]{4,3,1,2,0:T(8,128)S(1)} %stack.37), channel_id=1, source_target_pairs={{0,32},{1,33},{2,34},{3,35},{4,36},{5,37},{6,38},{7,39},{8,40},{9,... | collective-permute-start | bytes 1572872 | tf_op jit(solution)/shard_map/ppermute | solution.py:15
  16.1 12.6 %collective-permute-start.1 = (f32[2,2,1,256,128]{4,3,1,2,0:T(8,128)S(1)}, f32[2,2,1,256,128]{4,3,1,2,0:T(8,128)S(1)}, u32[]{:S(2)}, u32[]{:S(2)}) collective-permute-start(f32[2,2,1,256,128]{4,3,1,2,0:T(8,128)S(1)} %maximum_select_fusion), channel_id=1, source_target_pairs={{0,16},{1,17},{2,18},{3,19},{4,20},{5,21},{6,22},{7,23},{8,24},{9,... | collective-permute-start | bytes 1572872 | tf_op jit(solution)/shard_map/ppermute | solution.py:15
  29.1 19.1 %collective-permute-start.2 = (f32[2,2,1,256,128]{4,3,1,2,0:T(8,128)S(1)}, f32[2,2,1,256,128]{4,3,1,2,0:T(8,128)S(1)}, u32[]{:S(2)}, u32[]{:S(2)}) collective-permute-start(f32[2,2,1,256,128]{4,3,1,2,0:T(8,128)S(1)} %maximum_select_fusion.1), channel_id=1, source_target_pairs={{0,8},{1,9},{2,10},{3,11},{4,12},{5,13},{6,14},{7,15},{8,0},{9,1},... | collective-permute-start | bytes 1572872 | tf_op jit(solution)/shard_map/ppermute | solution.py:15
  48.4 36.1 %collective-permute-start.3 = (f32[2,2,1,256,128]{4,3,1,2,0:T(8,128)S(1)}, f32[2,2,1,256,128]{4,3,1,2,0:T(8,128)S(1)}, u32[]{:S(2)}, u32[]{:S(2)}) collective-permute-start(f32[2,2,1,256,128]{4,3,1,2,0:T(8,128)S(1)} %maximum_select_fusion.2), channel_id=1, source_target_pairs={{0,4},{1,5},{2,6},{3,7},{4,0},{5,1},{6,2},{7,3},{8,12},{9,13},{10,... | collective-permute-start | bytes 1572872 | tf_op jit(solution)/shard_map/ppermute | solution.py:15
  84.8 13.1 %collective-permute-start.4 = (f32[2,2,1,256,128]{4,3,1,2,0:T(8,128)S(1)}, f32[2,2,1,256,128]{4,3,1,2,0:T(8,128)S(1)}, u32[]{:S(2)}, u32[]{:S(2)}) collective-permute-start(f32[2,2,1,256,128]{4,3,1,2,0:T(8,128)S(1)} %maximum_select_fusion.3), channel_id=1, source_target_pairs={{0,2},{1,3},{2,0},{3,1},{4,6},{5,7},{6,4},{7,5},{8,10},{9,11},{10,... | collective-permute-start | bytes 1572872 | tf_op jit(solution)/shard_map/ppermute | solution.py:15
  98.0 1.7 copy-start.2
  98.1 3.0 %collective-permute-start.5 = (f32[2,2,1,256,128]{4,3,1,2,0:T(8,128)S(1)}, f32[2,2,1,256,128]{4,3,1,2,0:T(8,128)S(1)}, u32[]{:S(2)}, u32[]{:S(2)}) collective-permute-start(f32[2,2,1,256,128]{4,3,1,2,0:T(8,128)S(1)} %maximum_select_fusion.4), channel_id=1, source_target_pairs={{0,1},{1,0},{2,3},{3,2},{4,5},{5,4},{6,7},{7,6},{8,9},{9,8},{10,11... | collective-permute-start | bytes 1572872 | tf_op jit(solution)/shard_map/ppermute | solution.py:15
  99.6 0.7 copy-start.1
  106.5 2.0 collective-permute-start.6
  108.7 13.4 %collective-permute-start.7 = (f32[2,2,1,256,128]{4,3,1,2,0:T(8,128)S(1)}, f32[2,2,1,256,128]{4,3,1,2,0:T(8,128)S(1)}, u32[]{:S(2)}, u32[]{:S(2)}) collective-permute-start(f32[2,2,1,256,128]{4,3,1,2,0:T(8,128)S(1)} %maximum_select_fusion.7), channel_id=1, source_target_pairs={{0,2},{1,3},{2,0},{3,1},{4,6},{5,7},{6,4},{7,5},{8,10},{9,11},{10,... | collective-permute-start | bytes 1572872 | tf_op jit(solution)/shard_map/ppermute | solution.py:15
  122.3 25.8 %collective-permute-start.8 = (f32[2,2,1,256,128]{4,3,1,2,0:T(8,128)S(1)}, f32[2,2,1,256,128]{4,3,1,2,0:T(8,128)S(1)}, u32[]{:S(2)}, u32[]{:S(2)}) collective-permute-start(f32[2,2,1,256,128]{4,3,1,2,0:T(8,128)S(1)} %maximum_select_fusion.8), channel_id=1, source_target_pairs={{0,4},{1,5},{2,6},{3,7},{4,0},{5,1},{6,2},{7,3},{8,12},{9,13},{10,... | collective-permute-start | bytes 1572872 | tf_op jit(solution)/shard_map/ppermute | solution.py:15
  148.4 28.3 %collective-permute-start.9 = (f32[2,2,1,256,128]{4,3,1,2,0:T(8,128)S(1)}, f32[2,2,1,256,128]{4,3,1,2,0:T(8,128)S(1)}, u32[]{:S(2)}, u32[]{:S(2)}) collective-permute-start(f32[2,2,1,256,128]{4,3,1,2,0:T(8,128)S(1)} %maximum_select_fusion.9), channel_id=1, source_target_pairs={{0,8},{1,9},{2,10},{3,11},{4,12},{5,13},{6,14},{7,15},{8,0},{9,1},... | collective-permute-start | bytes 1572872 | tf_op jit(solution)/shard_map/ppermute | solution.py:15
  176.8 12.1 %collective-permute-start.10 = (f32[2,2,1,256,128]{4,3,1,2,0:T(8,128)S(1)}, f32[2,2,1,256,128]{4,3,1,2,0:T(8,128)S(1)}, u32[]{:S(2)}, u32[]{:S(2)}) collective-permute-start(f32[2,2,1,256,128]{4,3,1,2,0:T(8,128)S(1)} %maximum_select_fusion.10), channel_id=1, source_target_pairs={{0,16},{1,17},{2,18},{3,19},{4,20},{5,21},{6,22},{7,23},{8,24},{9,... | collective-permute-start | bytes 1572872 | tf_op jit(solution)/shard_map/ppermute | solution.py:15
  189.1 3.0 %copy-start.3 = (f32[256]{0:T(256)S(1)}, f32[256]{0:T(256)}, u32[]{:S(2)}) copy-start(f32[256]{0:T(256)} %param.7) | copy-start | bytes 3076
  189.2 12.7 %collective-permute-start.11 = (f32[2,2,1,256,128]{4,3,1,2,0:T(8,128)S(1)}, f32[2,2,1,256,128]{4,3,1,2,0:T(8,128)S(1)}, u32[]{:S(2)}, u32[]{:S(2)}) collective-permute-start(f32[2,2,1,256,128]{4,3,1,2,0:T(8,128)S(1)} %maximum_select_fusion.11), channel_id=1, source_target_pairs={{0,32},{1,33},{2,34},{3,35},{4,36},{5,37},{6,38},{7,39},{8,40},{9,... | collective-permute-start | bytes 1572872 | tf_op jit(solution)/shard_map/ppermute | solution.py:15
  202.7 5.5 %collective-permute-start.12 = (f32[2,1,1,128]{3,2,0,1:T(1,128)S(1)}, f32[2,1,1,128]{3,2,0,1:T(1,128)S(1)}, u32[]{:S(2)}, u32[]{:S(2)}) collective-permute-start(f32[2,1,1,128]{3,2,0,1:T(1,128)S(1)} %get-tuple-element.31), channel_id=1, source_target_pairs={{64,0},{128,64},{192,128},{65,1},{129,65},{193,129},{66,2},{130,66... | collective-permute-start | bytes 3080 | tf_op jit(solution)/shard_map/ppermute | solution.py:28
  204.0 4.7 %collective-permute-start.13 = (f32[2,1,1,128]{3,2,0,1:T(1,128)S(1)}, f32[2,1,1,128]{3,2,0,1:T(1,128)S(1)}, u32[]{:S(2)}, u32[]{:S(2)}) collective-permute-start(f32[2,1,1,128]{3,2,0,1:T(1,128)S(1)} %get-tuple-element.32), channel_id=1, source_target_pairs={{0,64},{64,128},{128,192},{1,65},{65,129},{129,193},{2,66},{66,130... | collective-permute-start | bytes 3080 | tf_op jit(solution)/shard_map/ppermute | solution.py:26
where the time goes:
time: 214 us; the launch traced here: 210 us
  waiting for transfers between devices  152 us (71%)
  starting transfers between devices  41.6 us (19%)
  matrix products  8.25 us (4%)
  other arithmetic  3.99 us (2%)
  between operations  2.75 us (1%)
    ppermute x12, waiting for transfers between devices, partner_2(): lax.ppermute(x, axis, [(i, i ^ 1 << apart) for i in range(lax.axis_size(a...  151 us
    ppermute x12, starting transfers between devices, partner_2(): lax.ppermute(x, axis, [(i, i ^ 1 << apart) for i in range(lax.axis_size(a...  36.3 us
  transfers between devices with their start and end apart: 14, of which 13 were waited for; matrix products, arithmetic and copies ran while one was open for 1% of the time, Pallas kernels for 0%

commit v1 on v0

v1 whole, which is shorter than its diff:
```python
import math

import jax
import jax.numpy as jnp
import numpy as np
from jax import lax
from jax.experimental import pallas as pl
from jax.experimental.pallas import tpu as pltpu
from jax.sharding import PartitionSpec as P

BLOCK = 128


def compact_inverse(size):
    identity = np.eye(size)
    offdiag = 0.25 * (np.eye(size, k=1) + np.eye(size, k=-1))
    inverse = identity - offdiag
    power = offdiag
    for _ in range(5):
        power = power @ power
        inverse = inverse @ (identity + power)
    return inverse.astype(np.float32)


def halves(table):
    high = np.asarray(table, np.float32).astype(jnp.bfloat16)
    low = (np.asarray(table, np.float32) - high.astype(np.float32)).astype(jnp.bfloat16)
    return high, low


def split(value):
    high = value.astype(jnp.bfloat16)
    return high, (value - high.astype(jnp.float32)).astype(jnp.bfloat16)


def dot3(left, right):
    def dot(a, b):
        return jnp.dot(a, b, preferred_element_type=jnp.float32)

    return dot(left[0], right[0]) + (dot(left[0], right[1]) + dot(left[1], right[0]))


def tables(groups, width, rows):
    half = groups // 2
    low = np.arange(half + 1)
    group = np.arange(groups)
    column = np.arange(width)
    across = 2 * np.pi * (low[:, None] * group[None, :] % groups) / groups
    real_rows = np.cos(across)
    imag_rows = -np.sin(across)[1:half]
    forward = np.concatenate([real_rows, imag_rows])
    weight = np.where((low == 0) | (low == half), 1.0, 2.0)[:, None]
    inverse = np.concatenate([weight * real_rows, 2.0 * imag_rows]).T / (groups * width)
    same_row = np.eye(rows)
    forward = np.kron(forward, same_row)
    inverse = np.kron(inverse, same_row)
    grid = 2 * np.pi * (column[:, None] * column[None, :] % width) / width
    cosine, sine = np.cos(grid), np.sin(grid)
    along = np.block([[cosine, -sine], [sine, cosine]])
    back = np.block([[cosine, sine], [-sine, cosine]])
    twist = 2 * np.pi * low[:, None] * column[None, :] / (groups * width)
    twist = np.stack([np.cos(twist), np.sin(twist)]).astype(np.float32)
    return [*halves(forward), *halves(along), *halves(back), *halves(inverse), twist]


def row_values(ref, first, rows):
    shape = (rows, ref.shape[1])
    lane = lax.broadcasted_iota(jnp.int32, shape, 1)
    row = lax.broadcasted_iota(jnp.int32, shape, 0)
    picked = jnp.where(lane == first + row, jnp.broadcast_to(ref[...], shape), 0.0)
    return jnp.sum(picked, axis=1, keepdims=True)


def shear_kernel(
    position_ref,
    signal_ref,
    whole_ref,
    frac_ref,
    forward_high,
    forward_low,
    along_high,
    along_low,
    back_high,
    back_low,
    inverse_high,
    inverse_low,
    twist_ref,
    out_ref,
    spectrum_ref,
    signal_scratch,
):
    groups, rows, width = signal_ref.shape
    half = groups // 2
    total = groups * width
    row_count = whole_ref.shape[1]
    first = lax.rem(position_ref[0] * rows, row_count)
    whole = row_values(whole_ref, first, rows).astype(jnp.int32)
    frac = row_values(frac_ref, first, rows)

    column = lax.broadcasted_iota(jnp.int32, (rows, width), 1)
    signed = jnp.where(column < width // 2, column, column - width)
    turns = ((signed * whole) & (width - 1)).astype(jnp.float32) + signed.astype(jnp.float32) * frac
    angle = (2.0 * math.pi / width) * turns
    wide_cos, wide_sin = jnp.cos(angle), jnp.sin(angle)
    turns = ((column * whole) & (total - 1)).astype(jnp.float32) + column.astype(jnp.float32) * frac
    angle = (2.0 * math.pi / total) * turns
    fine_cos, fine_sin = jnp.cos(angle), jnp.sin(angle)

    signal = signal_ref[...].reshape(groups * rows, width)
    signal_scratch[...] = dot3((forward_high[...], forward_low[...]), split(signal))
    for k in range(half + 1):
        here = pl.ds(k * rows, rows)
        cosine, sine = twist_ref[0, pl.ds(k, 1), :], twist_ref[1, pl.ds(k, 1), :]
        real = signal_scratch[here, :]
        if 0 < k < half:
            imag = signal_scratch[pl.ds((half + k) * rows, rows), :]
            spectrum_ref[here, :width] = real * cosine + imag * sine
            spectrum_ref[here, width:] = imag * cosine - real * sine
        else:
            spectrum_ref[here, :width] = real * cosine
            spectrum_ref[here, width:] = -real * sine
    spectrum_ref[...] = dot3(split(spectrum_ref[...]), (along_high[...], along_low[...]))
    for k in range(half + 1):
        here = pl.ds(k * rows, rows)
        cosine, sine = fine_cos[:, k : k + 1], fine_sin[:, k : k + 1]
        shift_cos = wide_cos * cosine - wide_sin * sine
        shift_sin = wide_cos * sine + wide_sin * cosine
        real, imag = spectrum_ref[here, :width], spectrum_ref[here, width:]
        spectrum_ref[here, :width] = real * shift_cos + imag * shift_sin
        spectrum_ref[here, width:] = imag * shift_cos - real * shift_sin
    spectrum_ref[...] = dot3(split(spectrum_ref[...]), (back_high[...], back_low[...]))
    for k in range(half + 1):
        here = pl.ds(k * rows, rows)
        cosine, sine = twist_ref[0, pl.ds(k, 1), :], twist_ref[1, pl.ds(k, 1), :]
        real, imag = spectrum_ref[here, :width], spectrum_ref[here, width:]
        signal_scratch[here, :] = real * cosine - imag * sine
        if 0 < k < half:
            signal_scratch[pl.ds((half + k) * rows, rows), :] = real * sine + imag * cosine
    shifted = dot3((inverse_high[...], inverse_low[...]), split(signal_scratch[...]))
    out_ref[...] = shifted.reshape(groups, rows, width)


def shear(signal, whole, frac, position):
    groups, rows, width = signal.shape
    return pl.pallas_call(
        shear_kernel,
        out_shape=jax.ShapeDtypeStruct(signal.shape, jnp.float32),
        in_specs=[pl.BlockSpec(memory_space=pltpu.SMEM)] + [pl.BlockSpec(memory_space=pltpu.VMEM)] * 12,
        out_specs=pl.BlockSpec(memory_space=pltpu.VMEM),
        scratch_shapes=[
            pltpu.VMEM(((groups // 2 + 1) * rows, 2 * width), jnp.float32),
            pltpu.VMEM((groups * rows, width), jnp.float32),
        ],
        compiler_params=pltpu.CompilerParams(vmem_limit_bytes=32 * 2**20),
    )(position, signal, whole, frac, *[jnp.asarray(t) for t in tables(groups, width, rows)])


def derivative_kernel(remapped_ref, before_ref, after_ref, spacing_ref, compact_ref, out_ref):
    field_count, row_count, width = remapped_ref.shape
    scale = 0.75 * spacing_ref[...]
    row = lax.broadcasted_iota(jnp.int32, (row_count, width), 0)
    for field in range(field_count):
        cells = remapped_ref[field]
        above = jnp.where(row == 0, before_ref[field], pltpu.roll(cells, 1, 0))
        below = jnp.where(row == row_count - 1, after_ref[field], pltpu.roll(cells, row_count - 1, 0))
        difference = split(below - above)
        for start in range(0, row_count, BLOCK):
            here = slice(start, start + BLOCK)
            matrix = split(compact_ref[...] * scale[:, here])
            out_ref[field, here, :] = dot3(matrix, (difference[0][here], difference[1][here]))


def derivative(remapped, before, after, spacing):
    return pl.pallas_call(
        derivative_kernel,
        out_shape=jax.ShapeDtypeStruct(remapped.shape, jnp.float32),
        in_specs=[pl.BlockSpec(memory_space=pltpu.VMEM)] * 5,
        out_specs=pl.BlockSpec(memory_space=pltpu.VMEM),
        compiler_params=pltpu.CompilerParams(vmem_limit_bytes=32 * 2**20),
    )(remapped, before, after, spacing, jnp.asarray(compact_inverse(BLOCK)))


def on_device(fields, whole_shift, frac_shift, inv_spacing):
    groups = lax.axis_size("az")
    ends = lax.axis_size("rad") - 1
    position = lax.axis_index("az").astype(jnp.int32).reshape(1)
    field_count, plane_count, row_count, width = fields.shape
    sets = field_count * plane_count
    rows = sets * row_count // groups
    signal = fields.reshape(groups, rows, width)
    signal = lax.all_to_all(signal, "az", 0, 0, tiled=True)
    whole = whole_shift.astype(jnp.float32).reshape(1, row_count)
    signal = shear(signal, whole, frac_shift.reshape(1, row_count), position)
    signal = lax.all_to_all(signal, "az", 0, 0, tiled=True)
    remapped = signal.reshape(sets, row_count, width)
    before = lax.ppermute(remapped[:, -1:], "rad", [(i, i + 1) for i in range(ends)])
    after = lax.ppermute(remapped[:, :1], "rad", [(i + 1, i) for i in range(ends)])
    radial = derivative(remapped, before, after, inv_spacing.reshape(1, row_count))
    return remapped.reshape(fields.shape), radial.reshape(fields.shape)


def solution(mesh):
    return jax.shard_map(
        on_device,
        mesh=mesh,
        in_specs=(P(None, None, "rad", "az"), P("rad"), P("rad"), P("rad")),
        out_specs=(P(None, None, "rad", "az"), P(None, None, "rad", "az")),
        check_vma=False,
    )
```

time: 214 us -> 63.5 us (0.30)
  the two profiles are of different devices: /device:TPU:1 before, /device:TPU:24 now
where the time goes in v1:
time: 63.5 us; the launch traced here: 63 us
  blocking collectives  18 us (28%)
  starting transfers between devices  16 us (25%)
  waiting for transfers between devices  15.4 us (24%)
  local copies, waits for them, and re-layouts  9.59 us (15%)
  Pallas kernels  3.23 us (5%)
  between operations  0.72 us (1%)
    all_to_all x1, blocking collectives, on_device(): signal = lax.all_to_all(signal, 'az', 0, 0, tiled=True)  18 us
    all_to_all x1, starting transfers between devices, on_device(): signal = lax.all_to_all(signal, 'az', 0, 0, tiled=True)  12.1 us
    all_to_all x1, waiting for transfers between devices, on_device(): signal = lax.all_to_all(signal, 'az', 0, 0, tiled=True)  11.3 us
    unnamed x27, local copies, waits for them, and re-layouts  9.59 us
    ppermute x1, waiting for transfers between devices, on_device(): lax.ppermute(remapped[:, -1:], 'rad', [(i, i + 1) for i in range(ends)])  4.14 us
    ppermute x1, starting transfers between devices, on_device(): lax.ppermute(remapped[:, :1], 'rad', [(i + 1, i) for i in range(ends)])  2.64 us
    pallas_call x1, Pallas kernels, shear(): pl.pallas_call(shear_kernel, out_shape=jax.ShapeDtypeStruct(signal.shape,...  2.25 us
    ppermute x1, starting transfers between devices, on_device(): lax.ppermute(remapped[:, -1:], 'rad', [(i, i + 1) for i in range(ends)])  1.29 us
  transfers between devices with their start and end apart: 3, of which 2 were waited for; matrix products, arithmetic and copies ran while one was open for 0% of the time, Pallas kernels for 0%

profile of v1, /device:TPU:24, one launch (start us, length us, event | category | flops | bytes accessed | tf_op | source)
XLA Modules:
  0.0 63.0 jit_solution(15071996208275503847)
XLA Ops:
  0.6 0.0 copy-start
  0.6 12.1 %all-to-all-start = ((f32[64,8,128]{2,1,0:T(8,128)}), f32[64,8,128]{2,1,0:T(8,128)S(1)}, u32[]{:S(2)}, u32[]{:S(2)}) async-start(f32[64,8,128]{2,1,0:T(8,128)} %bitcast.18), calls=%async_computation | async-start | bytes 524288 | tf_op jit(solution)/shard_map/all_to_all | solution.py:191
  12.7 0.0 copy-start.12
  12.7 0.7 %copy-done.12 = s32[256]{0:T(256)S(1)} copy-done((s32[256]{0:T(256)S(1)}, s32[256]{0:T(256)}, u32[]{:S(2)}) %copy-start.12) | copy-done | bytes 1048
  13.4 11.3 %all-to-all-done.signal_ref = f32[64,8,128]{2,1,0:T(8,128)S(1)} async-done(((f32[64,8,128]{2,1,0:T(8,128)}), f32[64,8,128]{2,1,0:T(8,128)S(1)}, u32[]{:S(2)}, u32[]{:S(2)}) %all-to-all-start) | async-done | bytes 262176 | tf_op jit(solution)/shard_map/all_to_all | solution.py:191
  24.7 0.7 %copy-done.10 = f32[256]{0:T(256)S(1)} copy-done((f32[256]{0:T(256)S(1)}, f32[256]{0:T(256)}, u32[]{:S(2)}) %copy-start.10) | copy-done | bytes 1048
  25.4 1.0 %copy-done.1 = bf16[512,512]{1,0:T(8,128)(2,1)S(1)} copy-done((bf16[512,512]{1,0:T(8,128)(2,1)S(1)}, bf16[512,512]{1,0:T(8,128)(2,1)}, u32[]{:S(2)}) %copy-start.1) | copy-done | bytes 524312
  26.4 1.0 %copy-done.2 = bf16[512,512]{1,0:T(8,128)(2,1)S(1)} copy-done((bf16[512,512]{1,0:T(8,128)(2,1)S(1)}, bf16[512,512]{1,0:T(8,128)(2,1)}, u32[]{:S(2)}) %copy-start.2) | copy-done | bytes 524312
  27.5 1.0 %copy-done.3 = bf16[512,512]{1,0:T(8,128)(2,1)S(1)} copy-done((bf16[512,512]{1,0:T(8,128)(2,1)S(1)}, bf16[512,512]{1,0:T(8,128)(2,1)}, u32[]{:S(2)}) %copy-start.3) | copy-done | bytes 524312
  28.5 0.9 %copy-done.4 = bf16[256,256]{1,0:T(8,128)(2,1)S(1)} copy-done((bf16[256,256]{1,0:T(8,128)(2,1)S(1)}, bf16[256,256]{1,0:T(8,128)(2,1)}, u32[]{:S(2)}) %copy-start.4) | copy-done | bytes 131096
  29.4 0.9 %copy-done.5 = bf16[256,256]{1,0:T(8,128)(2,1)S(1)} copy-done((bf16[256,256]{1,0:T(8,128)(2,1)S(1)}, bf16[256,256]{1,0:T(8,128)(2,1)}, u32[]{:S(2)}) %copy-start.5) | copy-done | bytes 131096
  30.3 0.9 %copy-done.6 = bf16[256,256]{1,0:T(8,128)(2,1)S(1)} copy-done((bf16[256,256]{1,0:T(8,128)(2,1)S(1)}, bf16[256,256]{1,0:T(8,128)(2,1)}, u32[]{:S(2)}) %copy-start.6) | copy-done | bytes 131096
  31.2 0.9 %copy-done.7 = bf16[256,256]{1,0:T(8,128)(2,1)S(1)} copy-done((bf16[256,256]{1,0:T(8,128)(2,1)S(1)}, bf16[256,256]{1,0:T(8,128)(2,1)}, u32[]{:S(2)}) %copy-start.7) | copy-done | bytes 131096
  32.1 0.8 %copy-done.9 = f32[2,33,128]{2,1,0:T(8,128)S(1)} copy-done((f32[2,33,128]{2,1,0:T(8,128)S(1)}, f32[2,33,128]{2,1,0:T(8,128)}, u32[]{:S(2)}) %copy-start.9) | copy-done | bytes 33816
  32.9 2.2 %shard_map.149 = f32[64,8,128]{2,1,0:T(8,128)S(1)} custom-call(s32[1]{0:T(128)} %bitcast.position_ref, f32[64,8,128]{2,1,0:T(8,128)S(1)} %all-to-all-done.signal_ref, f32[1,256]{1,0:T(1,128)S(1)} %bitcast.15, f32[1,256]{1,0:T(1,128)S(1)} %bitcast.16, bf16[512,512]{1,0:T(8,128)(2,1)S(1)} %copy-done.3, bf16[512,512]{1,0:T(8,128)(2,1)S(1)} %copy-done.2, ...), custom_call_target="tpu_custom_call" | custom-call | tf_op jit(solution)/shard_map/pallas_call | solution.py:145
  35.2 0.0 copy-start.8
  35.2 18.0 %all_to_all.10 = f32[64,8,128]{2,1,0:T(8,128)S(1)} all-to-all(f32[64,8,128]{2,1,0:T(8,128)S(1)} %shard_map.149), channel_id=1, replica_groups=mesh['rad'=4,'az'=64] {'az'}, dimensions={0} | all-to-all | bytes 524288 | tf_op jit(solution)/shard_map/all_to_all | solution.py:194
  53.2 2.6 %collective-permute-start.1 = (f32[2,1,128]{2,1,0:T(1,128)S(1)}, f32[2,1,128]{2,1,0:T(1,128)S(1)}, u32[]{:S(2)}, u32[]{:S(2)}) collective-permute-start(f32[2,1,128]{2,1,0:T(1,128)S(1)} %get-tuple-element.4), channel_id=1, source_target_pairs={{64,0},{128,64},{192,128},{65,1},{129,65},{193,129},{66,2},{130,66... | collective-permute-start | bytes 3080 | tf_op jit(solution)/shard_map/ppermute | solution.py:197
  55.8 1.3 %collective-permute-start = (f32[2,1,128]{2,1,0:T(1,128)S(1)}, f32[2,1,128]{2,1,0:T(1,128)S(1)}, u32[]{:S(2)}, u32[]{:S(2)}) collective-permute-start(f32[2,1,128]{2,1,0:T(1,128)S(1)} %get-tuple-element.5), channel_id=1, source_target_pairs={{0,64},{64,128},{128,192},{1,65},{65,129},{129,193},{2,66},{66,130... | collective-permute-start | bytes 3080 | tf_op jit(solution)/shard_map/ppermute | solution.py:196
  57.1 0.0 copy-start.11
  57.1 0.0 collective-permute-done.1.after_ref
  57.1 4.1 %collective-permute-done.before_ref = f32[2,1,128]{2,1,0:T(1,128)S(1)} collective-permute-done((f32[2,1,128]{2,1,0:T(1,128)S(1)}, f32[2,1,128]{2,1,0:T(1,128)S(1)}, u32[]{:S(2)}, u32[]{:S(2)}) %collective-permute-start) | collective-permute-done | bytes 1056 | tf_op jit(solution)/shard_map/ppermute | solution.py:196
  61.3 1.0 %shard_map.150 = f32[2,256,128]{2,1,0:T(8,128)} custom-call(f32[2,256,128]{2,1,0:T(8,128)S(1)} %bitcast.13, f32[2,1,128]{2,1,0:T(1,128)S(1)} %collective-permute-done.before_ref, f32[2,1,128]{2,1,0:T(1,128)S(1)} %collective-permute-done.1.after_ref, f32[1,256]{1,0:T(1,128)S(1)} %bitcast.17, f32[128,128]{1,0:T(8,128)S(1)} %copy-done.8), custom_call_target="tpu_custom_call" | custom-call | tf_op jit(solution)/shard_map/pallas_call | solution.py:174
  62.3 0.7 %copy.19 = f32[2,1,256,128]{3,2,1,0:T(8,128)} copy(f32[2,1,256,128]{3,2,1,0:T(8,128)S(1)} %bitcast.14) | data formatting | bytes 524288
  (14 shorter events, 0.0 us)
Async XLA Ops:
  0.6 24.1 %copy-start = (bf16[512,512]{1,0:T(8,128)(2,1)S(1)}, bf16[512,512]{1,0:T(8,128)(2,1)}, u32[]{:S(2)}) copy-start(bf16[512,512]{1,0:T(8,128)(2,1)} %constant.31.clone.inverse_low) | copy-start | bytes 1572868
  0.6 24.1 %all-to-all-start = ((f32[64,8,128]{2,1,0:T(8,128)}), f32[64,8,128]{2,1,0:T(8,128)S(1)}, u32[]{:S(2)}, u32[]{:S(2)}) async-start(f32[64,8,128]{2,1,0:T(8,128)} %bitcast.18), calls=%async_computation | async-start | bytes 524288 | tf_op jit(solution)/shard_map/all_to_all | solution.py:191
  12.7 0.7 %copy-start.12 = (s32[256]{0:T(256)S(1)}, s32[256]{0:T(256)}, u32[]{:S(2)}) copy-start(s32[256]{0:T(256)} %param.15) | copy-start | bytes 3076
  24.7 0.7 %copy-start.10 = (f32[256]{0:T(256)S(1)}, f32[256]{0:T(256)}, u32[]{:S(2)}) copy-start(f32[256]{0:T(256)} %param.16) | copy-start | bytes 3076
  25.4 1.0 %copy-start.1 = (bf16[512,512]{1,0:T(8,128)(2,1)S(1)}, bf16[512,512]{1,0:T(8,128)(2,1)}, u32[]{:S(2)}) copy-start(bf16[512,512]{1,0:T(8,128)(2,1)} %constant.30.clone.inverse_high) | copy-start | bytes 1572868
  26.4 1.0 %copy-start.2 = (bf16[512,512]{1,0:T(8,128)(2,1)S(1)}, bf16[512,512]{1,0:T(8,128)(2,1)}, u32[]{:S(2)}) copy-start(bf16[512,512]{1,0:T(8,128)(2,1)} %constant.25.clone.forward_low) | copy-start | bytes 1572868
  27.5 1.0 %copy-start.3 = (bf16[512,512]{1,0:T(8,128)(2,1)S(1)}, bf16[512,512]{1,0:T(8,128)(2,1)}, u32[]{:S(2)}) copy-start(bf16[512,512]{1,0:T(8,128)(2,1)} %constant.24.clone.forward_high) | copy-start | bytes 1572868
  28.5 0.9 %copy-start.4 = (bf16[256,256]{1,0:T(8,128)(2,1)S(1)}, bf16[256,256]{1,0:T(8,128)(2,1)}, u32[]{:S(2)}) copy-start(bf16[256,256]{1,0:T(8,128)(2,1)} %constant.29.clone.back_low) | copy-start | bytes 393220
  29.4 0.9 %copy-start.5 = (bf16[256,256]{1,0:T(8,128)(2,1)S(1)}, bf16[256,256]{1,0:T(8,128)(2,1)}, u32[]{:S(2)}) copy-start(bf16[256,256]{1,0:T(8,128)(2,1)} %constant.28.clone.back_high) | copy-start | bytes 393220
  30.3 0.9 %copy-start.6 = (bf16[256,256]{1,0:T(8,128)(2,1)S(1)}, bf16[256,256]{1,0:T(8,128)(2,1)}, u32[]{:S(2)}) copy-start(bf16[256,256]{1,0:T(8,128)(2,1)} %constant.27.clone.along_low) | copy-start | bytes 393220
  31.2 0.9 %copy-start.7 = (bf16[256,256]{1,0:T(8,128)(2,1)S(1)}, bf16[256,256]{1,0:T(8,128)(2,1)}, u32[]{:S(2)}) copy-start(bf16[256,256]{1,0:T(8,128)(2,1)} %constant.26.clone.along_high) | copy-start | bytes 393220
  32.1 0.8 %copy-start.9 = (f32[2,33,128]{2,1,0:T(8,128)S(1)}, f32[2,33,128]{2,1,0:T(8,128)}, u32[]{:S(2)}) copy-start(f32[2,33,128]{2,1,0:T(8,128)} %constant.32.clone.twist_ref) | copy-start | bytes 101380
  35.2 26.1 %copy-start.8 = (f32[128,128]{1,0:T(8,128)S(1)}, f32[128,128]{1,0:T(8,128)}, u32[]{:S(2)}) copy-start(f32[128,128]{1,0:T(8,128)} %constant.33.clone.compact_ref) | copy-start | bytes 196612
  53.2 4.0 %collective-permute-start.1 = (f32[2,1,128]{2,1,0:T(1,128)S(1)}, f32[2,1,128]{2,1,0:T(1,128)S(1)}, u32[]{:S(2)}, u32[]{:S(2)}) collective-permute-start(f32[2,1,128]{2,1,0:T(1,128)S(1)} %get-tuple-element.4), channel_id=1, source_target_pairs={{64,0},{128,64},{192,128},{65,1},{129,65},{193,129},{66,2},{130,66... | collective-permute-start | bytes 3080 | tf_op jit(solution)/shard_map/ppermute | solution.py:197
  55.8 5.5 %collective-permute-start = (f32[2,1,128]{2,1,0:T(1,128)S(1)}, f32[2,1,128]{2,1,0:T(1,128)S(1)}, u32[]{:S(2)}, u32[]{:S(2)}) collective-permute-start(f32[2,1,128]{2,1,0:T(1,128)S(1)} %get-tuple-element.5), channel_id=1, source_target_pairs={{0,64},{64,128},{128,192},{1,65},{65,129},{129,193},{2,66},{66,130... | collective-permute-start | bytes 3080 | tf_op jit(solution)/shard_map/ppermute | solution.py:196
  57.1 4.2 %copy-start.11 = (f32[256]{0:T(256)S(1)}, f32[256]{0:T(256)}, u32[]{:S(2)}) copy-start(f32[256]{0:T(256)} %param.17) | copy-start | bytes 3076

commit v2 on v1

v2 whole, which is shorter than its diff:
```python
import functools
import math

import jax
import jax.numpy as jnp
import numpy as np
from jax import lax
from jax.experimental import pallas as pl
from jax.experimental.pallas import tpu as pltpu
from jax.sharding import PartitionSpec as P

BLOCK = 128
VMEM = pl.BlockSpec(memory_space=pltpu.VMEM)
SMEM = pl.BlockSpec(memory_space=pltpu.SMEM)
HBM = pl.BlockSpec(memory_space=pltpu.HBM)
PARAMS = pltpu.CompilerParams(vmem_limit_bytes=24 * 2**20)


def compact_inverse(size):
    identity = np.eye(size)
    offdiag = 0.25 * (np.eye(size, k=1) + np.eye(size, k=-1))
    inverse = identity - offdiag
    power = offdiag
    for _ in range(5):
        power = power @ power
        inverse = inverse @ (identity + power)
    return inverse.astype(np.float32)


def halves(table):
    high = np.asarray(table, np.float32).astype(jnp.bfloat16)
    low = (np.asarray(table, np.float32) - high.astype(np.float32)).astype(jnp.bfloat16)
    return high, low


def split(value):
    high = value.astype(jnp.bfloat16)
    return high, (value - high.astype(jnp.float32)).astype(jnp.bfloat16)


def dot(left, right):
    return jnp.dot(left, right, preferred_element_type=jnp.float32)


def dot3(left, right):
    return dot(left[0], right[0]) + (dot(left[0], right[1]) + dot(left[1], right[0]))


def fourier_tables(groups, width):
    half = groups // 2
    low = np.arange(half + 1)
    column = np.arange(width)
    across = 2 * np.pi * (low[:, None] * np.arange(groups)[None, :] % groups) / groups
    cosine, sine = np.cos(across), np.sin(across)
    forward = np.concatenate([cosine, -sine[1:half]])
    inverse = np.concatenate([cosine[:1], 2 * cosine[1:half], cosine[half:], -2 * sine[1:half]]).T / (groups * width)
    across = []
    for table in (forward, inverse):
        high, low = halves(table)
        across.append(np.pad(np.concatenate([high, high, low], axis=1), ((0, 0), (0, 2 * width - 3 * groups))))
    grid = 2 * np.pi * (column[:, None] * column[None, :] % width) / width
    cosine, sine = np.cos(grid), np.sin(grid)
    along = halves(np.block([[cosine, -sine], [sine, cosine]]))
    return np.concatenate([*across, *along])


def prepare_kernel(
    position_ref, whole_ref, frac_ref, spacing_ref, compact_ref, table_ref,
    table_out, twist_out, phase_out, matrix_out,
    *, groups, rows,
):
    table_out[...] = table_ref[...]
    scale = 0.75 * spacing_ref[...]
    for start in range(0, scale.shape[1], BLOCK):
        here = slice(start, start + BLOCK)
        matrix_out[:BLOCK, here], matrix_out[BLOCK:, here] = split(compact_ref[...] * scale[:, here])
    half = groups // 2
    width = twist_out.shape[2]
    total = groups * width
    row_count = whole_ref.shape[0]
    shape = (half, width)
    low = lax.broadcasted_iota(jnp.int32, shape, 0)
    column = lax.broadcasted_iota(jnp.int32, shape, 1)
    angle = (2.0 * math.pi / total) * (low * column).astype(jnp.float32)
    twist_out[0, :half, :] = jnp.cos(angle)
    twist_out[1, :half, :] = jnp.sin(angle)
    edge = lax.broadcasted_iota(jnp.int32, (rows, width), 1)
    angle = (2.0 * math.pi / total) * (half * edge).astype(jnp.float32)
    twist_out[0, half:, :] = jnp.cos(angle)
    twist_out[1, half:, :] = jnp.sin(angle)
    signed = low + groups * jnp.where(column < width // 2, column, column - width)
    edge = half + groups * jnp.where(edge < width // 2, edge, edge - width)
    edge_row = lax.broadcasted_iota(jnp.int32, (rows, width), 0)
    first = lax.rem(position_ref[0] * rows, row_count)
    edge_angle = jnp.zeros((rows, width), jnp.float32)
    for row in range(rows):
        whole, frac = whole_ref[first + row], frac_ref[first + row]
        turns = ((signed * whole) & (total - 1)).astype(jnp.float32) + signed.astype(jnp.float32) * frac
        angle = (2.0 * math.pi / total) * turns
        here = pl.ds(row * half, half)
        phase_out[0, here, :] = jnp.cos(angle)
        phase_out[1, here, :] = jnp.sin(angle)
        turns = ((edge * whole) & (total - 1)).astype(jnp.float32) + edge.astype(jnp.float32) * frac
        edge_angle = jnp.where(edge_row == row, (2.0 * math.pi / total) * turns, edge_angle)
    here = pl.ds(rows * half, rows)
    phase_out[0, here, :] = jnp.cos(edge_angle)
    phase_out[1, here, :] = jnp.sin(edge_angle)


def shear_kernel(signal_ref, phase_ref, table_ref, twist_ref, out_ref, edge_ref, *, groups):
    rows, width = edge_ref.shape
    half = groups // 2
    across, back = table_ref[:groups, : 3 * groups], table_ref[groups : 2 * groups, : 3 * groups]
    start = 2 * groups
    along_high = table_ref[start : start + 2 * width, :]
    along = jnp.concatenate([along_high, along_high, table_ref[start + 2 * width :, :]], axis=0)
    twist_cos, twist_sin = twist_ref[0, :half, :], twist_ref[1, :half, :]
    edge_cos, edge_sin = twist_ref[0, half:, :], twist_ref[1, half:, :]
    first = lax.broadcasted_iota(jnp.int32, (half, width), 0) == 0

    def stacked(blocks):
        high, low = split(jnp.concatenate(blocks, axis=1))
        return jnp.concatenate([high, low, high], axis=0)

    def transformed(value):
        high, low = split(value)
        return dot(jnp.concatenate([high, low, high], axis=1), along)

    signal = dot(across, stacked([signal_ref[pl.ds(row, groups, stride=rows), :] for row in range(rows)]))
    blocks = []
    for row in range(rows):
        here = slice(row * width, (row + 1) * width)
        real, imag = signal[:half, here], signal[half:, here]
        edge_ref[pl.ds(row, 1), :] = imag[:1, :]
        imag = jnp.where(first, 0.0, imag)
        blocks.append(
            jnp.concatenate([real * twist_cos + imag * twist_sin, imag * twist_cos - real * twist_sin], axis=1)
        )
    edge = edge_ref[...]
    edge = jnp.concatenate([edge * edge_cos, -edge * edge_sin], axis=1)
    spectrum = transformed(jnp.concatenate([*blocks, edge, jnp.zeros_like(edge)], axis=0))
    size = (half + 1) * rows
    shift_cos, shift_sin = phase_ref[0], phase_ref[1]
    real, imag = spectrum[:size, :width], spectrum[:size, width:]
    spectrum = jnp.concatenate([real * shift_cos + imag * shift_sin, real * shift_sin - imag * shift_cos], axis=1)
    spectrum = transformed(jnp.concatenate([spectrum, jnp.zeros_like(edge)], axis=0))
    edge = spectrum[half * rows : size, :]
    edge_ref[...] = edge[:, :width] * edge_cos + edge[:, width:] * edge_sin
    blocks = []
    for row in range(rows):
        here = slice(row * half, (row + 1) * half)
        real, imag = spectrum[here, :width], spectrum[here, width:]
        edge = jnp.broadcast_to(edge_ref[pl.ds(row, 1), :], (half, width))
        blocks.append(
            jnp.concatenate(
                [
                    real * twist_cos + imag * twist_sin,
                    jnp.where(first, edge, real * twist_sin - imag * twist_cos),
                ],
                axis=0,
            )
        )
    signal = dot(back, stacked(blocks))
    for row in range(rows):
        out_ref[pl.ds(row, groups, stride=rows), :] = signal[:, row * width : (row + 1) * width]


def derivative_kernel(
    block_ref, remapped_ref, before_ref, after_ref, matrix_ref, remapped_out, radial_out, radial, sems,
    *, blocks,
):
    field_count, row_count, width = remapped_ref.shape
    stores = [pltpu.make_async_copy(remapped_ref, remapped_out, sems.at[field_count])]
    stores[0].start()
    row = lax.broadcasted_iota(jnp.int32, (row_count, width), 0)
    parts = [slice(start, start + BLOCK) for start in range(0, row_count, BLOCK)]
    before = jnp.where(block_ref[0] > 0, before_ref[...], 0.0)
    after = jnp.where(block_ref[0] < blocks - 1, after_ref[...], 0.0)
    for field in range(field_count):
        cells = remapped_ref[field]
        above = jnp.where(row == 0, before[field : field + 1], pltpu.roll(cells, 1, 0))
        below = jnp.where(row == row_count - 1, after[field : field + 1], pltpu.roll(cells, row_count - 1, 0))
        high, low = split(below - above)
        for here in parts:
            matrix = (matrix_ref[:BLOCK, here], matrix_ref[BLOCK:, here])
            radial[field, here, :] = dot3(matrix, (high[here], low[here]))
        stores.append(pltpu.make_async_copy(radial.at[field], radial_out.at[field], sems.at[field]))
        stores[-1].start()
    for store in stores:
        store.wait()


def on_device(fields, whole_shift, frac_shift, inv_spacing):
    groups = lax.axis_size("az")
    blocks = lax.axis_size("rad")
    column = lax.axis_index("az").astype(jnp.int32).reshape(1)
    block = lax.axis_index("rad").astype(jnp.int32).reshape(1)
    field_count, plane_count, row_count, width = fields.shape
    sets = field_count * plane_count
    rows = sets * row_count // groups
    half = groups // 2
    table = fourier_tables(groups, width)
    float_of = functools.partial(jax.ShapeDtypeStruct, dtype=jnp.float32)

    signal = lax.all_to_all(fields.reshape(groups, rows, width), "az", 0, 0, tiled=True)
    table, twist, phases, matrix = pl.pallas_call(
        functools.partial(prepare_kernel, groups=groups, rows=rows),
        out_shape=(
            jax.ShapeDtypeStruct(table.shape, jnp.bfloat16),
            float_of((2, half + rows, width)),
            float_of((2, (half + 1) * rows, width)),
            jax.ShapeDtypeStruct((2 * BLOCK, row_count), jnp.bfloat16),
        ),
        in_specs=[SMEM] * 3 + [VMEM] * 3,
        out_specs=(VMEM,) * 4,
        compiler_params=PARAMS,
        cost_estimate=pl.CostEstimate(flops=10**9, transcendentals=10**5, bytes_accessed=2**21),
    )(
        column,
        whole_shift,
        frac_shift,
        inv_spacing.reshape(1, row_count),
        jnp.asarray(compact_inverse(BLOCK)),
        jnp.asarray(table),
    )
    signal = pl.pallas_call(
        functools.partial(shear_kernel, groups=groups),
        out_shape=float_of((groups * rows, width)),
        in_specs=[VMEM] * 4,
        out_specs=VMEM,
        scratch_shapes=[pltpu.VMEM((rows, width), jnp.float32)],
        compiler_params=PARAMS,
        cost_estimate=pl.CostEstimate(flops=10**9, transcendentals=0, bytes_accessed=2**21),
    )(signal.reshape(groups * rows, width), phases, table, twist)
    signal = lax.all_to_all(signal.reshape(groups, rows, width), "az", 0, 0, tiled=True)
    remapped = signal.reshape(sets, row_count, width)
    before = lax.ppermute(remapped[:, -1], "rad", [(i, (i + 1) % blocks) for i in range(blocks)])
    after = lax.ppermute(remapped[:, 0], "rad", [((i + 1) % blocks, i) for i in range(blocks)])
    remapped, radial = pl.pallas_call(
        functools.partial(derivative_kernel, blocks=blocks),
        out_shape=(float_of(remapped.shape), float_of(remapped.shape)),
        in_specs=[SMEM] + [VMEM] * 4,
        out_specs=(HBM, HBM),
        scratch_shapes=[pltpu.VMEM(remapped.shape, jnp.float32), pltpu.SemaphoreType.DMA((sets + 1,))],
        compiler_params=PARAMS,
    )(block, remapped, before, after, matrix)
    return remapped.reshape(fields.shape), radial.reshape(fields.shape)


def solution(mesh):
    return jax.shard_map(
        on_device,
        mesh=mesh,
        in_specs=(P(None, None, "rad", "az"), P("rad"), P("rad"), P("rad")),
        out_specs=(P(None, None, "rad", "az"), P(None, None, "rad", "az")),
        check_vma=False,
    )
```

time: 63.5 us -> 49.9 us (0.79)
  the two profiles are of different devices: /device:TPU:24 before, /device:TPU:1 now
where the time goes in v2:
time: 49.9 us; the launch traced here: 49.3 us
  blocking collectives  17.8 us (36%)
  starting transfers between devices  15.9 us (32%)
  waiting for transfers between devices  11 us (22%)
  Pallas kernels  3.13 us (6%)
  between operations  0.71 us (1%)
  local copies, waits for them, and re-layouts  0.68 us (1%)
    all_to_all x1, blocking collectives, on_device(): lax.all_to_all(signal.reshape(groups, rows, width), 'az', 0, 0, tiled=True)  17.8 us
    all_to_all x1, starting transfers between devices, on_device(): lax.all_to_all(fields.reshape(groups, rows, width), 'az', 0, 0, tiled=True)  13.1 us
    all_to_all x1, waiting for transfers between devices, on_device(): lax.all_to_all(fields.reshape(groups, rows, width), 'az', 0, 0, tiled=True)  10.1 us
    ppermute x1, starting transfers between devices, on_device(): lax.ppermute(remapped[:, 0], 'rad', [((i + 1) % blocks, i) for i in range...  1.52 us
    ppermute x1, starting transfers between devices, on_device(): lax.ppermute(remapped[:, -1], 'rad', [(i, (i + 1) % blocks) for i in rang...  1.3 us
    pallas_call x1, Pallas kernels, on_device(): pl.pallas_call(functools.partial(prepare_kernel, groups=groups, rows=rows...  1.21 us
  transfers between devices with their start and end apart: 3, of which 2 were waited for; matrix products, arithmetic and copies ran while one was open for 0% of the time, Pallas kernels for 2%

profile of v2, /device:TPU:1, one launch (start us, length us, event | category | flops | bytes accessed | tf_op | source)
XLA Modules:
  0.0 49.3 jit_solution(12622228204388313255)
XLA Ops:
  0.6 0.0 copy-start.3
  0.6 0.0 copy-start.4
  0.7 13.1 %all-to-all-start = ((f32[64,8,128]{2,1,0:T(8,128)}), f32[64,8,128]{2,1,0:T(8,128)S(1)}, u32[]{:S(2)}, u32[]{:S(2)}) async-start(f32[64,8,128]{2,1,0:T(8,128)} %bitcast.24), calls=%async_computation | async-start | bytes 524288 | tf_op jit(solution)/shard_map/all_to_all | solution.py:205
  13.8 0.0 copy-start.1
  13.8 0.0 copy-start.2
  13.8 0.0 copy-start
  13.8 0.0 copy-done.3
  13.8 0.0 copy-done.4
  13.9 0.6 %copy-done.1 = f32[256]{0:T(256)S(1)} copy-done((f32[256]{0:T(256)S(1)}, f32[256]{0:T(256)}, u32[]{:S(2)}) %copy-start.1) | copy-done | bytes 1048
  14.5 0.0 copy-done.2
  14.5 0.0 copy-done
  14.5 1.2 %shard_map.77 = (bf16[640,256]{1,0:T(8,128)(2,1)S(1)}, f32[2,40,128]{2,1,0:T(8,128)S(1)}, f32[2,264,128]{2,1,0:T(8,128)S(1)}, bf16[256,256]{1,0:T(8,128)(2,1)S(1)}) custom-call(s32[1]{0:T(128)} %bitcast.3.position_ref, s32[256]{0:T(256)S(1)} %copy-done, f32[256]{0:T(256)S(1)} %copy-done.1, f32[1,256]{1,0:T(1,128)S(1)} %bitcast.23, f32[128,128]{1,0:T(8,128)S(1)} %copy-done.4, ...), custom_call_target="tpu_custom_call" | custom-call | flops 1000000000 | bytes 2097152 | tf_op jit(solution)/shard_map/pallas_call | solution.py:206
  15.7 10.1 %all-to-all-done = f32[64,8,128]{2,1,0:T(8,128)S(1)} async-done(((f32[64,8,128]{2,1,0:T(8,128)}), f32[64,8,128]{2,1,0:T(8,128)S(1)}, u32[]{:S(2)}, u32[]{:S(2)}) %all-to-all-start) | async-done | bytes 262176 | tf_op jit(solution)/shard_map/all_to_all | solution.py:205
  25.8 1.0 %shard_map.78 = f32[512,128]{1,0:T(8,128)S(1)} custom-call(f32[512,128]{1,0:T(8,128)S(1)} %bitcast.21, f32[2,264,128]{2,1,0:T(8,128)S(1)} %get-tuple-element.8.phase_ref, bf16[640,256]{1,0:T(8,128)(2,1)S(1)} %get-tuple-element.9.table_ref, f32[2,40,128]{2,1,0:T(8,128)S(1)} %get-tuple-element.10.twist_ref), custom_call_target="tpu_custom_call" | custom-call | flops 1000000000 | bytes 2097152 | tf_op jit(solution)/shard_map/pallas_call | solution.py:226
  26.8 17.8 %all_to_all.10 = f32[64,8,128]{2,1,0:T(8,128)S(1)} all-to-all(f32[64,8,128]{2,1,0:T(8,128)S(1)} %bitcast.22), channel_id=1, replica_groups=mesh['rad'=4,'az'=64] {'az'}, dimensions={0} | all-to-all | bytes 524288 | tf_op jit(solution)/shard_map/all_to_all | solution.py:235
  44.6 1.3 %collective-permute-start = (f32[2,128]{1,0:T(2,128)S(1)}, f32[2,128]{1,0:T(2,128)S(1)}, u32[]{:S(2)}, u32[]{:S(2)}) collective-permute-start(f32[2,128]{1,0:T(2,128)S(1)} %bitcast.26), channel_id=1, source_target_pairs={{0,64},{64,128},{128,192},{192,0},{1,65},{65,129},{129,193},{193,1... | collective-permute-start | bytes 3080 | tf_op jit(solution)/shard_map/ppermute | solution.py:237
  45.9 1.5 %collective-permute-start.1 = (f32[2,128]{1,0:T(2,128)S(1)}, f32[2,128]{1,0:T(2,128)S(1)}, u32[]{:S(2)}, u32[]{:S(2)}) collective-permute-start(f32[2,128]{1,0:T(2,128)S(1)} %bitcast.25), channel_id=1, source_target_pairs={{64,0},{128,64},{192,128},{0,192},{65,1},{129,65},{193,129},{1,193... | collective-permute-start | bytes 3080 | tf_op jit(solution)/shard_map/ppermute | solution.py:238
  47.4 0.9 %collective-permute-done.before_ref = f32[2,128]{1,0:T(2,128)S(1)} collective-permute-done((f32[2,128]{1,0:T(2,128)S(1)}, f32[2,128]{1,0:T(2,128)S(1)}, u32[]{:S(2)}, u32[]{:S(2)}) %collective-permute-start) | collective-permute-done | bytes 1056 | tf_op jit(solution)/shard_map/ppermute | solution.py:237
  48.3 0.0 collective-permute-done.1.after_ref
  48.3 1.0 %shard_map.79 = (f32[2,256,128]{2,1,0:T(8,128)}, f32[2,256,128]{2,1,0:T(8,128)}) custom-call(s32[1]{0:T(128)} %bitcast.block_ref, f32[2,256,128]{2,1,0:T(8,128)S(1)} %bitcast.20, f32[2,128]{1,0:T(2,128)S(1)} %collective-permute-done.before_ref, f32[2,128]{1,0:T(2,128)S(1)} %collective-permute-done.1.after_ref, bf16[256,256]{1,0:T(8,128)(2,1)S(1)} %get-tuple-element.11.matrix_ref), custom_call_target="tpu_custom_call" | custom-call | tf_op jit(solution)/shard_map/pallas_call | solution.py:239
  (1 shorter events, 0.0 us)
Async XLA Ops:
  0.6 13.2 %copy-start.3 = (bf16[640,256]{1,0:T(8,128)(2,1)S(1)}, bf16[640,256]{1,0:T(8,128)(2,1)}, u32[]{:S(2)}) copy-start(bf16[640,256]{1,0:T(8,128)(2,1)} %constant.14.clone.table_ref) | copy-start | bytes 983044
  0.6 13.2 %copy-start.4 = (f32[128,128]{1,0:T(8,128)S(1)}, f32[128,128]{1,0:T(8,128)}, u32[]{:S(2)}) copy-start(f32[128,128]{1,0:T(8,128)} %constant.13.clone.compact_ref) | copy-start | bytes 196612
  0.7 25.1 %all-to-all-start = ((f32[64,8,128]{2,1,0:T(8,128)}), f32[64,8,128]{2,1,0:T(8,128)S(1)}, u32[]{:S(2)}, u32[]{:S(2)}) async-start(f32[64,8,128]{2,1,0:T(8,128)} %bitcast.24), calls=%async_computation | async-start | bytes 524288 | tf_op jit(solution)/shard_map/all_to_all | solution.py:205
  13.8 0.7 %copy-start.1 = (f32[256]{0:T(256)S(1)}, f32[256]{0:T(256)}, u32[]{:S(2)}) copy-start(f32[256]{0:T(256)} %frac_ref.1) | copy-start | bytes 3076
  13.8 0.7 %copy-start.2 = (f32[256]{0:T(256)S(1)}, f32[256]{0:T(256)}, u32[]{:S(2)}) copy-start(f32[256]{0:T(256)} %param.9) | copy-start | bytes 3076
  13.8 0.7 %copy-start = (s32[256]{0:T(256)S(1)}, s32[256]{0:T(256)}, u32[]{:S(2)}) copy-start(s32[256]{0:T(256)} %whole_ref.1) | copy-start | bytes 3076
  44.6 3.7 %collective-permute-start = (f32[2,128]{1,0:T(2,128)S(1)}, f32[2,128]{1,0:T(2,128)S(1)}, u32[]{:S(2)}, u32[]{:S(2)}) collective-permute-start(f32[2,128]{1,0:T(2,128)S(1)} %bitcast.26), channel_id=1, source_target_pairs={{0,64},{64,128},{128,192},{192,0},{1,65},{65,129},{129,193},{193,1... | collective-permute-start | bytes 3080 | tf_op jit(solution)/shard_map/ppermute | solution.py:237
  45.9 2.4 %collective-permute-start.1 = (f32[2,128]{1,0:T(2,128)S(1)}, f32[2,128]{1,0:T(2,128)S(1)}, u32[]{:S(2)}, u32[]{:S(2)}) collective-permute-start(f32[2,128]{1,0:T(2,128)S(1)} %bitcast.25), channel_id=1, source_target_pairs={{64,0},{128,64},{192,128},{0,192},{65,1},{129,65},{193,129},{1,193... | collective-permute-start | bytes 3080 | tf_op jit(solution)/shard_map/ppermute | solution.py:238

commit v3 on v2

v3 whole, which is shorter than its diff:
```python
import functools
import math

import jax
import jax.numpy as jnp
import numpy as np
from jax import lax
from jax.experimental import pallas as pl
from jax.experimental.pallas import tpu as pltpu
from jax.sharding import PartitionSpec as P

BLOCK = 128
VMEM = pl.BlockSpec(memory_space=pltpu.VMEM)
SMEM = pl.BlockSpec(memory_space=pltpu.SMEM)
HBM = pl.BlockSpec(memory_space=pltpu.HBM)
PARAMS = pltpu.CompilerParams(vmem_limit_bytes=24 * 2**20)


def compact_inverse(size):
    identity = np.eye(size)
    offdiag = 0.25 * (np.eye(size, k=1) + np.eye(size, k=-1))
    inverse = identity - offdiag
    power = offdiag
    for _ in range(5):
        power = power @ power
        inverse = inverse @ (identity + power)
    return inverse.astype(np.float32)


def halves(table):
    high = np.asarray(table, np.float32).astype(jnp.bfloat16)
    low = (np.asarray(table, np.float32) - high.astype(np.float32)).astype(jnp.bfloat16)
    return high, low


def split(value):
    high = value.astype(jnp.bfloat16)
    return high, (value - high.astype(jnp.float32)).astype(jnp.bfloat16)


def dot(left, right):
    return jnp.dot(left, right, preferred_element_type=jnp.float32)


def dot3(left, right):
    return dot(left[0], right[0]) + (dot(left[0], right[1]) + dot(left[1], right[0]))


def fourier_tables(groups, width):
    half = groups // 2
    low = np.arange(half + 1)
    column = np.arange(width)
    across = 2 * np.pi * (low[:, None] * np.arange(groups)[None, :] % groups) / groups
    cosine, sine = np.cos(across), np.sin(across)
    forward = np.concatenate([cosine, -sine[1:half]])
    inverse = np.concatenate([cosine[:1], 2 * cosine[1:half], cosine[half:], -2 * sine[1:half]]).T / (groups * width)
    across = []
    for table in (forward, inverse):
        high, low = halves(table)
        across.append(np.pad(np.concatenate([high, high, low], axis=1), ((0, 0), (0, 2 * width - 3 * groups))))
    grid = 2 * np.pi * (column[:, None] * column[None, :] % width) / width
    cosine, sine = np.cos(grid), np.sin(grid)
    along = halves(np.block([[cosine, -sine], [sine, cosine]]))
    return np.concatenate([*across, *along])


def phase_angle(signed, whole, frac, total):
    turns = ((signed * whole) & (total - 1)).astype(jnp.float32) + signed.astype(jnp.float32) * frac
    return (2.0 * math.pi / total) * turns


def prepare_kernel(
    position_ref, whole_ref, frac_ref, spacing_ref, compact_ref, table_ref,
    table_out, twist_out, phase_out, matrix_out,
    *, groups, rows,
):
    table_out[...] = table_ref[...]
    scale = 0.75 * spacing_ref[...]
    for start in range(0, scale.shape[1], BLOCK):
        here = slice(start, start + BLOCK)
        matrix_out[:BLOCK, here], matrix_out[BLOCK:, here] = split(compact_ref[...] * scale[:, here])
    half = groups // 2
    width = twist_out.shape[2]
    total = groups * width
    row_count = whole_ref.shape[1]
    shape = (half, width)
    low = lax.broadcasted_iota(jnp.int32, shape, 0)
    column = lax.broadcasted_iota(jnp.int32, shape, 1)
    angle = (2.0 * math.pi / total) * (low * column).astype(jnp.float32)
    twist_out[0, :half, :] = jnp.cos(angle)
    twist_out[1, :half, :] = jnp.sin(angle)
    edge = lax.broadcasted_iota(jnp.int32, (rows, width), 1)
    angle = (2.0 * math.pi / total) * (half * edge).astype(jnp.float32)
    twist_out[0, half:, :] = jnp.cos(angle)
    twist_out[1, half:, :] = jnp.sin(angle)
    signed = low + groups * jnp.where(column < width // 2, column, column - width)
    edge = half + groups * jnp.where(edge < width // 2, edge, edge - width)
    edge_row = lax.broadcasted_iota(jnp.int32, (rows, width), 0)
    lane = lax.broadcasted_iota(jnp.int32, (rows, row_count), 1)
    first = lax.rem(position_ref[0] * rows, row_count)
    own = lane == first + lax.broadcasted_iota(jnp.int32, (rows, row_count), 0)
    wholes = jnp.sum(jnp.where(own, whole_ref[...].astype(jnp.float32), 0.0), axis=1, keepdims=True).astype(jnp.int32)
    fracs = jnp.sum(jnp.where(own, frac_ref[...], 0.0), axis=1, keepdims=True)
    edge_angle = jnp.zeros((rows, width), jnp.float32)
    for row in range(rows):
        whole, frac = wholes[row : row + 1], fracs[row : row + 1]
        angle = phase_angle(signed, whole, frac, total)
        here = pl.ds(row * half, half)
        phase_out[0, here, :] = jnp.cos(angle)
        phase_out[1, here, :] = jnp.sin(angle)
        edge_angle = jnp.where(edge_row == row, phase_angle(edge, whole, frac, total), edge_angle)
    here = pl.ds(rows * half, rows)
    phase_out[0, here, :] = jnp.cos(edge_angle)
    phase_out[1, here, :] = jnp.sin(edge_angle)


def sheared(signals, table_ref, twist_ref, shift_cos, shift_sin, edge_ref):
    groups, width = signals[0].shape
    half = groups // 2
    edges = edge_ref.shape[0]
    size = half * len(signals)
    across, back = table_ref[:groups, : 3 * groups], table_ref[groups : 2 * groups, : 3 * groups]
    start = 2 * groups
    along_high = table_ref[start : start + 2 * width, :]
    along = jnp.concatenate([along_high, along_high, table_ref[start + 2 * width :, :]], axis=0)
    twist_cos, twist_sin = twist_ref[0, :half, :], twist_ref[1, :half, :]
    edge_cos, edge_sin = twist_ref[0, half : half + 1, :], twist_ref[1, half : half + 1, :]
    first = lax.broadcasted_iota(jnp.int32, (half, width), 0) == 0

    def stacked(blocks):
        high, low = split(jnp.concatenate(blocks, axis=1))
        return jnp.concatenate([high, low, high], axis=0)

    def transformed(value):
        high, low = split(value)
        return dot(jnp.concatenate([high, low, high], axis=1), along)

    signal = dot(across, stacked(signals))
    blocks = []
    edge_ref[...] = jnp.zeros_like(edge_ref)
    for row in range(len(signals)):
        here = slice(row * width, (row + 1) * width)
        real, imag = signal[:half, here], signal[half:, here]
        edge_ref[pl.ds(row, 1), :] = imag[:1, :]
        imag = jnp.where(first, 0.0, imag)
        blocks.append(
            jnp.concatenate([real * twist_cos + imag * twist_sin, imag * twist_cos - real * twist_sin], axis=1)
        )
    edge = edge_ref[...]
    edge = jnp.concatenate([edge * edge_cos, -edge * edge_sin], axis=1)
    spectrum = transformed(jnp.concatenate([*blocks, edge], axis=0))
    real, imag = spectrum[:, :width], spectrum[:, width:]
    spectrum = jnp.concatenate([real * shift_cos + imag * shift_sin, real * shift_sin - imag * shift_cos], axis=1)
    spectrum = transformed(spectrum)
    edge = spectrum[size:, :]
    edge_ref[...] = edge[:, :width] * edge_cos + edge[:, width:] * edge_sin
    blocks = []
    for row in range(len(signals)):
        here = slice(row * half, (row + 1) * half)
        real, imag = spectrum[here, :width], spectrum[here, width:]
        edge = jnp.broadcast_to(edge_ref[pl.ds(row, 1), :], (half, width))
        parts = [real * twist_cos + imag * twist_sin, jnp.where(first, edge, real * twist_sin - imag * twist_cos)]
        blocks.append(jnp.concatenate(parts, axis=0))
    return dot(back, stacked(blocks))


def edge_kernel(block_ref, whole_ref, frac_ref, _, cells_ref, near_out, far_out, tiles, sems, *, blocks):
    sets, row_count, width = cells_ref.shape
    depth = tiles.shape[2]
    loads = []
    for side, start in enumerate((row_count - depth, 0)):
        for field in range(sets):
            source = cells_ref.at[field, pl.ds(start, depth)]
            loads.append(pltpu.make_async_copy(source, tiles.at[side, field], sems.at[side, field]))
            loads[-1].start()
    for load in loads:
        load.wait()
    edges = []
    for side, (row, place) in enumerate(((depth - 1, row_count - 1), (0, 0))):
        rows = [tiles[side, field, row : row + 1, :] for field in range(sets)]
        shifts = [whole_ref[:, place : place + 1].astype(jnp.float32), frac_ref[:, place : place + 1]]
        edges.append(jnp.concatenate(rows + [jnp.broadcast_to(shift, (1, width)) for shift in shifts], axis=0))
    is_odd = block_ref[0] & 1 == 1
    near_out[...] = jnp.where(is_odd, edges[1], edges[0])
    is_end = (block_ref[0] == 0) | (block_ref[0] == blocks - 1)
    far_out[...] = jnp.where(is_end, 0.0, jnp.where(is_odd, edges[0], edges[1]))


def halo_kernel(block_ref, near_ref, far_ref, phase_out, halo_out, *, groups, rows):
    is_odd = block_ref[0] & 1 == 1
    near, far = near_ref[...], far_ref[...]
    sides = (jnp.where(is_odd, near, far), jnp.where(is_odd, far, near))
    width = phase_out.shape[2]
    half = groups // 2
    shape = (half, width)
    sets = near_ref.shape[0] - 2
    low = lax.broadcasted_iota(jnp.int32, shape, 0)
    column = lax.broadcasted_iota(jnp.int32, shape, 1)
    signed = low + groups * jnp.where(column < width // 2, column, column - width)
    edge = lax.broadcasted_iota(jnp.int32, (rows, width), 1)
    edge = half + groups * jnp.where(edge < width // 2, edge, edge - width)
    edge_row = lax.broadcasted_iota(jnp.int32, (rows, width), 0)
    edge_angle = jnp.zeros((rows, width), jnp.float32)
    for side, cells in enumerate(sides):
        halo_out[pl.ds(side * sets, sets), :] = cells[:sets]
        whole, frac = cells[sets : sets + 1].astype(jnp.int32), cells[sets + 1 : sets + 2]
        angle = phase_angle(signed, whole, frac, groups * width)
        cosine, sine = jnp.cos(angle), jnp.sin(angle)
        for field in range(sets):
            here = pl.ds((side * sets + field) * half, half)
            phase_out[0, here, :] = cosine
            phase_out[1, here, :] = sine
        edge_angle = jnp.where(edge_row // sets == side, phase_angle(edge, whole, frac, groups * width), edge_angle)
    here = pl.ds(2 * sets * half, rows)
    phase_out[0, here, :] = jnp.cos(edge_angle)
    phase_out[1, here, :] = jnp.sin(edge_angle)


def shear_kernel(
    position_ref, signal_ref, phase_ref, halo_ref, halo_phase_ref, table_ref, twist_ref, out_ref, edge_ref,
    *, groups, rows,
):
    halos = halo_ref.shape[0]
    pitch = rows + halos
    half = groups // 2
    signals = [signal_ref[pl.ds(row, groups, stride=rows), :] for row in range(rows)]
    width = signals[0].shape[1]
    own = lax.broadcasted_iota(jnp.int32, (groups, width), 0) == position_ref[0]
    signals += [jnp.where(own, halo_ref[row : row + 1, :], 0.0) for row in range(halos)]
    shifts = []
    for part in range(2):
        ours, theirs = phase_ref[part], halo_phase_ref[part]
        cut, halo_cut = rows * half, halos * half
        shifts.append(jnp.concatenate([ours[:cut], theirs[:halo_cut], ours[cut:], theirs[halo_cut:]], axis=0))
    signal = sheared(signals, table_ref, twist_ref, *shifts, edge_ref)
    for row in range(pitch):
        out_ref[pl.ds(row, groups, stride=pitch), :] = signal[:, row * width : (row + 1) * width]


def derivative_kernel(
    cells_ref, matrix_ref, remapped_out, radial_out, remapped, radial, sems, *, groups, rows
):
    field_count, row_count, width = remapped.shape
    pitch = cells_ref.shape[0] // groups
    parts = row_count // rows
    for group in range(groups):
        here = pl.ds(group % parts * rows, rows)
        remapped[group // parts, here, :] = cells_ref[pl.ds(group * pitch, rows), :]
    stores = [pltpu.make_async_copy(remapped, remapped_out, sems.at[field_count])]
    stores[0].start()

    halos = [cells_ref[pl.ds(row, groups, stride=pitch), :] for row in range(rows, pitch)]
    halos = [jnp.sum(halo, axis=0, keepdims=True) for halo in halos]
    before, after = halos[:field_count], halos[field_count:]

    row = lax.broadcasted_iota(jnp.int32, (row_count, width), 0)
    for field in range(field_count):
        cells = remapped[field]
        above = jnp.where(row == 0, 0.0, pltpu.roll(cells, 1, 0))
        below = jnp.where(row == row_count - 1, 0.0, pltpu.roll(cells, row_count - 1, 0))
        high, low = split(below - above)
        for start in range(0, row_count, BLOCK):
            here = slice(start, start + BLOCK)
            matrix = (matrix_ref[:BLOCK, here], matrix_ref[BLOCK:, here])
            result = dot3(matrix, (high[here], low[here]))
            if start == 0:
                result -= (matrix[0][:, :1].astype(jnp.float32) + matrix[1][:, :1].astype(jnp.float32)) * before[field]
            if start == row_count - BLOCK:
                result += (matrix[0][:, -1:].astype(jnp.float32) + matrix[1][:, -1:].astype(jnp.float32)) * after[field]
            radial[field, here, :] = result
        stores.append(pltpu.make_async_copy(radial.at[field], radial_out.at[field], sems.at[field]))
        stores[-1].start()
    for store in stores:
        store.wait()


def on_device(fields, whole_shift, frac_shift, inv_spacing):
    groups = lax.axis_size("az")
    blocks = lax.axis_size("rad")
    column = lax.axis_index("az").astype(jnp.int32).reshape(1)
    block = lax.axis_index("rad").astype(jnp.int32).reshape(1)
    field_count, plane_count, row_count, width = fields.shape
    sets = field_count * plane_count
    rows = sets * row_count // groups
    half = groups // 2
    table = fourier_tables(groups, width)
    shifts = [row.reshape(1, row_count) for row in (whole_shift, frac_shift, inv_spacing)]
    float_of = functools.partial(jax.ShapeDtypeStruct, dtype=jnp.float32)

    signal = lax.all_to_all(fields.reshape(groups, rows, width), "az", 0, 0, tiled=True)
    table, twist, phases, matrix = pl.pallas_call(
        functools.partial(prepare_kernel, groups=groups, rows=rows),
        out_shape=(
            jax.ShapeDtypeStruct(table.shape, jnp.bfloat16),
            float_of((2, half + rows, width)),
            float_of((2, (half + 1) * rows, width)),
            jax.ShapeDtypeStruct((2 * BLOCK, row_count), jnp.bfloat16),
        ),
        in_specs=[SMEM] + [VMEM] * 5,
        out_specs=(VMEM,) * 4,
        compiler_params=PARAMS,
        cost_estimate=pl.CostEstimate(flops=10**9, transcendentals=10**5, bytes_accessed=2**21),
    )(
        column,
        *shifts,
        jnp.asarray(compact_inverse(BLOCK)),
        jnp.asarray(table),
    )
    planes = fields.reshape(sets, row_count, width)
    near, far = pl.pallas_call(
        functools.partial(edge_kernel, blocks=blocks),
        out_shape=(float_of((sets + 2, width)),) * 2,
        in_specs=[SMEM] + [VMEM] * 3 + [HBM],
        out_specs=(VMEM,) * 2,
        scratch_shapes=[pltpu.VMEM((2, sets, 8, width), jnp.float32), pltpu.SemaphoreType.DMA((2, sets))],
        compiler_params=PARAMS,
    )(block, *shifts, planes)
    near = lax.ppermute(near, "rad", [(i, i ^ 1) for i in range(blocks)])
    pairs = [(i, i + 1) for i in range(1, blocks - 1, 2)]
    far = lax.ppermute(far, "rad", pairs + [(j, i) for i, j in pairs] + [(0, blocks - 1), (blocks - 1, 0)])
    halo_phases, halo = pl.pallas_call(
        functools.partial(halo_kernel, groups=groups, rows=rows),
        out_shape=(float_of((2, 2 * sets * half + rows, width)), float_of((2 * sets, width))),
        in_specs=[SMEM] + [VMEM] * 2,
        out_specs=(VMEM,) * 2,
        compiler_params=PARAMS,
        cost_estimate=pl.CostEstimate(flops=10**8, transcendentals=10**4, bytes_accessed=2**18),
    )(block, near, far)
    pitch = rows + 2 * sets
    signal = pl.pallas_call(
        functools.partial(shear_kernel, groups=groups, rows=rows),
        out_shape=float_of((groups * pitch, width)),
        in_specs=[SMEM] + [VMEM] * 6,
        out_specs=VMEM,
        scratch_shapes=[pltpu.VMEM((2 * rows, width), jnp.float32)],
        compiler_params=PARAMS,
        cost_estimate=pl.CostEstimate(flops=10**9, transcendentals=0, bytes_accessed=2**21),
    )(column, signal.reshape(groups * rows, width), phases, halo, halo_phases, table, twist)
    signal = signal.reshape(groups, pitch // 4, 4, width)
    signal = lax.all_to_all(signal, "az", 0, 0, tiled=True).reshape(groups * pitch, width)
    whole_shape = (sets, row_count, width)
    remapped, radial = pl.pallas_call(
        functools.partial(derivative_kernel, groups=groups, rows=rows),
        out_shape=(float_of(whole_shape), float_of(whole_shape)),
        in_specs=[VMEM] * 2,
        out_specs=(HBM, HBM),
        scratch_shapes=[
            pltpu.VMEM(whole_shape, jnp.float32),
            pltpu.VMEM(whole_shape, jnp.float32),
            pltpu.SemaphoreType.DMA((sets + 1,)),
        ],
        compiler_params=PARAMS,
    )(signal, matrix)
    return remapped.reshape(fields.shape), radial.reshape(fields.shape)


def solution(mesh):
    return jax.shard_map(
        on_device,
        mesh=mesh,
        in_specs=(P(None, None, "rad", "az"), P("rad"), P("rad"), P("rad")),
        out_specs=(P(None, None, "rad", "az"), P(None, None, "rad", "az")),
        check_vma=False,
    )
```

time: 49.9 us -> 48.6 us (0.974)
  waiting for transfers between devices: 11 us -> 6.07 us
  blocking collectives: 17.8 us -> 20.4 us
  local copies, waits for them, and re-layouts: 0.68 us -> 1.66 us
  starting transfers between devices: 15.9 us -> 16.4 us
    all_to_all x1, waiting for transfers between devices: 10.1 us -> 5.65 us  [on_device(): lax.all_to_all(fields.reshape(groups, rows, width), 'az', 0, 0, tiled=True)]
    all_to_all x1, blocking collectives: 17.8 us -> 20.4 us  [on_device(): lax.all_to_all(signal, 'az', 0, 0, tiled=True)]
    unnamed x10 -> x12, local copies, waits for them, and re-layouts: 0.68 us -> 1.66 us
    pallas_call x1, Pallas kernels: 1.21 us -> 0.64 us  [on_device(): pl.pallas_call(functools.partial(prepare_kernel, groups=groups, rows=rows...]
    pallas_call x2 -> x4, Pallas kernels: 1.93 us -> 2.43 us  [the longest x1 1.18 us: on_device(): pl.pallas_call(functools.partial(shear_kernel, groups=groups, rows=rows),...]
where the time goes in v3:
time: 48.6 us; the launch traced here: 48.4 us
  blocking collectives  20.4 us (42%)
  starting transfers between devices  16.4 us (34%)
  waiting for transfers between devices  6.07 us (12%)
  Pallas kernels  3.07 us (6%)
  local copies, waits for them, and re-layouts  1.66 us (3%)
  between operations  0.71 us (1%)
    all_to_all x1, blocking collectives, on_device(): lax.all_to_all(signal, 'az', 0, 0, tiled=True)  20.4 us
    all_to_all x1, starting transfers between devices, on_device(): lax.all_to_all(fields.reshape(groups, rows, width), 'az', 0, 0, tiled=True)  13.1 us
    all_to_all x1, waiting for transfers between devices, on_device(): lax.all_to_all(fields.reshape(groups, rows, width), 'az', 0, 0, tiled=True)  5.65 us
    ppermute x1, starting transfers between devices, on_device(): lax.ppermute(far, 'rad', pairs + [(j, i) for i, j in pairs] + [(0, blocks...  1.9 us
    unnamed x12, local copies, waits for them, and re-layouts  1.66 us
    ppermute x1, starting transfers between devices, on_device(): near = lax.ppermute(near, 'rad', [(i, i ^ 1) for i in range(blocks)])  1.38 us
    pallas_call x1, Pallas kernels, on_device(): pl.pallas_call(functools.partial(shear_kernel, groups=groups, rows=rows),...  1.18 us
  transfers between devices with their start and end apart: 3, of which 2 were waited for; matrix products, arithmetic and copies ran while one was open for 0% of the time, Pallas kernels for 2%

profile of v3, /device:TPU:1, one launch (start us, length us, event | category | flops | bytes accessed | tf_op | source)
XLA Modules:
  0.0 48.4 jit_solution(2645669077575156326)
XLA Ops:
  0.6 0.0 copy-start
  0.6 13.1 %all-to-all-start = ((f32[64,8,128]{2,1,0:T(8,128)}), f32[64,8,128]{2,1,0:T(8,128)S(1)}, u32[]{:S(2)}, u32[]{:S(2)}) async-start(f32[64,8,128]{2,1,0:T(8,128)} %bitcast.17), calls=%async_computation | async-start | bytes 524288 | tf_op jit(solution)/shard_map/all_to_all | solution.py:290
  13.8 0.0 copy-start.2
  13.8 0.0 copy-start.3
  13.8 0.0 copy-start.1
  13.8 0.0 copy-done
  13.8 0.6 %copy-done.2 = f32[256]{0:T(256)S(1)} copy-done((f32[256]{0:T(256)S(1)}, f32[256]{0:T(256)}, u32[]{:S(2)}) %copy-start.2) | copy-done | bytes 1048
  14.5 0.0 copy-done.3
  14.5 0.0 copy-done.1
  14.5 0.0 copy-start.5
  14.5 0.1 shard_map.78
  14.6 1.4 %collective-permute-start = (f32[4,128]{1,0:T(4,128)S(1)}, f32[4,128]{1,0:T(4,128)S(1)}, u32[]{:S(2)}, u32[]{:S(2)}) collective-permute-start(f32[4,128]{1,0:T(4,128)S(1)} %get-tuple-element.13), channel_id=1, source_target_pairs={{0,64},{64,0},{128,192},{192,128},{1,65},{65,1},{129,193},{193,129... | collective-permute-start | bytes 6152 | tf_op jit(solution)/shard_map/ppermute | solution.py:318
  16.0 1.9 %collective-permute-start.1 = (f32[4,128]{1,0:T(4,128)S(1)}, f32[4,128]{1,0:T(4,128)S(1)}, u32[]{:S(2)}, u32[]{:S(2)}) collective-permute-start(f32[4,128]{1,0:T(4,128)S(1)} %get-tuple-element.14), channel_id=1, source_target_pairs={{64,128},{128,64},{0,192},{192,0},{65,129},{129,65},{1,193},{193,1... | collective-permute-start | bytes 6152 | tf_op jit(solution)/shard_map/ppermute | solution.py:320
  17.9 0.0 copy-done.5
  17.9 0.0 copy-start.4
  17.9 1.0 %copy-done.4 = bf16[640,256]{1,0:T(8,128)(2,1)S(1)} copy-done((bf16[640,256]{1,0:T(8,128)(2,1)S(1)}, bf16[640,256]{1,0:T(8,128)(2,1)}, u32[]{:S(2)}) %copy-start.4) | copy-done | bytes 327704
  18.9 0.6 %shard_map.77 = (bf16[640,256]{1,0:T(8,128)(2,1)S(1)}, f32[2,40,128]{2,1,0:T(8,128)S(1)}, f32[2,264,128]{2,1,0:T(8,128)S(1)}, bf16[256,256]{1,0:T(8,128)(2,1)S(1)}) custom-call(s32[1]{0:T(128)} %bitcast.position_ref, s32[1,256]{1,0:T(1,128)S(1)} %bitcast.22, f32[1,256]{1,0:T(1,128)S(1)} %bitcast.24, f32[1,256]{1,0:T(1,128)S(1)} %bitcast.26, ...), custom_call_target="tpu_custom_call" | custom-call | flops 1000000000 | bytes 2097152 | tf_op jit(solution)/shard_map/pallas_call | solution.py:291
  19.5 0.0 collective-permute-done.near_ref
  19.5 0.4 collective-permute-done.1.far_ref
  20.0 0.2 shard_map.79
  20.1 5.7 %all-to-all-done = f32[64,8,128]{2,1,0:T(8,128)S(1)} async-done(((f32[64,8,128]{2,1,0:T(8,128)}), f32[64,8,128]{2,1,0:T(8,128)S(1)}, u32[]{:S(2)}, u32[]{:S(2)}) %all-to-all-start) | async-done | bytes 262176 | tf_op jit(solution)/shard_map/all_to_all | solution.py:290
  25.8 1.2 %shard_map.80 = f32[768,128]{1,0:T(8,128)S(1)} custom-call(s32[1]{0:T(128)} %bitcast.position_ref, f32[512,128]{1,0:T(8,128)S(1)} %bitcast.20, f32[2,264,128]{2,1,0:T(8,128)S(1)} %get-tuple-element.12.phase_ref, f32[4,128]{1,0:T(4,128)S(1)} %get-tuple-element.15.halo_ref, f32[2,136,128]{2,1,0:T(8,128)S(1)} %get-tuple-element.16.halo_phase_ref, ...), custom_call_target="tpu_custom_call" | custom-call | flops 1000000000 | bytes 2097152 | tf_op jit(solution)/shard_map/pallas_call | solution.py:330
  27.0 20.4 %all_to_all.10 = f32[64,3,4,128]{3,2,1,0:T(4,128)S(1)} all-to-all(f32[64,3,4,128]{3,2,1,0:T(4,128)S(1)} %bitcast.19), channel_id=1, replica_groups=mesh['rad'=4,'az'=64] {'az'}, dimensions={0} | all-to-all | bytes 786432 | tf_op jit(solution)/shard_map/all_to_all | solution.py:340
  47.4 1.0 %shard_map.81 = (f32[2,256,128]{2,1,0:T(8,128)}, f32[2,256,128]{2,1,0:T(8,128)}) custom-call(f32[768,128]{1,0:T(8,128)S(1)} %bitcast.16, bf16[256,256]{1,0:T(8,128)(2,1)S(1)} %get-tuple-element.19.matrix_ref), custom_call_target="tpu_custom_call" | custom-call | tf_op jit(solution)/shard_map/pallas_call | solution.py:342
Async XLA Ops:
  0.6 13.2 %copy-start = (f32[2,1,256,128]{3,2,1,0:T(8,128)S(1)}, f32[2,1,256,128]{3,2,1,0:T(8,128)}, u32[]{:S(2)}) copy-start(f32[2,1,256,128]{3,2,1,0:T(8,128)} %param.6) | copy-start | bytes 786436
  0.6 25.1 %all-to-all-start = ((f32[64,8,128]{2,1,0:T(8,128)}), f32[64,8,128]{2,1,0:T(8,128)S(1)}, u32[]{:S(2)}, u32[]{:S(2)}) async-start(f32[64,8,128]{2,1,0:T(8,128)} %bitcast.17), calls=%async_computation | async-start | bytes 524288 | tf_op jit(solution)/shard_map/all_to_all | solution.py:290
  13.8 0.7 %copy-start.2 = (f32[256]{0:T(256)S(1)}, f32[256]{0:T(256)}, u32[]{:S(2)}) copy-start(f32[256]{0:T(256)} %param.8) | copy-start | bytes 3076
  13.8 0.7 %copy-start.3 = (f32[256]{0:T(256)S(1)}, f32[256]{0:T(256)}, u32[]{:S(2)}) copy-start(f32[256]{0:T(256)} %param.9) | copy-start | bytes 3076
  13.8 0.7 %copy-start.1 = (s32[256]{0:T(256)S(1)}, s32[256]{0:T(256)}, u32[]{:S(2)}) copy-start(s32[256]{0:T(256)} %param.7) | copy-start | bytes 3076
  14.5 3.4 %copy-start.5 = (f32[128,128]{1,0:T(8,128)S(1)}, f32[128,128]{1,0:T(8,128)}, u32[]{:S(2)}) copy-start(f32[128,128]{1,0:T(8,128)} %constant.13.clone.compact_ref) | copy-start | bytes 196612
  14.6 4.9 %collective-permute-start = (f32[4,128]{1,0:T(4,128)S(1)}, f32[4,128]{1,0:T(4,128)S(1)}, u32[]{:S(2)}, u32[]{:S(2)}) collective-permute-start(f32[4,128]{1,0:T(4,128)S(1)} %get-tuple-element.13), channel_id=1, source_target_pairs={{0,64},{64,0},{128,192},{192,128},{1,65},{65,1},{129,193},{193,129... | collective-permute-start | bytes 6152 | tf_op jit(solution)/shard_map/ppermute | solution.py:318
  16.0 3.9 %collective-permute-start.1 = (f32[4,128]{1,0:T(4,128)S(1)}, f32[4,128]{1,0:T(4,128)S(1)}, u32[]{:S(2)}, u32[]{:S(2)}) collective-permute-start(f32[4,128]{1,0:T(4,128)S(1)} %get-tuple-element.14), channel_id=1, source_target_pairs={{64,128},{128,64},{0,192},{192,0},{65,129},{129,65},{1,193},{193,1... | collective-permute-start | bytes 6152 | tf_op jit(solution)/shard_map/ppermute | solution.py:320
  17.9 1.0 %copy-start.4 = (bf16[640,256]{1,0:T(8,128)(2,1)S(1)}, bf16[640,256]{1,0:T(8,128)(2,1)}, u32[]{:S(2)}) copy-start(bf16[640,256]{1,0:T(8,128)(2,1)} %constant.14.clone.table_ref) | copy-start | bytes 983044

commit v4 on v3

--- a/solution.py
+++ b/solution.py
@@ -164,7 +164,7 @@
     return dot(back, stacked(blocks))
 
 
-def edge_kernel(block_ref, whole_ref, frac_ref, _, cells_ref, near_out, far_out, tiles, sems, *, blocks):
+def edge_kernel(position_ref, whole_ref, frac_ref, _, cells_ref, keep_out, give_out, tiles, sems):
     sets, row_count, width = cells_ref.shape
     depth = tiles.shape[2]
     loads = []
@@ -175,62 +175,67 @@
             loads[-1].start()
     for load in loads:
         load.wait()
-    edges = []
-    for side, (row, place) in enumerate(((depth - 1, row_count - 1), (0, 0))):
-        rows = [tiles[side, field, row : row + 1, :] for field in range(sets)]
-        shifts = [whole_ref[:, place : place + 1].astype(jnp.float32), frac_ref[:, place : place + 1]]
-        edges.append(jnp.concatenate(rows + [jnp.broadcast_to(shift, (1, width)) for shift in shifts], axis=0))
-    is_odd = block_ref[0] & 1 == 1
-    near_out[...] = jnp.where(is_odd, edges[1], edges[0])
-    is_end = (block_ref[0] == 0) | (block_ref[0] == blocks - 1)
-    far_out[...] = jnp.where(is_end, 0.0, jnp.where(is_odd, edges[0], edges[1]))
-
-
-def halo_kernel(block_ref, near_ref, far_ref, phase_out, halo_out, *, groups, rows):
-    is_odd = block_ref[0] & 1 == 1
-    near, far = near_ref[...], far_ref[...]
-    sides = (jnp.where(is_odd, near, far), jnp.where(is_odd, far, near))
+    is_odd = position_ref[0] & 1 == 1
+    last = [tiles[0, field, depth - 1 :, :] for field in range(sets)]
+    first = [tiles[1, field, :1, :] for field in range(sets)]
+    shifts = []
+    for ref in (whole_ref, frac_ref):
+        shift = jnp.where(is_odd, ref[:, :1].astype(jnp.float32), ref[:, row_count - 1 :].astype(jnp.float32))
+        shifts.append(jnp.broadcast_to(shift, (1, width)))
+    keep = [jnp.where(is_odd, theirs, ours) for ours, theirs in zip(last, first, strict=True)]
+    keep_out[...] = jnp.concatenate(keep + shifts, axis=0)
+    give_out[...] = jnp.concatenate([jnp.where(is_odd, ours, theirs) for ours, theirs in zip(last, first, strict=True)], axis=0)
+
+
+def join_kernel(keep_ref, got_ref, out_ref):
+    sets, _ = got_ref.shape
+    out_ref[...] = jnp.zeros_like(out_ref)
+    out_ref[pl.ds(0, sets + 2), :] = keep_ref[...]
+    out_ref[pl.ds(sets + 2, sets), :] = got_ref[...]
+
+
+def halo_kernel(position_ref, block_ref, edges_ref, phase_out, halo_out, *, groups, rows, blocks):
+    is_odd = position_ref[0] & 1 == 1
+    is_end = jnp.where(is_odd, block_ref[0] == blocks - 1, block_ref[0] == 0)
+    cells = edges_ref[...]
+    sets = halo_out.shape[0] // 2
+    keep, got = cells[:sets], cells[sets + 2 : 2 * sets + 2]
+    both = jnp.where(is_odd, jnp.concatenate([got, keep], axis=0), jnp.concatenate([keep, got], axis=0))
+    halo_out[...] = jnp.where(is_end, 0.0, both)
+    whole, frac = cells[sets : sets + 1].astype(jnp.int32), cells[sets + 1 : sets + 2]
     width = phase_out.shape[2]
     half = groups // 2
     shape = (half, width)
-    sets = near_ref.shape[0] - 2
     low = lax.broadcasted_iota(jnp.int32, shape, 0)
     column = lax.broadcasted_iota(jnp.int32, shape, 1)
     signed = low + groups * jnp.where(column < width // 2, column, column - width)
     edge = lax.broadcasted_iota(jnp.int32, (rows, width), 1)
     edge = half + groups * jnp.where(edge < width // 2, edge, edge - width)
-    edge_row = lax.broadcasted_iota(jnp.int32, (rows, width), 0)
-    edge_angle = jnp.zeros((rows, width), jnp.float32)
-    for side, cells in enumerate(sides):
-        halo_out[pl.ds(side * sets, sets), :] = cells[:sets]
-        whole, frac = cells[sets : sets + 1].astype(jnp.int32), cells[sets + 1 : sets + 2]
-        angle = phase_angle(signed, whole, frac, groups * width)
-        cosine, sine = jnp.cos(angle), jnp.sin(angle)
+    angle, edge_angle = [phase_angle(place, whole, frac, groups * width) for place in (signed, edge)]
+    for part, wave in enumerate((jnp.cos, jnp.sin)):
+        shift = wave(angle)
         for field in range(sets):
-            here = pl.ds((side * sets + field) * half, half)
-            phase_out[0, here, :] = cosine
-            phase_out[1, here, :] = sine
-        edge_angle = jnp.where(edge_row // sets == side, phase_angle(edge, whole, frac, groups * width), edge_angle)
-    here = pl.ds(2 * sets * half, rows)
-    phase_out[0, here, :] = jnp.cos(edge_angle)
-    phase_out[1, here, :] = jnp.sin(edge_angle)
+            phase_out[part, pl.ds(field * half, half), :] = shift
+        phase_out[part, pl.ds(sets * half, rows), :] = wave(edge_angle)
 
 
 def shear_kernel(
     position_ref, signal_ref, phase_ref, halo_ref, halo_phase_ref, table_ref, twist_ref, out_ref, edge_ref,
     *, groups, rows,
 ):
-    halos = halo_ref.shape[0]
-    pitch = rows + halos
+    sets = halo_ref.shape[0] // 2
+    pitch = rows + sets
     half = groups // 2
     signals = [signal_ref[pl.ds(row, groups, stride=rows), :] for row in range(rows)]
     width = signals[0].shape[1]
-    own = lax.broadcasted_iota(jnp.int32, (groups, width), 0) == position_ref[0]
-    signals += [jnp.where(own, halo_ref[row : row + 1, :], 0.0) for row in range(halos)]
+    group = lax.broadcasted_iota(jnp.int32, (groups, width), 0) - (position_ref[0] & -2)
+    for field in range(sets):
+        even, odd = halo_ref[field : field + 1, :], halo_ref[sets + field : sets + field + 1, :]
+        signals.append(jnp.where(group == 0, even, jnp.where(group == 1, odd, 0.0)))
     shifts = []
     for part in range(2):
         ours, theirs = phase_ref[part], halo_phase_ref[part]
-        cut, halo_cut = rows * half, halos * half
+        cut, halo_cut = rows * half, sets * half
         shifts.append(jnp.concatenate([ours[:cut], theirs[:halo_cut], ours[cut:], theirs[halo_cut:]], axis=0))
     signal = sheared(signals, table_ref, twist_ref, *shifts, edge_ref)
     for row in range(pitch):
@@ -249,9 +254,11 @@
     stores = [pltpu.make_async_copy(remapped, remapped_out, sems.at[field_count])]
     stores[0].start()
 
-    halos = [cells_ref[pl.ds(row, groups, stride=pitch), :] for row in range(rows, pitch)]
-    halos = [jnp.sum(halo, axis=0, keepdims=True) for halo in halos]
-    before, after = halos[:field_count], halos[field_count:]
+    def total(place):
+        return jnp.sum(cells_ref[pl.ds(place, groups // 2, stride=2 * pitch), :], axis=0, keepdims=True)
+
+    before = [total(rows + field) for field in range(field_count)]
+    after = [total(pitch + rows + field) for field in range(field_count)]
 
     row = lax.broadcasted_iota(jnp.int32, (row_count, width), 0)
     for field in range(field_count):
@@ -307,26 +314,33 @@
         jnp.asarray(table),
     )
     planes = fields.reshape(sets, row_count, width)
-    near, far = pl.pallas_call(
-        functools.partial(edge_kernel, blocks=blocks),
-        out_shape=(float_of((sets + 2, width)),) * 2,
+    keep, give = pl.pallas_call(
+        edge_kernel,
+        out_shape=(float_of((sets + 2, width)), float_of((sets, width))),
         in_specs=[SMEM] + [VMEM] * 3 + [HBM],
         out_specs=(VMEM,) * 2,
         scratch_shapes=[pltpu.VMEM((2, sets, 8, width), jnp.float32), pltpu.SemaphoreType.DMA((2, sets))],
         compiler_params=PARAMS,
-    )(block, *shifts, planes)
-    near = lax.ppermute(near, "rad", [(i, i ^ 1) for i in range(blocks)])
-    pairs = [(i, i + 1) for i in range(1, blocks - 1, 2)]
-    far = lax.ppermute(far, "rad", pairs + [(j, i) for i, j in pairs] + [(0, blocks - 1), (blocks - 1, 0)])
+    )(column, *shifts, planes)
+    got = lax.ppermute(give, "az", [(i, i ^ 1) for i in range(groups)])
+    edges = pl.pallas_call(
+        join_kernel,
+        out_shape=float_of((8, width)),
+        in_specs=[VMEM] * 2,
+        out_specs=VMEM,
+        compiler_params=PARAMS,
+    )(keep, got)
+    pairs = [(i, j, (i + 1 - 2 * (j & 1)) % blocks) for i in range(blocks) for j in range(groups)]
+    edges = lax.ppermute(edges, ("rad", "az"), [(i * groups + j, k * groups + j) for i, j, k in pairs])
     halo_phases, halo = pl.pallas_call(
-        functools.partial(halo_kernel, groups=groups, rows=rows),
-        out_shape=(float_of((2, 2 * sets * half + rows, width)), float_of((2 * sets, width))),
-        in_specs=[SMEM] + [VMEM] * 2,
+        functools.partial(halo_kernel, groups=groups, rows=rows, blocks=blocks),
+        out_shape=(float_of((2, sets * half + rows, width)), float_of((2 * sets, width))),
+        in_specs=[SMEM] * 2 + [VMEM],
         out_specs=(VMEM,) * 2,
         compiler_params=PARAMS,
         cost_estimate=pl.CostEstimate(flops=10**8, transcendentals=10**4, bytes_accessed=2**18),
-    )(block, near, far)
-    pitch = rows + 2 * sets
+    )(column, block, edges)
+    pitch = rows + sets
     signal = pl.pallas_call(
         functools.partial(shear_kernel, groups=groups, rows=rows),
         out_shape=float_of((groups * pitch, width)),
@@ -336,7 +350,7 @@
         compiler_params=PARAMS,
         cost_estimate=pl.CostEstimate(flops=10**9, transcendentals=0, bytes_accessed=2**21),
     )(column, signal.reshape(groups * rows, width), phases, halo, halo_phases, table, twist)
-    signal = signal.reshape(groups, pitch // 4, 4, width)
+    signal = signal.reshape(groups, pitch // 2, 2, width)
     signal = lax.all_to_all(signal, "az", 0, 0, tiled=True).reshape(groups * pitch, width)
     whole_shape = (sets, row_count, width)
     remapped, radial = pl.pallas_call(

time: 48.6 us -> 47.2 us (0.971)
  blocking collectives: 20.4 us -> 19.1 us
    all_to_all x1, blocking collectives: 20.4 us -> 19.1 us  [on_device(): lax.all_to_all(signal, 'az', 0, 0, tiled=True)]
where the time goes in v4:
time: 47.2 us; the launch traced here: 46.9 us
  blocking collectives  19.1 us (40%)
  starting transfers between devices  16.4 us (35%)
  waiting for transfers between devices  6.06 us (13%)
  Pallas kernels  2.98 us (6%)
  local copies, waits for them, and re-layouts  1.66 us (4%)
  between operations  0.72 us (2%)
    all_to_all x1, blocking collectives, on_device(): lax.all_to_all(signal, 'az', 0, 0, tiled=True)  19.1 us
    all_to_all x1, starting transfers between devices, on_device(): lax.all_to_all(fields.reshape(groups, rows, width), 'az', 0, 0, tiled=True)  13.1 us
    all_to_all x1, waiting for transfers between devices, on_device(): lax.all_to_all(fields.reshape(groups, rows, width), 'az', 0, 0, tiled=True)  5.24 us
    ppermute x1, starting transfers between devices, on_device(): lax.ppermute(edges, ('rad', 'az'), [(i * groups + j, k * groups + j) for...  2.73 us
    unnamed x12, local copies, waits for them, and re-layouts  1.66 us
    pallas_call x1, Pallas kernels, on_device(): pl.pallas_call(functools.partial(shear_kernel, groups=groups, rows=rows),...  1.09 us
    pallas_call x1, Pallas kernels, on_device(): pl.pallas_call(functools.partial(derivative_kernel, groups=groups, rows=r...  0.96 us
  transfers between devices with their start and end apart: 3, of which 2 were waited for; matrix products, arithmetic and copies ran while one was open for 0% of the time, Pallas kernels for 2%

profile of v4, /device:TPU:1, one launch (start us, length us, event | category | flops | bytes accessed | tf_op | source)
XLA Modules:
  0.0 46.9 jit_solution(8552581070359062913)
XLA Ops:
  0.6 0.0 copy-start
  0.6 13.1 %all-to-all-start = ((f32[64,8,128]{2,1,0:T(8,128)}), f32[64,8,128]{2,1,0:T(8,128)S(1)}, u32[]{:S(2)}, u32[]{:S(2)}) async-start(f32[64,8,128]{2,1,0:T(8,128)} %bitcast.17), calls=%async_computation | async-start | bytes 524288 | tf_op jit(solution)/shard_map/all_to_all | solution.py:297
  13.8 0.0 copy-start.2
  13.8 0.0 copy-start.3
  13.8 0.0 copy-start.1
  13.8 0.0 copy-done
  13.8 0.6 %copy-done.2 = f32[256]{0:T(256)S(1)} copy-done((f32[256]{0:T(256)S(1)}, f32[256]{0:T(256)}, u32[]{:S(2)}) %copy-start.2) | copy-done | bytes 1048
  14.5 0.0 copy-done.3
  14.5 0.0 copy-done.1
  14.5 0.0 copy-start.5
  14.5 0.2 shard_map.78
  14.7 0.5 %collective-permute-start = (f32[2,128]{1,0:T(2,128)S(1)}, f32[2,128]{1,0:T(2,128)S(1)}, u32[]{:S(2)}, u32[]{:S(2)}) collective-permute-start(f32[2,128]{1,0:T(2,128)S(1)} %get-tuple-element.14), channel_id=1, source_target_pairs={{0,1},{1,0},{2,3},{3,2},{4,5},{5,4},{6,7},{7,6},{8,9},{9,8},{10,11... | collective-permute-start | bytes 3080 | tf_op jit(solution)/shard_map/ppermute | solution.py:325
  15.2 0.8 %collective-permute-done.got_ref = f32[2,128]{1,0:T(2,128)S(1)} collective-permute-done((f32[2,128]{1,0:T(2,128)S(1)}, f32[2,128]{1,0:T(2,128)S(1)}, u32[]{:S(2)}, u32[]{:S(2)}) %collective-permute-start) | collective-permute-done | bytes 1056 | tf_op jit(solution)/shard_map/ppermute | solution.py:325
  16.1 2.7 %collective-permute-start.1 = (f32[8,128]{1,0:T(8,128)S(1)}, f32[8,128]{1,0:T(8,128)S(1)}, u32[]{:S(2)}, u32[]{:S(2)}) collective-permute-start(f32[8,128]{1,0:T(8,128)S(1)} %shard_map.79), channel_id=1, source_target_pairs={{0,64},{1,193},{2,66},{3,195},{4,68},{5,197},{6,70},{7,199},{8,72}... | collective-permute-start | bytes 12296 | tf_op jit(solution)/shard_map/ppermute | solution.py:334
  18.8 0.0 copy-done.5
  18.8 0.0 copy-start.4
  18.8 1.0 %copy-done.4 = bf16[640,256]{1,0:T(8,128)(2,1)S(1)} copy-done((bf16[640,256]{1,0:T(8,128)(2,1)S(1)}, bf16[640,256]{1,0:T(8,128)(2,1)}, u32[]{:S(2)}) %copy-start.4) | copy-done | bytes 327704
  19.8 0.6 %shard_map.77 = (bf16[640,256]{1,0:T(8,128)(2,1)S(1)}, f32[2,40,128]{2,1,0:T(8,128)S(1)}, f32[2,264,128]{2,1,0:T(8,128)S(1)}, bf16[256,256]{1,0:T(8,128)(2,1)S(1)}) custom-call(s32[1]{0:T(128)} %bitcast.position_ref, s32[1,256]{1,0:T(1,128)S(1)} %bitcast.22, f32[1,256]{1,0:T(1,128)S(1)} %bitcast.24, f32[1,256]{1,0:T(1,128)S(1)} %bitcast.26, ...), custom_call_target="tpu_custom_call" | custom-call | flops 1000000000 | bytes 2097152 | tf_op jit(solution)/shard_map/pallas_call | solution.py:298
  20.4 0.0 collective-permute-done.1.edges_ref
  20.4 0.1 shard_map.80
  20.5 5.2 %all-to-all-done = f32[64,8,128]{2,1,0:T(8,128)S(1)} async-done(((f32[64,8,128]{2,1,0:T(8,128)}), f32[64,8,128]{2,1,0:T(8,128)S(1)}, u32[]{:S(2)}, u32[]{:S(2)}) %all-to-all-start) | async-done | bytes 262176 | tf_op jit(solution)/shard_map/all_to_all | solution.py:297
  25.8 1.1 %shard_map.81 = f32[640,128]{1,0:T(8,128)S(1)} custom-call(s32[1]{0:T(128)} %bitcast.position_ref, f32[512,128]{1,0:T(8,128)S(1)} %bitcast.20, f32[2,264,128]{2,1,0:T(8,128)S(1)} %get-tuple-element.12.phase_ref, f32[4,128]{1,0:T(4,128)S(1)} %get-tuple-element.15.halo_ref, f32[2,72,128]{2,1,0:T(8,128)S(1)} %get-tuple-element.16.halo_phase_ref, ...), custom_call_target="tpu_custom_call" | custom-call | flops 1000000000 | bytes 2097152 | tf_op jit(solution)/shard_map/pallas_call | solution.py:344
  26.9 19.1 %all_to_all.10 = f32[64,5,2,128]{3,2,1,0:T(2,128)S(1)} all-to-all(f32[64,5,2,128]{3,2,1,0:T(2,128)S(1)} %bitcast.19), channel_id=1, replica_groups=mesh['rad'=4,'az'=64] {'az'}, dimensions={0} | all-to-all | bytes 655360 | tf_op jit(solution)/shard_map/all_to_all | solution.py:354
  45.9 1.0 %shard_map.82 = (f32[2,256,128]{2,1,0:T(8,128)}, f32[2,256,128]{2,1,0:T(8,128)}) custom-call(f32[640,128]{1,0:T(8,128)S(1)} %bitcast.16, bf16[256,256]{1,0:T(8,128)(2,1)S(1)} %get-tuple-element.19.matrix_ref), custom_call_target="tpu_custom_call" | custom-call | tf_op jit(solution)/shard_map/pallas_call | solution.py:356
  (1 shorter events, 0.0 us)
Async XLA Ops:
  0.6 13.2 %copy-start = (f32[2,1,256,128]{3,2,1,0:T(8,128)S(1)}, f32[2,1,256,128]{3,2,1,0:T(8,128)}, u32[]{:S(2)}) copy-start(f32[2,1,256,128]{3,2,1,0:T(8,128)} %param.6) | copy-start | bytes 786436
  0.6 25.1 %all-to-all-start = ((f32[64,8,128]{2,1,0:T(8,128)}), f32[64,8,128]{2,1,0:T(8,128)S(1)}, u32[]{:S(2)}, u32[]{:S(2)}) async-start(f32[64,8,128]{2,1,0:T(8,128)} %bitcast.17), calls=%async_computation | async-start | bytes 524288 | tf_op jit(solution)/shard_map/all_to_all | solution.py:297
  13.8 0.7 %copy-start.2 = (f32[256]{0:T(256)S(1)}, f32[256]{0:T(256)}, u32[]{:S(2)}) copy-start(f32[256]{0:T(256)} %param.8) | copy-start | bytes 3076
  13.8 0.7 %copy-start.3 = (f32[256]{0:T(256)S(1)}, f32[256]{0:T(256)}, u32[]{:S(2)}) copy-start(f32[256]{0:T(256)} %param.9) | copy-start | bytes 3076
  13.8 0.7 %copy-start.1 = (s32[256]{0:T(256)S(1)}, s32[256]{0:T(256)}, u32[]{:S(2)}) copy-start(s32[256]{0:T(256)} %param.7) | copy-start | bytes 3076
  14.5 4.3 %copy-start.5 = (f32[128,128]{1,0:T(8,128)S(1)}, f32[128,128]{1,0:T(8,128)}, u32[]{:S(2)}) copy-start(f32[128,128]{1,0:T(8,128)} %constant.13.clone.compact_ref) | copy-start | bytes 196612
  14.7 1.4 %collective-permute-start = (f32[2,128]{1,0:T(2,128)S(1)}, f32[2,128]{1,0:T(2,128)S(1)}, u32[]{:S(2)}, u32[]{:S(2)}) collective-permute-start(f32[2,128]{1,0:T(2,128)S(1)} %get-tuple-element.14), channel_id=1, source_target_pairs={{0,1},{1,0},{2,3},{3,2},{4,5},{5,4},{6,7},{7,6},{8,9},{9,8},{10,11... | collective-permute-start | bytes 3080 | tf_op jit(solution)/shard_map/ppermute | solution.py:325
  16.1 4.4 %collective-permute-start.1 = (f32[8,128]{1,0:T(8,128)S(1)}, f32[8,128]{1,0:T(8,128)S(1)}, u32[]{:S(2)}, u32[]{:S(2)}) collective-permute-start(f32[8,128]{1,0:T(8,128)S(1)} %shard_map.79), channel_id=1, source_target_pairs={{0,64},{1,193},{2,66},{3,195},{4,68},{5,197},{6,70},{7,199},{8,72}... | collective-permute-start | bytes 12296 | tf_op jit(solution)/shard_map/ppermute | solution.py:334
  18.8 1.0 %copy-start.4 = (bf16[640,256]{1,0:T(8,128)(2,1)S(1)}, bf16[640,256]{1,0:T(8,128)(2,1)}, u32[]{:S(2)}) copy-start(bf16[640,256]{1,0:T(8,128)(2,1)} %constant.14.clone.table_ref) | copy-start | bytes 983044

commit v5 on v4

--- a/solution.py
+++ b/solution.py
@@ -10,6 +10,8 @@
 from jax.sharding import PartitionSpec as P
 
 BLOCK = 128
+THERE = (41, 59)
+BACK = (41, 47)
 VMEM = pl.BlockSpec(memory_space=pltpu.VMEM)
 SMEM = pl.BlockSpec(memory_space=pltpu.SMEM)
 HBM = pl.BlockSpec(memory_space=pltpu.HBM)
@@ -46,6 +48,11 @@
     return dot(left[0], right[0]) + (dot(left[0], right[1]) + dot(left[1], right[0]))
 
 
+def listed(order, groups):
+    first, step = order
+    return [(first + step * place) % groups for place in range(groups)]
+
+
 def fourier_tables(groups, width):
     half = groups // 2
     low = np.arange(half + 1)
@@ -55,7 +62,7 @@
     forward = np.concatenate([cosine, -sine[1:half]])
     inverse = np.concatenate([cosine[:1], 2 * cosine[1:half], cosine[half:], -2 * sine[1:half]]).T / (groups * width)
     across = []
-    for table in (forward, inverse):
+    for table in (forward[:, listed(THERE, groups)], inverse[listed(BACK, groups)]):
         high, low = halves(table)
         across.append(np.pad(np.concatenate([high, high, low], axis=1), ((0, 0), (0, 2 * width - 3 * groups))))
     grid = 2 * np.pi * (column[:, None] * column[None, :] % width) / width
@@ -70,7 +77,7 @@
 
 
 def prepare_kernel(
-    position_ref, whole_ref, frac_ref, spacing_ref, compact_ref, table_ref,
+    part_ref, whole_ref, frac_ref, spacing_ref, compact_ref, table_ref,
     table_out, twist_out, phase_out, matrix_out,
     *, groups, rows,
 ):
@@ -97,7 +104,7 @@
     edge = half + groups * jnp.where(edge < width // 2, edge, edge - width)
     edge_row = lax.broadcasted_iota(jnp.int32, (rows, width), 0)
     lane = lax.broadcasted_iota(jnp.int32, (rows, row_count), 1)
-    first = lax.rem(position_ref[0] * rows, row_count)
+    first = lax.rem(part_ref[0] * rows, row_count)
     own = lane == first + lax.broadcasted_iota(jnp.int32, (rows, row_count), 0)
     wholes = jnp.sum(jnp.where(own, whole_ref[...].astype(jnp.float32), 0.0), axis=1, keepdims=True).astype(jnp.int32)
     fracs = jnp.sum(jnp.where(own, frac_ref[...], 0.0), axis=1, keepdims=True)
@@ -164,7 +171,7 @@
     return dot(back, stacked(blocks))
 
 
-def edge_kernel(position_ref, whole_ref, frac_ref, _, cells_ref, keep_out, give_out, tiles, sems):
+def edge_kernel(position_ref, cells_ref, keep_out, give_out, tiles, sems):
     sets, row_count, width = cells_ref.shape
     depth = tiles.shape[2]
     loads = []
@@ -178,20 +185,21 @@
     is_odd = position_ref[0] & 1 == 1
     last = [tiles[0, field, depth - 1 :, :] for field in range(sets)]
     first = [tiles[1, field, :1, :] for field in range(sets)]
-    shifts = []
-    for ref in (whole_ref, frac_ref):
-        shift = jnp.where(is_odd, ref[:, :1].astype(jnp.float32), ref[:, row_count - 1 :].astype(jnp.float32))
-        shifts.append(jnp.broadcast_to(shift, (1, width)))
     keep = [jnp.where(is_odd, theirs, ours) for ours, theirs in zip(last, first, strict=True)]
-    keep_out[...] = jnp.concatenate(keep + shifts, axis=0)
+    keep_out[...] = jnp.concatenate(keep, axis=0)
     give_out[...] = jnp.concatenate([jnp.where(is_odd, ours, theirs) for ours, theirs in zip(last, first, strict=True)], axis=0)
 
 
-def join_kernel(keep_ref, got_ref, out_ref):
-    sets, _ = got_ref.shape
+def join_kernel(position_ref, whole_ref, frac_ref, _, keep_ref, got_ref, out_ref):
+    sets, width = keep_ref.shape
+    is_odd = position_ref[0] & 1 == 1
+    last = whole_ref.shape[1] - 1
     out_ref[...] = jnp.zeros_like(out_ref)
-    out_ref[pl.ds(0, sets + 2), :] = keep_ref[...]
-    out_ref[pl.ds(sets + 2, sets), :] = got_ref[...]
+    out_ref[pl.ds(0, sets), :] = keep_ref[...]
+    out_ref[pl.ds(sets, sets), :] = got_ref[...]
+    for place, ref in enumerate((whole_ref, frac_ref)):
+        shift = jnp.where(is_odd, ref[:, :1].astype(jnp.float32), ref[:, last:].astype(jnp.float32))
+        out_ref[pl.ds(2 * sets + place, 1), :] = jnp.broadcast_to(shift, (1, width))
 
 
 def halo_kernel(position_ref, block_ref, edges_ref, phase_out, halo_out, *, groups, rows, blocks):
@@ -199,10 +207,10 @@
     is_end = jnp.where(is_odd, block_ref[0] == blocks - 1, block_ref[0] == 0)
     cells = edges_ref[...]
     sets = halo_out.shape[0] // 2
-    keep, got = cells[:sets], cells[sets + 2 : 2 * sets + 2]
+    keep, got = cells[:sets], cells[sets : 2 * sets]
     both = jnp.where(is_odd, jnp.concatenate([got, keep], axis=0), jnp.concatenate([keep, got], axis=0))
     halo_out[...] = jnp.where(is_end, 0.0, both)
-    whole, frac = cells[sets : sets + 1].astype(jnp.int32), cells[sets + 1 : sets + 2]
+    whole, frac = cells[2 * sets : 2 * sets + 1].astype(jnp.int32), cells[2 * sets + 1 : 2 * sets + 2]
     width = phase_out.shape[2]
     half = groups // 2
     shape = (half, width)
@@ -228,7 +236,9 @@
     half = groups // 2
     signals = [signal_ref[pl.ds(row, groups, stride=rows), :] for row in range(rows)]
     width = signals[0].shape[1]
-    group = lax.broadcasted_iota(jnp.int32, (groups, width), 0) - (position_ref[0] & -2)
+    first, step = THERE
+    group = (first + step * lax.broadcasted_iota(jnp.int32, (groups, width), 0)) & (groups - 1)
+    group -= position_ref[0] & -2
     for field in range(sets):
         even, odd = halo_ref[field : field + 1, :], halo_ref[sets + field : sets + field + 1, :]
         signals.append(jnp.where(group == 0, even, jnp.where(group == 1, odd, 0.0)))
@@ -248,17 +258,19 @@
     field_count, row_count, width = remapped.shape
     pitch = cells_ref.shape[0] // groups
     parts = row_count // rows
-    for group in range(groups):
-        here = pl.ds(group % parts * rows, rows)
-        remapped[group // parts, here, :] = cells_ref[pl.ds(group * pitch, rows), :]
+    there, back = listed(THERE, groups), listed(BACK, groups)
+    for place, group in enumerate(back):
+        part = there.index(group)
+        here = pl.ds(part % parts * rows, rows)
+        remapped[part // parts, here, :] = cells_ref[pl.ds(place * pitch, rows), :]
     stores = [pltpu.make_async_copy(remapped, remapped_out, sems.at[field_count])]
     stores[0].start()
 
     def total(place):
         return jnp.sum(cells_ref[pl.ds(place, groups // 2, stride=2 * pitch), :], axis=0, keepdims=True)
 
-    before = [total(rows + field) for field in range(field_count)]
-    after = [total(pitch + rows + field) for field in range(field_count)]
+    before = [total(back[0] % 2 * pitch + rows + field) for field in range(field_count)]
+    after = [total((1 - back[0] % 2) * pitch + rows + field) for field in range(field_count)]
 
     row = lax.broadcasted_iota(jnp.int32, (row_count, width), 0)
     for field in range(field_count):
@@ -285,6 +297,7 @@
     groups = lax.axis_size("az")
     blocks = lax.axis_size("rad")
     column = lax.axis_index("az").astype(jnp.int32).reshape(1)
+    part = (column - THERE[0]) * pow(THERE[1], -1, groups) & (groups - 1)
     block = lax.axis_index("rad").astype(jnp.int32).reshape(1)
     field_count, plane_count, row_count, width = fields.shape
     sets = field_count * plane_count
@@ -294,7 +307,9 @@
     shifts = [row.reshape(1, row_count) for row in (whole_shift, frac_shift, inv_spacing)]
     float_of = functools.partial(jax.ShapeDtypeStruct, dtype=jnp.float32)
 
-    signal = lax.all_to_all(fields.reshape(groups, rows, width), "az", 0, 0, tiled=True)
+    signal = lax.all_to_all(
+        fields.reshape(groups, rows, width), "az", 0, 0, axis_index_groups=[listed(THERE, groups)], tiled=True
+    )
     table, twist, phases, matrix = pl.pallas_call(
         functools.partial(prepare_kernel, groups=groups, rows=rows),
         out_shape=(
@@ -308,7 +323,7 @@
         compiler_params=PARAMS,
         cost_estimate=pl.CostEstimate(flops=10**9, transcendentals=10**5, bytes_accessed=2**21),
     )(
-        column,
+        part,
         *shifts,
         jnp.asarray(compact_inverse(BLOCK)),
         jnp.asarray(table),
@@ -316,20 +331,20 @@
     planes = fields.reshape(sets, row_count, width)
     keep, give = pl.pallas_call(
         edge_kernel,
-        out_shape=(float_of((sets + 2, width)), float_of((sets, width))),
-        in_specs=[SMEM] + [VMEM] * 3 + [HBM],
+        out_shape=(float_of((sets, width)),) * 2,
+        in_specs=[SMEM, HBM],
         out_specs=(VMEM,) * 2,
         scratch_shapes=[pltpu.VMEM((2, sets, 8, width), jnp.float32), pltpu.SemaphoreType.DMA((2, sets))],
         compiler_params=PARAMS,
-    )(column, *shifts, planes)
+    )(column, planes)
     got = lax.ppermute(give, "az", [(i, i ^ 1) for i in range(groups)])
     edges = pl.pallas_call(
         join_kernel,
         out_shape=float_of((8, width)),
-        in_specs=[VMEM] * 2,
+        in_specs=[SMEM] + [VMEM] * 5,
         out_specs=VMEM,
         compiler_params=PARAMS,
-    )(keep, got)
+    )(column, *shifts, keep, got)
     pairs = [(i, j, (i + 1 - 2 * (j & 1)) % blocks) for i in range(blocks) for j in range(groups)]
     edges = lax.ppermute(edges, ("rad", "az"), [(i * groups + j, k * groups + j) for i, j, k in pairs])
     halo_phases, halo = pl.pallas_call(
@@ -351,7 +366,8 @@
         cost_estimate=pl.CostEstimate(flops=10**9, transcendentals=0, bytes_accessed=2**21),
     )(column, signal.reshape(groups * rows, width), phases, halo, halo_phases, table, twist)
     signal = signal.reshape(groups, pitch // 2, 2, width)
-    signal = lax.all_to_all(signal, "az", 0, 0, tiled=True).reshape(groups * pitch, width)
+    signal = lax.all_to_all(signal, "az", 0, 0, axis_index_groups=[listed(BACK, groups)], tiled=True)
+    signal = signal.reshape(groups * pitch, width)
     whole_shape = (sets, row_count, width)
     remapped, radial = pl.pallas_call(
         functools.partial(derivative_kernel, groups=groups, rows=rows),

time: 47.2 us -> 43.4 us (0.919)
  waiting for transfers between devices: 6.06 us -> 1.41 us
  starting transfers between devices: 16.4 us -> 18.3 us
  local copies, waits for them, and re-layouts: 1.66 us -> 0.7 us
    all_to_all x1, waiting for transfers between devices: 5.24 us -> 0.49 us  [on_device(): lax.all_to_all(fields.reshape(groups, rows, width), 'az', 0, 0, axis_inde...]
    all_to_all x1, starting transfers between devices: 13.1 us -> 15 us  [on_device(): lax.all_to_all(fields.reshape(groups, rows, width), 'az', 0, 0, axis_inde...]
    unnamed x12, local copies, waits for them, and re-layouts: 1.66 us -> 0.7 us
  transfers between devices with their start and end apart: 3 -> 3, of which waited for: 2 -> 3; matrix products, arithmetic and copies ran while one was open for 0% -> 0% of each run, Pallas kernels for 2% -> 2%
where the time goes in v5:
time: 43.4 us; the launch traced here: 43.2 us
  blocking collectives  19.1 us (44%)
  starting transfers between devices  18.3 us (42%)
  Pallas kernels  3 us (7%)
  waiting for transfers between devices  1.41 us (3%)
  local copies, waits for them, and re-layouts  0.7 us (2%)
  between operations  0.7 us (2%)
    all_to_all x1, blocking collectives, on_device(): lax.all_to_all(signal, 'az', 0, 0, axis_index_groups=[listed(BACK, groups...  19.1 us
    all_to_all x1, starting transfers between devices, on_device(): lax.all_to_all(fields.reshape(groups, rows, width), 'az', 0, 0, axis_inde...  15 us
    ppermute x1, starting transfers between devices, on_device(): lax.ppermute(edges, ('rad', 'az'), [(i * groups + j, k * groups + j) for...  2.73 us
    pallas_call x1, Pallas kernels, on_device(): pl.pallas_call(functools.partial(shear_kernel, groups=groups, rows=rows),...  1.09 us
    pallas_call x1, Pallas kernels, on_device(): pl.pallas_call(functools.partial(derivative_kernel, groups=groups, rows=r...  0.96 us
  transfers between devices with their start and end apart: 3, of which 3 were waited for; matrix products, arithmetic and copies ran while one was open for 0% of the time, Pallas kernels for 2%

profile of v5, /device:TPU:1, one launch (start us, length us, event | category | flops | bytes accessed | tf_op | source)
XLA Modules:
  0.0 43.2 jit_solution(14444438687486370397)
XLA Ops:
  0.6 0.0 copy-start
  0.6 0.0 copy-start.4
  0.7 15.0 %all-to-all-start = ((f32[64,8,128]{2,1,0:T(8,128)}), f32[64,8,128]{2,1,0:T(8,128)S(1)}, u32[]{:S(2)}, u32[]{:S(2)}) async-start(f32[64,8,128]{2,1,0:T(8,128)} %bitcast.17), calls=%async_computation | async-start | bytes 524288 | tf_op jit(solution)/shard_map/all_to_all | solution.py:310
  15.7 0.0 copy-done
  15.7 0.0 copy-start.5
  15.7 0.1 shard_map.78
  15.8 0.5 %collective-permute-start = (f32[2,128]{1,0:T(2,128)S(1)}, f32[2,128]{1,0:T(2,128)S(1)}, u32[]{:S(2)}, u32[]{:S(2)}) collective-permute-start(f32[2,128]{1,0:T(2,128)S(1)} %get-tuple-element.14), channel_id=1, source_target_pairs={{0,1},{1,0},{2,3},{3,2},{4,5},{5,4},{6,7},{7,6},{8,9},{9,8},{10,11... | collective-permute-start | bytes 3080 | tf_op jit(solution)/shard_map/ppermute | solution.py:340
  16.3 0.0 copy-start.2
  16.3 0.0 copy-start.3
  16.3 0.8 %collective-permute-done.got_ref = f32[2,128]{1,0:T(2,128)S(1)} collective-permute-done((f32[2,128]{1,0:T(2,128)S(1)}, f32[2,128]{1,0:T(2,128)S(1)}, u32[]{:S(2)}, u32[]{:S(2)}) %collective-permute-start) | collective-permute-done | bytes 1056 | tf_op jit(solution)/shard_map/ppermute | solution.py:340
  17.1 0.0 copy-done.2
  17.1 0.0 copy-done.3
  17.1 0.7 %copy-done.1 = s32[256]{0:T(256)S(1)} copy-done((s32[256]{0:T(256)S(1)}, s32[256]{0:T(256)}, u32[]{:S(2)}) %copy-start.1) | copy-done | bytes 1048
  17.8 0.1 shard_map.79
  17.9 2.7 %collective-permute-start.1 = (f32[8,128]{1,0:T(8,128)S(1)}, f32[8,128]{1,0:T(8,128)S(1)}, u32[]{:S(2)}, u32[]{:S(2)}) collective-permute-start(f32[8,128]{1,0:T(8,128)S(1)} %shard_map.79), channel_id=1, source_target_pairs={{0,64},{1,193},{2,66},{3,195},{4,68},{5,197},{6,70},{7,199},{8,72}... | collective-permute-start | bytes 12296 | tf_op jit(solution)/shard_map/ppermute | solution.py:349
  20.7 0.0 copy-done.4
  20.7 0.0 copy-done.5
  20.7 0.6 %shard_map.77 = (bf16[640,256]{1,0:T(8,128)(2,1)S(1)}, f32[2,40,128]{2,1,0:T(8,128)S(1)}, f32[2,264,128]{2,1,0:T(8,128)S(1)}, bf16[256,256]{1,0:T(8,128)(2,1)S(1)}) custom-call(s32[1]{0:T(128)S(6)} %and.5.part_ref, s32[1,256]{1,0:T(1,128)S(1)} %bitcast.22, f32[1,256]{1,0:T(1,128)S(1)} %bitcast.24, f32[1,256]{1,0:T(1,128)S(1)} %bitcast.26, ...), custom_call_target="tpu_custom_call" | custom-call | flops 1000000000 | bytes 2097152 | tf_op jit(solution)/shard_map/pallas_call | solution.py:313
  21.3 0.1 collective-permute-done.1.edges_ref
  21.4 0.1 shard_map.80
  21.5 0.5 %all-to-all-done = f32[64,8,128]{2,1,0:T(8,128)S(1)} async-done(((f32[64,8,128]{2,1,0:T(8,128)}), f32[64,8,128]{2,1,0:T(8,128)S(1)}, u32[]{:S(2)}, u32[]{:S(2)}) %all-to-all-start) | async-done | bytes 262176 | tf_op jit(solution)/shard_map/all_to_all | solution.py:310
  22.0 1.1 %shard_map.81 = f32[640,128]{1,0:T(8,128)S(1)} custom-call(s32[1]{0:T(128)} %bitcast.position_ref, f32[512,128]{1,0:T(8,128)S(1)} %bitcast.20, f32[2,264,128]{2,1,0:T(8,128)S(1)} %get-tuple-element.12.phase_ref, f32[4,128]{1,0:T(4,128)S(1)} %get-tuple-element.15.halo_ref, f32[2,72,128]{2,1,0:T(8,128)S(1)} %get-tuple-element.16.halo_phase_ref, ...), custom_call_target="tpu_custom_call" | custom-call | flops 1000000000 | bytes 2097152 | tf_op jit(solution)/shard_map/pallas_call | solution.py:359
  23.1 19.1 %all_to_all.10 = f32[64,5,2,128]{3,2,1,0:T(2,128)S(1)} all-to-all(f32[64,5,2,128]{3,2,1,0:T(2,128)S(1)} %bitcast.19), channel_id=1, replica_groups={{41,24,7,54,37,20,3,50,33,16,63,46,29,12,59,42,25,8,55,38,21,4,51,34,17..., dimensions={0} | all-to-all | bytes 655360 | tf_op jit(solution)/shard_map/all_to_all | solution.py:369
  42.2 1.0 %shard_map.82 = (f32[2,256,128]{2,1,0:T(8,128)}, f32[2,256,128]{2,1,0:T(8,128)}) custom-call(f32[640,128]{1,0:T(8,128)S(1)} %bitcast.16, bf16[256,256]{1,0:T(8,128)(2,1)S(1)} %get-tuple-element.19.matrix_ref), custom_call_target="tpu_custom_call" | custom-call | tf_op jit(solution)/shard_map/pallas_call | solution.py:372
  (1 shorter events, 0.0 us)
Async XLA Ops:
  0.6 15.1 %copy-start = (f32[2,1,256,128]{3,2,1,0:T(8,128)S(1)}, f32[2,1,256,128]{3,2,1,0:T(8,128)}, u32[]{:S(2)}) copy-start(f32[2,1,256,128]{3,2,1,0:T(8,128)} %param.6) | copy-start | bytes 786436
  0.6 20.0 %copy-start.4 = (bf16[640,256]{1,0:T(8,128)(2,1)S(1)}, bf16[640,256]{1,0:T(8,128)(2,1)}, u32[]{:S(2)}) copy-start(bf16[640,256]{1,0:T(8,128)(2,1)} %constant.21.clone.table_ref) | copy-start | bytes 983044
  0.7 21.4 %all-to-all-start = ((f32[64,8,128]{2,1,0:T(8,128)}), f32[64,8,128]{2,1,0:T(8,128)S(1)}, u32[]{:S(2)}, u32[]{:S(2)}) async-start(f32[64,8,128]{2,1,0:T(8,128)} %bitcast.17), calls=%async_computation | async-start | bytes 524288 | tf_op jit(solution)/shard_map/all_to_all | solution.py:310
  15.7 5.0 %copy-start.5 = (f32[128,128]{1,0:T(8,128)S(1)}, f32[128,128]{1,0:T(8,128)}, u32[]{:S(2)}) copy-start(f32[128,128]{1,0:T(8,128)} %constant.20.clone.compact_ref) | copy-start | bytes 196612
  15.8 1.3 %collective-permute-start = (f32[2,128]{1,0:T(2,128)S(1)}, f32[2,128]{1,0:T(2,128)S(1)}, u32[]{:S(2)}, u32[]{:S(2)}) collective-permute-start(f32[2,128]{1,0:T(2,128)S(1)} %get-tuple-element.14), channel_id=1, source_target_pairs={{0,1},{1,0},{2,3},{3,2},{4,5},{5,4},{6,7},{7,6},{8,9},{9,8},{10,11... | collective-permute-start | bytes 3080 | tf_op jit(solution)/shard_map/ppermute | solution.py:340
  16.3 0.8 %copy-start.2 = (f32[256]{0:T(256)S(1)}, f32[256]{0:T(256)}, u32[]{:S(2)}) copy-start(f32[256]{0:T(256)} %param.8) | copy-start | bytes 3076
  16.3 0.8 %copy-start.3 = (f32[256]{0:T(256)S(1)}, f32[256]{0:T(256)}, u32[]{:S(2)}) copy-start(f32[256]{0:T(256)} %param.9) | copy-start | bytes 3076
  17.1 0.7 %copy-start.1 = (s32[256]{0:T(256)S(1)}, s32[256]{0:T(256)}, u32[]{:S(2)}) copy-start(s32[256]{0:T(256)} %param.7) | copy-start | bytes 3076
  17.9 3.5 %collective-permute-start.1 = (f32[8,128]{1,0:T(8,128)S(1)}, f32[8,128]{1,0:T(8,128)S(1)}, u32[]{:S(2)}, u32[]{:S(2)}) collective-permute-start(f32[8,128]{1,0:T(8,128)S(1)} %shard_map.79), channel_id=1, source_target_pairs={{0,64},{1,193},{2,66},{3,195},{4,68},{5,197},{6,70},{7,199},{8,72}... | collective-permute-start | bytes 12296 | tf_op jit(solution)/shard_map/ppermute | solution.py:349

commit v6 on v5

--- a/solution.py
+++ b/solution.py
@@ -10,7 +10,7 @@
 from jax.sharding import PartitionSpec as P
 
 BLOCK = 128
-THERE = (41, 59)
+THERE = (43, 59)
 BACK = (41, 47)
 VMEM = pl.BlockSpec(memory_space=pltpu.VMEM)
 SMEM = pl.BlockSpec(memory_space=pltpu.SMEM)
@@ -345,8 +345,11 @@
         out_specs=VMEM,
         compiler_params=PARAMS,
     )(column, *shifts, keep, got)
-    pairs = [(i, j, (i + 1 - 2 * (j & 1)) % blocks) for i in range(blocks) for j in range(groups)]
-    edges = lax.ppermute(edges, ("rad", "az"), [(i * groups + j, k * groups + j) for i, j, k in pairs])
+    turns = []
+    for place in range(blocks * groups):
+        step = -groups if place % 2 else groups
+        turns.append((place, place + step if 0 <= place + step < blocks * groups else place ^ 1))
+    edges = lax.ppermute(edges, ("rad", "az"), turns)
     halo_phases, halo = pl.pallas_call(
         functools.partial(halo_kernel, groups=groups, rows=rows, blocks=blocks),
         out_shape=(float_of((2, sets * half + rows, width)), float_of((2 * sets, width))),

time: 43.4 us -> 43.1 us (level)
  starting transfers between devices: 18.3 us -> 15.1 us
  waiting for transfers between devices: 1.41 us -> 4.37 us
    ppermute x1, starting transfers between devices: 2.73 us -> 0.32 us  [on_device(): edges = lax.ppermute(edges, ('rad', 'az'), turns)]
    ppermute x1, waiting for transfers between devices: 0.1 us -> 1.78 us  [on_device(): edges = lax.ppermute(edges, ('rad', 'az'), turns)]
    all_to_all x1, waiting for transfers between devices: 0.49 us -> 1.77 us  [on_device(): lax.all_to_all(fields.reshape(groups, rows, width), 'az', 0, 0, axis_inde...]
    all_to_all x1, starting transfers between devices: 15 us -> 14.2 us  [on_device(): lax.all_to_all(fields.reshape(groups, rows, width), 'az', 0, 0, axis_inde...]
where the time goes in v6:
time: 43.1 us; the launch traced here: 42.9 us
  blocking collectives  19 us (44%)
  starting transfers between devices  15.1 us (35%)
  waiting for transfers between devices  4.37 us (10%)
  Pallas kernels  2.99 us (7%)
  local copies, waits for them, and re-layouts  0.7 us (2%)
  between operations  0.7 us (2%)
    all_to_all x1, blocking collectives, on_device(): lax.all_to_all(signal, 'az', 0, 0, axis_index_groups=[listed(BACK, groups...  19 us
    all_to_all x1, starting transfers between devices, on_device(): lax.all_to_all(fields.reshape(groups, rows, width), 'az', 0, 0, axis_inde...  14.2 us
    ppermute x1, waiting for transfers between devices, on_device(): edges = lax.ppermute(edges, ('rad', 'az'), turns)  1.78 us
    all_to_all x1, waiting for transfers between devices, on_device(): lax.all_to_all(fields.reshape(groups, rows, width), 'az', 0, 0, axis_inde...  1.77 us
    pallas_call x1, Pallas kernels, on_device(): pl.pallas_call(functools.partial(shear_kernel, groups=groups, rows=rows),...  1.09 us
    pallas_call x1, Pallas kernels, on_device(): pl.pallas_call(functools.partial(derivative_kernel, groups=groups, rows=r...  0.96 us
  transfers between devices with their start and end apart: 3, of which 3 were waited for; matrix products, arithmetic and copies ran while one was open for 0% of the time, Pallas kernels for 2%

profile of v6, /device:TPU:1, one launch (start us, length us, event | category | flops | bytes accessed | tf_op | source)
XLA Modules:
  0.0 42.9 jit_solution(290501303077089273)
XLA Ops:
  0.6 0.0 copy-start
  0.6 0.0 copy-start.4
  0.7 14.2 %all-to-all-start = ((f32[64,8,128]{2,1,0:T(8,128)}), f32[64,8,128]{2,1,0:T(8,128)S(1)}, u32[]{:S(2)}, u32[]{:S(2)}) async-start(f32[64,8,128]{2,1,0:T(8,128)} %bitcast.17), calls=%async_computation | async-start | bytes 524288 | tf_op jit(solution)/shard_map/all_to_all | solution.py:310
  14.9 0.0 copy-done
  14.9 0.0 copy-start.5
  14.9 0.1 shard_map.78
  15.0 0.6 %collective-permute-start = (f32[2,128]{1,0:T(2,128)S(1)}, f32[2,128]{1,0:T(2,128)S(1)}, u32[]{:S(2)}, u32[]{:S(2)}) collective-permute-start(f32[2,128]{1,0:T(2,128)S(1)} %get-tuple-element.14), channel_id=1, source_target_pairs={{0,1},{1,0},{2,3},{3,2},{4,5},{5,4},{6,7},{7,6},{8,9},{9,8},{10,11... | collective-permute-start | bytes 3080 | tf_op jit(solution)/shard_map/ppermute | solution.py:340
  15.6 0.0 copy-start.2
  15.6 0.0 copy-start.3
  15.6 0.8 %collective-permute-done.got_ref = f32[2,128]{1,0:T(2,128)S(1)} collective-permute-done((f32[2,128]{1,0:T(2,128)S(1)}, f32[2,128]{1,0:T(2,128)S(1)}, u32[]{:S(2)}, u32[]{:S(2)}) %collective-permute-start) | collective-permute-done | bytes 1056 | tf_op jit(solution)/shard_map/ppermute | solution.py:340
  16.4 0.0 copy-done.2
  16.4 0.0 copy-done.3
  16.4 0.7 %copy-done.1 = s32[256]{0:T(256)S(1)} copy-done((s32[256]{0:T(256)S(1)}, s32[256]{0:T(256)}, u32[]{:S(2)}) %copy-start.1) | copy-done | bytes 1048
  17.1 0.1 shard_map.79
  17.2 0.3 collective-permute-start.1
  17.5 0.0 copy-done.4
  17.5 0.0 copy-done.5
  17.5 0.6 %shard_map.77 = (bf16[640,256]{1,0:T(8,128)(2,1)S(1)}, f32[2,40,128]{2,1,0:T(8,128)S(1)}, f32[2,264,128]{2,1,0:T(8,128)S(1)}, bf16[256,256]{1,0:T(8,128)(2,1)S(1)}) custom-call(s32[1]{0:T(128)S(6)} %and.5.part_ref, s32[1,256]{1,0:T(1,128)S(1)} %bitcast.22, f32[1,256]{1,0:T(1,128)S(1)} %bitcast.24, f32[1,256]{1,0:T(1,128)S(1)} %bitcast.26, ...), custom_call_target="tpu_custom_call" | custom-call | flops 1000000000 | bytes 2097152 | tf_op jit(solution)/shard_map/pallas_call | solution.py:313
  18.2 1.8 %collective-permute-done.1.edges_ref = f32[8,128]{1,0:T(8,128)S(1)} collective-permute-done((f32[8,128]{1,0:T(8,128)S(1)}, f32[8,128]{1,0:T(8,128)S(1)}, u32[]{:S(2)}, u32[]{:S(2)}) %collective-permute-start.1) | collective-permute-done | bytes 4128 | tf_op jit(solution)/shard_map/ppermute | solution.py:352
  20.0 0.1 shard_map.80
  20.1 1.8 %all-to-all-done = f32[64,8,128]{2,1,0:T(8,128)S(1)} async-done(((f32[64,8,128]{2,1,0:T(8,128)}), f32[64,8,128]{2,1,0:T(8,128)S(1)}, u32[]{:S(2)}, u32[]{:S(2)}) %all-to-all-start) | async-done | bytes 262176 | tf_op jit(solution)/shard_map/all_to_all | solution.py:310
  21.8 1.1 %shard_map.81 = f32[640,128]{1,0:T(8,128)S(1)} custom-call(s32[1]{0:T(128)} %bitcast.position_ref, f32[512,128]{1,0:T(8,128)S(1)} %bitcast.20, f32[2,264,128]{2,1,0:T(8,128)S(1)} %get-tuple-element.12.phase_ref, f32[4,128]{1,0:T(4,128)S(1)} %get-tuple-element.15.halo_ref, f32[2,72,128]{2,1,0:T(8,128)S(1)} %get-tuple-element.16.halo_phase_ref, ...), custom_call_target="tpu_custom_call" | custom-call | flops 1000000000 | bytes 2097152 | tf_op jit(solution)/shard_map/pallas_call | solution.py:362
  22.9 19.0 %all_to_all.10 = f32[64,5,2,128]{3,2,1,0:T(2,128)S(1)} all-to-all(f32[64,5,2,128]{3,2,1,0:T(2,128)S(1)} %bitcast.19), channel_id=1, replica_groups={{41,24,7,54,37,20,3,50,33,16,63,46,29,12,59,42,25,8,55,38,21,4,51,34,17..., dimensions={0} | all-to-all | bytes 655360 | tf_op jit(solution)/shard_map/all_to_all | solution.py:372
  41.9 1.0 %shard_map.82 = (f32[2,256,128]{2,1,0:T(8,128)}, f32[2,256,128]{2,1,0:T(8,128)}) custom-call(f32[640,128]{1,0:T(8,128)S(1)} %bitcast.16, bf16[256,256]{1,0:T(8,128)(2,1)S(1)} %get-tuple-element.19.matrix_ref), custom_call_target="tpu_custom_call" | custom-call | tf_op jit(solution)/shard_map/pallas_call | solution.py:375
  (1 shorter events, 0.0 us)
Async XLA Ops:
  0.6 14.3 %copy-start = (f32[2,1,256,128]{3,2,1,0:T(8,128)S(1)}, f32[2,1,256,128]{3,2,1,0:T(8,128)}, u32[]{:S(2)}) copy-start(f32[2,1,256,128]{3,2,1,0:T(8,128)} %param.6) | copy-start | bytes 786436
  0.6 16.9 %copy-start.4 = (bf16[640,256]{1,0:T(8,128)(2,1)S(1)}, bf16[640,256]{1,0:T(8,128)(2,1)}, u32[]{:S(2)}) copy-start(bf16[640,256]{1,0:T(8,128)(2,1)} %constant.21.clone.table_ref) | copy-start | bytes 983044
  0.7 21.2 %all-to-all-start = ((f32[64,8,128]{2,1,0:T(8,128)}), f32[64,8,128]{2,1,0:T(8,128)S(1)}, u32[]{:S(2)}, u32[]{:S(2)}) async-start(f32[64,8,128]{2,1,0:T(8,128)} %bitcast.17), calls=%async_computation | async-start | bytes 524288 | tf_op jit(solution)/shard_map/all_to_all | solution.py:310
  14.9 2.6 %copy-start.5 = (f32[128,128]{1,0:T(8,128)S(1)}, f32[128,128]{1,0:T(8,128)}, u32[]{:S(2)}) copy-start(f32[128,128]{1,0:T(8,128)} %constant.20.clone.compact_ref) | copy-start | bytes 196612
  15.0 1.4 %collective-permute-start = (f32[2,128]{1,0:T(2,128)S(1)}, f32[2,128]{1,0:T(2,128)S(1)}, u32[]{:S(2)}, u32[]{:S(2)}) collective-permute-start(f32[2,128]{1,0:T(2,128)S(1)} %get-tuple-element.14), channel_id=1, source_target_pairs={{0,1},{1,0},{2,3},{3,2},{4,5},{5,4},{6,7},{7,6},{8,9},{9,8},{10,11... | collective-permute-start | bytes 3080 | tf_op jit(solution)/shard_map/ppermute | solution.py:340
  15.6 0.8 %copy-start.2 = (f32[256]{0:T(256)S(1)}, f32[256]{0:T(256)}, u32[]{:S(2)}) copy-start(f32[256]{0:T(256)} %param.8) | copy-start | bytes 3076
  15.6 0.8 %copy-start.3 = (f32[256]{0:T(256)S(1)}, f32[256]{0:T(256)}, u32[]{:S(2)}) copy-start(f32[256]{0:T(256)} %param.9) | copy-start | bytes 3076
  16.4 0.7 %copy-start.1 = (s32[256]{0:T(256)S(1)}, s32[256]{0:T(256)}, u32[]{:S(2)}) copy-start(s32[256]{0:T(256)} %param.7) | copy-start | bytes 3076
  17.2 2.8 %collective-permute-start.1 = (f32[8,128]{1,0:T(8,128)S(1)}, f32[8,128]{1,0:T(8,128)S(1)}, u32[]{:S(2)}, u32[]{:S(2)}) collective-permute-start(f32[8,128]{1,0:T(8,128)S(1)} %shard_map.79), channel_id=1, source_target_pairs={{0,64},{1,0},{2,66},{3,2},{4,68},{5,4},{6,70},{7,6},{8,72},{9,8},{... | collective-permute-start | bytes 12296 | tf_op jit(solution)/shard_map/ppermute | solution.py:352

commit v7 on v6

--- a/solution.py
+++ b/solution.py
@@ -10,8 +10,8 @@
 from jax.sharding import PartitionSpec as P
 
 BLOCK = 128
-THERE = (43, 59)
-BACK = (41, 47)
+THERE = (43, 5)
+BACK = (43, 59)
 VMEM = pl.BlockSpec(memory_space=pltpu.VMEM)
 SMEM = pl.BlockSpec(memory_space=pltpu.SMEM)
 HBM = pl.BlockSpec(memory_space=pltpu.HBM)

time: 43.1 us -> 42.3 us (0.981)
  blocking collectives: 19 us -> 17.5 us
  waiting for transfers between devices: 4.37 us -> 5.27 us
    all_to_all x1, blocking collectives: 19 us -> 17.5 us  [on_device(): lax.all_to_all(signal, 'az', 0, 0, axis_index_groups=[listed(BACK, groups...]
    all_to_all x1, waiting for transfers between devices: 1.77 us -> 2.67 us  [on_device(): lax.all_to_all(fields.reshape(groups, rows, width), 'az', 0, 0, axis_inde...]
where the time goes in v7:
time: 42.3 us; the launch traced here: 42.1 us
  blocking collectives  17.5 us (41%)
  starting transfers between devices  14.9 us (35%)
  waiting for transfers between devices  5.27 us (12%)
  Pallas kernels  3 us (7%)
  local copies, waits for them, and re-layouts  0.7 us (2%)
  between operations  0.7 us (2%)
    all_to_all x1, blocking collectives, on_device(): lax.all_to_all(signal, 'az', 0, 0, axis_index_groups=[listed(BACK, groups...  17.5 us
    all_to_all x1, starting transfers between devices, on_device(): lax.all_to_all(fields.reshape(groups, rows, width), 'az', 0, 0, axis_inde...  14.2 us
    all_to_all x1, waiting for transfers between devices, on_device(): lax.all_to_all(fields.reshape(groups, rows, width), 'az', 0, 0, axis_inde...  2.67 us
    ppermute x1, waiting for transfers between devices, on_device(): edges = lax.ppermute(edges, ('rad', 'az'), turns)  1.78 us
    pallas_call x1, Pallas kernels, on_device(): pl.pallas_call(functools.partial(shear_kernel, groups=groups, rows=rows),...  1.09 us
    pallas_call x1, Pallas kernels, on_device(): pl.pallas_call(functools.partial(derivative_kernel, groups=groups, rows=r...  0.96 us
  transfers between devices with their start and end apart: 3, of which 3 were waited for; matrix products, arithmetic and copies ran while one was open for 0% of the time, Pallas kernels for 2%

profile of v7, /device:TPU:1, one launch (start us, length us, event | category | flops | bytes accessed | tf_op | source)
XLA Modules:
  0.0 42.1 jit_solution(8799769578639251744)
XLA Ops:
  0.6 0.0 copy-start
  0.6 0.0 copy-start.4
  0.7 14.2 %all-to-all-start = ((f32[64,8,128]{2,1,0:T(8,128)}), f32[64,8,128]{2,1,0:T(8,128)S(1)}, u32[]{:S(2)}, u32[]{:S(2)}) async-start(f32[64,8,128]{2,1,0:T(8,128)} %bitcast.17), calls=%async_computation | async-start | bytes 524288 | tf_op jit(solution)/shard_map/all_to_all | solution.py:310
  14.9 0.0 copy-done
  14.9 0.0 copy-start.5
  14.9 0.1 shard_map.78
  15.0 0.4 collective-permute-start
  15.4 0.0 copy-start.2
  15.4 0.0 copy-start.3
  15.4 0.8 %collective-permute-done.got_ref = f32[2,128]{1,0:T(2,128)S(1)} collective-permute-done((f32[2,128]{1,0:T(2,128)S(1)}, f32[2,128]{1,0:T(2,128)S(1)}, u32[]{:S(2)}, u32[]{:S(2)}) %collective-permute-start) | collective-permute-done | bytes 1056 | tf_op jit(solution)/shard_map/ppermute | solution.py:340
  16.2 0.0 copy-done.2
  16.2 0.0 copy-done.3
  16.2 0.7 %copy-done.1 = s32[256]{0:T(256)S(1)} copy-done((s32[256]{0:T(256)S(1)}, s32[256]{0:T(256)}, u32[]{:S(2)}) %copy-start.1) | copy-done | bytes 1048
  16.9 0.1 shard_map.79
  17.0 0.3 collective-permute-start.1
  17.3 0.0 copy-done.4
  17.3 0.0 copy-done.5
  17.3 0.6 %shard_map.77 = (bf16[640,256]{1,0:T(8,128)(2,1)S(1)}, f32[2,40,128]{2,1,0:T(8,128)S(1)}, f32[2,264,128]{2,1,0:T(8,128)S(1)}, bf16[256,256]{1,0:T(8,128)(2,1)S(1)}) custom-call(s32[1]{0:T(128)S(6)} %and.5.part_ref, s32[1,256]{1,0:T(1,128)S(1)} %bitcast.22, f32[1,256]{1,0:T(1,128)S(1)} %bitcast.24, f32[1,256]{1,0:T(1,128)S(1)} %bitcast.26, ...), custom_call_target="tpu_custom_call" | custom-call | flops 1000000000 | bytes 2097152 | tf_op jit(solution)/shard_map/pallas_call | solution.py:313
  18.0 1.8 %collective-permute-done.1.edges_ref = f32[8,128]{1,0:T(8,128)S(1)} collective-permute-done((f32[8,128]{1,0:T(8,128)S(1)}, f32[8,128]{1,0:T(8,128)S(1)}, u32[]{:S(2)}, u32[]{:S(2)}) %collective-permute-start.1) | collective-permute-done | bytes 4128 | tf_op jit(solution)/shard_map/ppermute | solution.py:352
  19.8 0.1 shard_map.80
  19.9 2.7 %all-to-all-done = f32[64,8,128]{2,1,0:T(8,128)S(1)} async-done(((f32[64,8,128]{2,1,0:T(8,128)}), f32[64,8,128]{2,1,0:T(8,128)S(1)}, u32[]{:S(2)}, u32[]{:S(2)}) %all-to-all-start) | async-done | bytes 262176 | tf_op jit(solution)/shard_map/all_to_all | solution.py:310
  22.5 1.1 %shard_map.81 = f32[640,128]{1,0:T(8,128)S(1)} custom-call(s32[1]{0:T(128)} %bitcast.position_ref, f32[512,128]{1,0:T(8,128)S(1)} %bitcast.20, f32[2,264,128]{2,1,0:T(8,128)S(1)} %get-tuple-element.12.phase_ref, f32[4,128]{1,0:T(4,128)S(1)} %get-tuple-element.15.halo_ref, f32[2,72,128]{2,1,0:T(8,128)S(1)} %get-tuple-element.16.halo_phase_ref, ...), custom_call_target="tpu_custom_call" | custom-call | flops 1000000000 | bytes 2097152 | tf_op jit(solution)/shard_map/pallas_call | solution.py:362
  23.6 17.5 %all_to_all.10 = f32[64,5,2,128]{3,2,1,0:T(2,128)S(1)} all-to-all(f32[64,5,2,128]{3,2,1,0:T(2,128)S(1)} %bitcast.19), channel_id=1, replica_groups={{43,38,33,28,23,18,13,8,3,62,57,52,47,42,37,32,27,22,17,12,7,2,61,56,51..., dimensions={0} | all-to-all | bytes 655360 | tf_op jit(solution)/shard_map/all_to_all | solution.py:372
  41.1 1.0 %shard_map.82 = (f32[2,256,128]{2,1,0:T(8,128)}, f32[2,256,128]{2,1,0:T(8,128)}) custom-call(f32[640,128]{1,0:T(8,128)S(1)} %bitcast.16, bf16[256,256]{1,0:T(8,128)(2,1)S(1)} %get-tuple-element.19.matrix_ref), custom_call_target="tpu_custom_call" | custom-call | tf_op jit(solution)/shard_map/pallas_call | solution.py:375
  (1 shorter events, 0.0 us)
Async XLA Ops:
  0.6 14.2 %copy-start = (f32[2,1,256,128]{3,2,1,0:T(8,128)S(1)}, f32[2,1,256,128]{3,2,1,0:T(8,128)}, u32[]{:S(2)}) copy-start(f32[2,1,256,128]{3,2,1,0:T(8,128)} %param.6) | copy-start | bytes 786436
  0.6 16.7 %copy-start.4 = (bf16[640,256]{1,0:T(8,128)(2,1)S(1)}, bf16[640,256]{1,0:T(8,128)(2,1)}, u32[]{:S(2)}) copy-start(bf16[640,256]{1,0:T(8,128)(2,1)} %constant.21.clone.table_ref) | copy-start | bytes 983044
  0.7 21.9 %all-to-all-start = ((f32[64,8,128]{2,1,0:T(8,128)}), f32[64,8,128]{2,1,0:T(8,128)S(1)}, u32[]{:S(2)}, u32[]{:S(2)}) async-start(f32[64,8,128]{2,1,0:T(8,128)} %bitcast.17), calls=%async_computation | async-start | bytes 524288 | tf_op jit(solution)/shard_map/all_to_all | solution.py:310
  14.9 2.5 %copy-start.5 = (f32[128,128]{1,0:T(8,128)S(1)}, f32[128,128]{1,0:T(8,128)}, u32[]{:S(2)}) copy-start(f32[128,128]{1,0:T(8,128)} %constant.20.clone.compact_ref) | copy-start | bytes 196612
  15.0 1.2 %collective-permute-start = (f32[2,128]{1,0:T(2,128)S(1)}, f32[2,128]{1,0:T(2,128)S(1)}, u32[]{:S(2)}, u32[]{:S(2)}) collective-permute-start(f32[2,128]{1,0:T(2,128)S(1)} %get-tuple-element.14), channel_id=1, source_target_pairs={{0,1},{1,0},{2,3},{3,2},{4,5},{5,4},{6,7},{7,6},{8,9},{9,8},{10,11... | collective-permute-start | bytes 3080 | tf_op jit(solution)/shard_map/ppermute | solution.py:340
  15.4 0.8 %copy-start.2 = (f32[256]{0:T(256)S(1)}, f32[256]{0:T(256)}, u32[]{:S(2)}) copy-start(f32[256]{0:T(256)} %param.8) | copy-start | bytes 3076
  15.4 0.8 %copy-start.3 = (f32[256]{0:T(256)S(1)}, f32[256]{0:T(256)}, u32[]{:S(2)}) copy-start(f32[256]{0:T(256)} %param.9) | copy-start | bytes 3076
  16.2 0.7 %copy-start.1 = (s32[256]{0:T(256)S(1)}, s32[256]{0:T(256)}, u32[]{:S(2)}) copy-start(s32[256]{0:T(256)} %param.7) | copy-start | bytes 3076
  17.0 2.8 %collective-permute-start.1 = (f32[8,128]{1,0:T(8,128)S(1)}, f32[8,128]{1,0:T(8,128)S(1)}, u32[]{:S(2)}, u32[]{:S(2)}) collective-permute-start(f32[8,128]{1,0:T(8,128)S(1)} %shard_map.79), channel_id=1, source_target_pairs={{0,64},{1,0},{2,66},{3,2},{4,68},{5,4},{6,70},{7,6},{8,72},{9,8},{... | collective-permute-start | bytes 12296 | tf_op jit(solution)/shard_map/ppermute | solution.py:352

commit v8 on v7

--- a/solution.py
+++ b/solution.py
@@ -10,6 +10,7 @@
 from jax.sharding import PartitionSpec as P
 
 BLOCK = 128
+QUAD = 4
 THERE = (43, 5)
 BACK = (43, 59)
 VMEM = pl.BlockSpec(memory_space=pltpu.VMEM)
@@ -171,6 +172,10 @@
     return dot(back, stacked(blocks))
 
 
+def quad_place(position, groups):
+    return (position & 1) + 2 * (position // (groups // 4) & 1)
+
+
 def edge_kernel(position_ref, cells_ref, keep_out, give_out, tiles, sems):
     sets, row_count, width = cells_ref.shape
     depth = tiles.shape[2]
@@ -190,27 +195,32 @@
     give_out[...] = jnp.concatenate([jnp.where(is_odd, ours, theirs) for ours, theirs in zip(last, first, strict=True)], axis=0)
 
 
-def join_kernel(position_ref, whole_ref, frac_ref, _, keep_ref, got_ref, out_ref):
-    sets, width = keep_ref.shape
-    is_odd = position_ref[0] & 1 == 1
+def shift_kernel(position_ref, whole_ref, frac_ref, _, out_ref):
+    is_first = position_ref[0] & 1 == 1
     last = whole_ref.shape[1] - 1
-    out_ref[...] = jnp.zeros_like(out_ref)
-    out_ref[pl.ds(0, sets), :] = keep_ref[...]
-    out_ref[pl.ds(sets, sets), :] = got_ref[...]
     for place, ref in enumerate((whole_ref, frac_ref)):
-        shift = jnp.where(is_odd, ref[:, :1].astype(jnp.float32), ref[:, last:].astype(jnp.float32))
-        out_ref[pl.ds(2 * sets + place, 1), :] = jnp.broadcast_to(shift, (1, width))
-
-
-def halo_kernel(position_ref, block_ref, edges_ref, phase_out, halo_out, *, groups, rows, blocks):
+        shift = jnp.where(is_first, ref[:, :1].astype(jnp.float32), ref[:, last:].astype(jnp.float32))
+        out_ref[pl.ds(place, 1), :] = jnp.broadcast_to(shift, (1, out_ref.shape[1]))
+
+
+def join_kernel(position_ref, shift_ref, keep_ref, got_ref, near_out, far_out, *, groups):
+    is_second = quad_place(position_ref[0], groups) >= 2
+    fields = [jnp.concatenate([ref[field : field + 1, :] for ref in (keep_ref, got_ref)], axis=0) for field in range(2)]
+    near = jnp.where(is_second, fields[1], fields[0])
+    near_out[...] = jnp.concatenate([near, shift_ref[...]], axis=0)
+    far_out[...] = jnp.where(is_second, fields[0], fields[1])
+
+
+def halo_kernel(position_ref, block_ref, near_ref, far_ref, phase_out, halo_out, *, groups, rows, blocks):
     is_odd = position_ref[0] & 1 == 1
     is_end = jnp.where(is_odd, block_ref[0] == blocks - 1, block_ref[0] == 0)
-    cells = edges_ref[...]
-    sets = halo_out.shape[0] // 2
-    keep, got = cells[:sets], cells[sets : 2 * sets]
-    both = jnp.where(is_odd, jnp.concatenate([got, keep], axis=0), jnp.concatenate([keep, got], axis=0))
-    halo_out[...] = jnp.where(is_end, 0.0, both)
-    whole, frac = cells[2 * sets : 2 * sets + 1].astype(jnp.int32), cells[2 * sets + 1 : 2 * sets + 2]
+    near, far = [
+        jnp.where(is_odd, jnp.concatenate([ref[1:2, :], ref[:1, :]], axis=0), ref[:2, :]) for ref in (near_ref, far_ref)
+    ]
+    is_second = quad_place(position_ref[0], groups) >= 2
+    cells = jnp.where(is_second, jnp.concatenate([far, near], axis=0), jnp.concatenate([near, far], axis=0))
+    halo_out[...] = jnp.where(is_end, 0.0, cells)
+    whole, frac = near_ref[2:3, :].astype(jnp.int32), near_ref[3:4, :]
     width = phase_out.shape[2]
     half = groups // 2
     shape = (half, width)
@@ -221,31 +231,30 @@
     edge = half + groups * jnp.where(edge < width // 2, edge, edge - width)
     angle, edge_angle = [phase_angle(place, whole, frac, groups * width) for place in (signed, edge)]
     for part, wave in enumerate((jnp.cos, jnp.sin)):
-        shift = wave(angle)
-        for field in range(sets):
-            phase_out[part, pl.ds(field * half, half), :] = shift
-        phase_out[part, pl.ds(sets * half, rows), :] = wave(edge_angle)
+        phase_out[part, pl.ds(0, half), :] = wave(angle)
+        phase_out[part, pl.ds(half, rows), :] = wave(edge_angle)
 
 
 def shear_kernel(
     position_ref, signal_ref, phase_ref, halo_ref, halo_phase_ref, table_ref, twist_ref, out_ref, edge_ref,
     *, groups, rows,
 ):
-    sets = halo_ref.shape[0] // 2
-    pitch = rows + sets
+    pitch = rows + 1
     half = groups // 2
     signals = [signal_ref[pl.ds(row, groups, stride=rows), :] for row in range(rows)]
     width = signals[0].shape[1]
     first, step = THERE
     group = (first + step * lax.broadcasted_iota(jnp.int32, (groups, width), 0)) & (groups - 1)
-    group -= position_ref[0] & -2
-    for field in range(sets):
-        even, odd = halo_ref[field : field + 1, :], halo_ref[sets + field : sets + field + 1, :]
-        signals.append(jnp.where(group == 0, even, jnp.where(group == 1, odd, 0.0)))
+    far = groups // 4
+    base = position_ref[0] & groups - 1 - 1 - far
+    halo = jnp.zeros((groups, width), jnp.float32)
+    for place in range(QUAD):
+        halo = jnp.where(group == base + place % 2 + place // 2 * far, halo_ref[place : place + 1, :], halo)
+    signals.append(halo)
     shifts = []
     for part in range(2):
         ours, theirs = phase_ref[part], halo_phase_ref[part]
-        cut, halo_cut = rows * half, sets * half
+        cut, halo_cut = rows * half, half
         shifts.append(jnp.concatenate([ours[:cut], theirs[:halo_cut], ours[cut:], theirs[halo_cut:]], axis=0))
     signal = sheared(signals, table_ref, twist_ref, *shifts, edge_ref)
     for row in range(pitch):
@@ -266,11 +275,15 @@
     stores = [pltpu.make_async_copy(remapped, remapped_out, sems.at[field_count])]
     stores[0].start()
 
+    shares = cells_ref[pl.ds(rows, groups, stride=pitch), :]
+    first, step = BACK
+    group = (first + step * lax.broadcasted_iota(jnp.int32, (groups, width), 0)) & (groups - 1)
+    taken = quad_place(group, groups)
+
     def total(place):
-        return jnp.sum(cells_ref[pl.ds(place, groups // 2, stride=2 * pitch), :], axis=0, keepdims=True)
-
-    before = [total(back[0] % 2 * pitch + rows + field) for field in range(field_count)]
-    after = [total((1 - back[0] % 2) * pitch + rows + field) for field in range(field_count)]
+        return jnp.sum(jnp.where(taken == place, shares, 0.0), axis=0, keepdims=True)
+
+    before, after = [[total(2 * field + side) for field in range(field_count)] for side in range(2)]
 
     row = lax.broadcasted_iota(jnp.int32, (row_count, width), 0)
     for field in range(field_count):
@@ -338,27 +351,36 @@
         compiler_params=PARAMS,
     )(column, planes)
     got = lax.ppermute(give, "az", [(i, i ^ 1) for i in range(groups)])
-    edges = pl.pallas_call(
-        join_kernel,
-        out_shape=float_of((8, width)),
-        in_specs=[SMEM] + [VMEM] * 5,
+    shift = pl.pallas_call(
+        shift_kernel,
+        out_shape=float_of((2, width)),
+        in_specs=[SMEM] + [VMEM] * 3,
         out_specs=VMEM,
         compiler_params=PARAMS,
-    )(column, *shifts, keep, got)
+        cost_estimate=pl.CostEstimate(flops=10**8, transcendentals=0, bytes_accessed=2**20),
+    )(column, *shifts)
+    near, far = pl.pallas_call(
+        functools.partial(join_kernel, groups=groups),
+        out_shape=(float_of((4, width)), float_of((2, width))),
+        in_specs=[SMEM] + [VMEM] * 3,
+        out_specs=(VMEM,) * 2,
+        compiler_params=PARAMS,
+    )(column, shift, keep, got)
     turns = []
     for place in range(blocks * groups):
         step = -groups if place % 2 else groups
         turns.append((place, place + step if 0 <= place + step < blocks * groups else place ^ 1))
-    edges = lax.ppermute(edges, ("rad", "az"), turns)
+    near = lax.ppermute(near, ("rad", "az"), turns)
+    far = lax.ppermute(far, ("rad", "az"), [(place, other ^ groups // 4) for place, other in turns])
     halo_phases, halo = pl.pallas_call(
         functools.partial(halo_kernel, groups=groups, rows=rows, blocks=blocks),
-        out_shape=(float_of((2, sets * half + rows, width)), float_of((2 * sets, width))),
-        in_specs=[SMEM] * 2 + [VMEM],
+        out_shape=(float_of((2, half + rows, width)), float_of((QUAD, width))),
+        in_specs=[SMEM] * 2 + [VMEM] * 2,
         out_specs=(VMEM,) * 2,
         compiler_params=PARAMS,
         cost_estimate=pl.CostEstimate(flops=10**8, transcendentals=10**4, bytes_accessed=2**18),
-    )(column, block, edges)
-    pitch = rows + sets
+    )(column, block, near, far)
+    pitch = rows + 1
     signal = pl.pallas_call(
         functools.partial(shear_kernel, groups=groups, rows=rows),
         out_shape=float_of((groups * pitch, width)),
@@ -368,7 +390,7 @@
         compiler_params=PARAMS,
         cost_estimate=pl.CostEstimate(flops=10**9, transcendentals=0, bytes_accessed=2**21),
     )(column, signal.reshape(groups * rows, width), phases, halo, halo_phases, table, twist)
-    signal = signal.reshape(groups, pitch // 2, 2, width)
+    signal = signal.reshape(groups, pitch, 1, width)
     signal = lax.all_to_all(signal, "az", 0, 0, axis_index_groups=[listed(BACK, groups)], tiled=True)
     signal = signal.reshape(groups * pitch, width)
     whole_shape = (sets, row_count, width)

time: 42.3 us -> 41.6 us (0.983)
  waiting for transfers between devices: 5.27 us -> 4.12 us
  starting transfers between devices: 14.9 us -> 16 us
  blocking collectives: 17.5 us -> 16.8 us
    ppermute x1 -> x2, starting transfers between devices: 0.32 us -> 1.42 us  [the longest x1 1.33 us: on_device(): near = lax.ppermute(near, ('rad', 'az'), turns)]
    ppermute x1, waiting for transfers between devices: 0.82 us -> 0.01 us  [on_device(): got = lax.ppermute(give, 'az', [(i, i ^ 1) for i in range(groups)])]
    all_to_all x1, blocking collectives: 17.5 us -> 16.8 us  [on_device(): lax.all_to_all(signal, 'az', 0, 0, axis_index_groups=[listed(BACK, groups...]
    ppermute x1 -> x2, waiting for transfers between devices: 1.78 us -> 1.62 us  [the longest x1 1.61 us: on_device(): lax.ppermute(far, ('rad', 'az'), [(place, other ^ groups // 4) for place,...]
  transfers between devices with their start and end apart: 3 -> 4, of which waited for: 3 -> 2; matrix products, arithmetic and copies ran while one was open for 0% -> 0% of each run, Pallas kernels for 2% -> 2%
where the time goes in v8:
time: 41.6 us; the launch traced here: 41.4 us
  blocking collectives  16.8 us (40%)
  starting transfers between devices  16 us (38%)
  waiting for transfers between devices  4.12 us (10%)
  Pallas kernels  3 us (7%)
  between operations  0.72 us (2%)
  local copies, waits for them, and re-layouts  0.7 us (2%)
    all_to_all x1, blocking collectives, on_device(): lax.all_to_all(signal, 'az', 0, 0, axis_index_groups=[listed(BACK, groups...  16.8 us
    all_to_all x1, starting transfers between devices, on_device(): lax.all_to_all(fields.reshape(groups, rows, width), 'az', 0, 0, axis_inde...  14.2 us
    all_to_all x1, waiting for transfers between devices, on_device(): lax.all_to_all(fields.reshape(groups, rows, width), 'az', 0, 0, axis_inde...  2.5 us
    ppermute x1, waiting for transfers between devices, on_device(): lax.ppermute(far, ('rad', 'az'), [(place, other ^ groups // 4) for place,...  1.61 us
    ppermute x1, starting transfers between devices, on_device(): near = lax.ppermute(near, ('rad', 'az'), turns)  1.33 us
    pallas_call x1, Pallas kernels, on_device(): pl.pallas_call(functools.partial(shear_kernel, groups=groups, rows=rows),...  1.04 us
    pallas_call x1, Pallas kernels, on_device(): pl.pallas_call(functools.partial(derivative_kernel, groups=groups, rows=r...  0.99 us
  transfers between devices with their start and end apart: 4, of which 2 were waited for; matrix products, arithmetic and copies ran while one was open for 0% of the time, Pallas kernels for 2%

profile of v8, /device:TPU:1, one launch (start us, length us, event | category | flops | bytes accessed | tf_op | source)
XLA Modules:
  0.0 41.4 jit_solution(2966899803252946973)
XLA Ops:
  0.6 0.0 copy-start
  0.6 14.2 %all-to-all-start = ((f32[64,8,128]{2,1,0:T(8,128)}), f32[64,8,128]{2,1,0:T(8,128)S(1)}, u32[]{:S(2)}, u32[]{:S(2)}) async-start(f32[64,8,128]{2,1,0:T(8,128)} %bitcast.17), calls=%async_computation | async-start | bytes 524288 | tf_op jit(solution)/shard_map/all_to_all | solution.py:323
  14.9 0.0 copy-done
  14.9 0.0 copy-start.2
  14.9 0.0 copy-start.3
  14.9 0.0 copy-start.5
  14.9 0.1 shard_map.79
  15.0 0.4 collective-permute-start
  15.4 0.2 copy-done.2
  15.5 0.0 copy-done.3
  15.6 0.5 %copy-done.1 = s32[256]{0:T(256)S(1)} copy-done((s32[256]{0:T(256)S(1)}, s32[256]{0:T(256)}, u32[]{:S(2)}) %copy-start.1) | copy-done | bytes 1048
  16.1 0.1 shard_map.78.shift_ref
  16.2 0.0 collective-permute-done.got_ref
  16.2 0.1 collective-permute-start.2
  16.3 1.3 %collective-permute-start.1 = (f32[4,128]{1,0:T(4,128)S(1)}, f32[4,128]{1,0:T(4,128)S(1)}, u32[]{:S(2)}, u32[]{:S(2)}) collective-permute-start(f32[4,128]{1,0:T(4,128)S(1)} %get-tuple-element.17), channel_id=1, source_target_pairs={{0,64},{1,0},{2,66},{3,2},{4,68},{5,4},{6,70},{7,6},{8,72},{9,8},{... | collective-permute-start | bytes 6152 | tf_op jit(solution)/shard_map/ppermute | solution.py:373
  17.7 0.0 copy-done.5
  17.7 0.6 %shard_map.77 = (bf16[640,256]{1,0:T(8,128)(2,1)S(1)}, f32[2,40,128]{2,1,0:T(8,128)S(1)}, f32[2,264,128]{2,1,0:T(8,128)S(1)}, bf16[256,256]{1,0:T(8,128)(2,1)S(1)}) custom-call(s32[1]{0:T(128)S(6)} %and.5.part_ref, s32[1,256]{1,0:T(1,128)S(1)} %bitcast.22, f32[1,256]{1,0:T(1,128)S(1)} %bitcast.24, f32[1,256]{1,0:T(1,128)S(1)} %bitcast.26, ...), custom_call_target="tpu_custom_call" | custom-call | flops 1000000000 | bytes 2097152 | tf_op jit(solution)/shard_map/pallas_call | solution.py:326
  18.3 1.6 %collective-permute-done.2.far_ref = f32[2,128]{1,0:T(2,128)S(1)} collective-permute-done((f32[2,128]{1,0:T(2,128)S(1)}, f32[2,128]{1,0:T(2,128)S(1)}, u32[]{:S(2)}, u32[]{:S(2)}) %collective-permute-start.2) | collective-permute-done | bytes 1056 | tf_op jit(solution)/shard_map/ppermute | solution.py:374
  19.9 0.0 collective-permute-done.1.near_ref
  19.9 0.1 shard_map.81
  20.0 2.5 %all-to-all-done = f32[64,8,128]{2,1,0:T(8,128)S(1)} async-done(((f32[64,8,128]{2,1,0:T(8,128)}), f32[64,8,128]{2,1,0:T(8,128)S(1)}, u32[]{:S(2)}, u32[]{:S(2)}) %all-to-all-start) | async-done | bytes 262176 | tf_op jit(solution)/shard_map/all_to_all | solution.py:323
  22.5 1.0 %shard_map.82 = f32[576,128]{1,0:T(8,128)S(1)} custom-call(s32[1]{0:T(128)} %bitcast.position_ref, f32[512,128]{1,0:T(8,128)S(1)} %bitcast.20, f32[2,264,128]{2,1,0:T(8,128)S(1)} %get-tuple-element.14.phase_ref, f32[4,128]{1,0:T(4,128)S(1)} %get-tuple-element.19.halo_ref, f32[2,40,128]{2,1,0:T(8,128)S(1)} %get-tuple-element.20.halo_phase_ref, ...), custom_call_target="tpu_custom_call" | custom-call | flops 1000000000 | bytes 2097152 | tf_op jit(solution)/shard_map/pallas_call | solution.py:384
  23.6 16.8 %all_to_all.10 = f32[64,9,1,128]{3,2,1,0:T(1,128)S(1)} all-to-all(f32[64,9,1,128]{3,2,1,0:T(1,128)S(1)} %bitcast.19), channel_id=1, replica_groups={{43,38,33,28,23,18,13,8,3,62,57,52,47,42,37,32,27,22,17,12,7,2,61,56,51..., dimensions={0} | all-to-all | bytes 589824 | tf_op jit(solution)/shard_map/all_to_all | solution.py:394
  40.4 1.0 %shard_map.83 = (f32[2,256,128]{2,1,0:T(8,128)}, f32[2,256,128]{2,1,0:T(8,128)}) custom-call(f32[576,128]{1,0:T(8,128)S(1)} %bitcast.16, bf16[256,256]{1,0:T(8,128)(2,1)S(1)} %get-tuple-element.23.matrix_ref), custom_call_target="tpu_custom_call" | custom-call | tf_op jit(solution)/shard_map/pallas_call | solution.py:397
  (4 shorter events, 0.0 us)
Async XLA Ops:
  0.6 14.2 %copy-start = (f32[2,1,256,128]{3,2,1,0:T(8,128)S(1)}, f32[2,1,256,128]{3,2,1,0:T(8,128)}, u32[]{:S(2)}) copy-start(f32[2,1,256,128]{3,2,1,0:T(8,128)} %param.6) | copy-start | bytes 786436
  0.6 21.9 %all-to-all-start = ((f32[64,8,128]{2,1,0:T(8,128)}), f32[64,8,128]{2,1,0:T(8,128)S(1)}, u32[]{:S(2)}, u32[]{:S(2)}) async-start(f32[64,8,128]{2,1,0:T(8,128)} %bitcast.17), calls=%async_computation | async-start | bytes 524288 | tf_op jit(solution)/shard_map/all_to_all | solution.py:323
  14.9 0.7 %copy-start.2 = (f32[256]{0:T(256)S(1)}, f32[256]{0:T(256)}, u32[]{:S(2)}) copy-start(f32[256]{0:T(256)} %param.8) | copy-start | bytes 3076
  14.9 0.7 %copy-start.3 = (f32[256]{0:T(256)S(1)}, f32[256]{0:T(256)}, u32[]{:S(2)}) copy-start(f32[256]{0:T(256)} %param.9) | copy-start | bytes 3076
  14.9 2.8 %copy-start.5 = (f32[128,128]{1,0:T(8,128)S(1)}, f32[128,128]{1,0:T(8,128)}, u32[]{:S(2)}) copy-start(f32[128,128]{1,0:T(8,128)} %constant.20.clone.compact_ref) | copy-start | bytes 196612
  15.0 1.2 %collective-permute-start = (f32[2,128]{1,0:T(2,128)S(1)}, f32[2,128]{1,0:T(2,128)S(1)}, u32[]{:S(2)}, u32[]{:S(2)}) collective-permute-start(f32[2,128]{1,0:T(2,128)S(1)} %get-tuple-element.16), channel_id=1, source_target_pairs={{0,1},{1,0},{2,3},{3,2},{4,5},{5,4},{6,7},{7,6},{8,9},{9,8},{10,11... | collective-permute-start | bytes 3080 | tf_op jit(solution)/shard_map/ppermute | solution.py:353
  15.4 0.7 %copy-start.1 = (s32[256]{0:T(256)S(1)}, s32[256]{0:T(256)}, u32[]{:S(2)}) copy-start(s32[256]{0:T(256)} %param.7) | copy-start | bytes 3076
  15.4 2.3 %copy-start.4 = (bf16[640,256]{1,0:T(8,128)(2,1)S(1)}, bf16[640,256]{1,0:T(8,128)(2,1)}, u32[]{:S(2)}) copy-start(bf16[640,256]{1,0:T(8,128)(2,1)} %constant.21.clone.table_ref) | copy-start | bytes 983044
  16.2 3.7 %collective-permute-start.2 = (f32[2,128]{1,0:T(2,128)S(1)}, f32[2,128]{1,0:T(2,128)S(1)}, u32[]{:S(2)}, u32[]{:S(2)}) collective-permute-start(f32[2,128]{1,0:T(2,128)S(1)} %get-tuple-element.18), channel_id=1, source_target_pairs={{0,80},{1,16},{2,82},{3,18},{4,84},{5,20},{6,86},{7,22},{8,88},{9,... | collective-permute-start | bytes 3080 | tf_op jit(solution)/shard_map/ppermute | solution.py:374
  16.3 3.6 %collective-permute-start.1 = (f32[4,128]{1,0:T(4,128)S(1)}, f32[4,128]{1,0:T(4,128)S(1)}, u32[]{:S(2)}, u32[]{:S(2)}) collective-permute-start(f32[4,128]{1,0:T(4,128)S(1)} %get-tuple-element.17), channel_id=1, source_target_pairs={{0,64},{1,0},{2,66},{3,2},{4,68},{5,4},{6,70},{7,6},{8,72},{9,8},{... | collective-permute-start | bytes 6152 | tf_op jit(solution)/shard_map/ppermute | solution.py:373

commit v9 on v8

--- a/solution.py
+++ b/solution.py
@@ -268,12 +268,17 @@
     pitch = cells_ref.shape[0] // groups
     parts = row_count // rows
     there, back = listed(THERE, groups), listed(BACK, groups)
-    for place, group in enumerate(back):
-        part = there.index(group)
-        here = pl.ds(part % parts * rows, rows)
-        remapped[part // parts, here, :] = cells_ref[pl.ds(place * pitch, rows), :]
-    stores = [pltpu.make_async_copy(remapped, remapped_out, sems.at[field_count])]
-    stores[0].start()
+    stores = []
+
+    def store(source, target):
+        stores.append(pltpu.make_async_copy(source, target, sems.at[len(stores)]))
+        stores[-1].start()
+
+    for field in range(field_count):
+        for part in range(parts):
+            place = back.index(there[field * parts + part])
+            remapped[field, pl.ds(part * rows, rows), :] = cells_ref[pl.ds(place * pitch, rows), :]
+        store(remapped.at[field], remapped_out.at[field])
 
     shares = cells_ref[pl.ds(rows, groups, stride=pitch), :]
     first, step = BACK
@@ -300,10 +305,10 @@
             if start == row_count - BLOCK:
                 result += (matrix[0][:, -1:].astype(jnp.float32) + matrix[1][:, -1:].astype(jnp.float32)) * after[field]
             radial[field, here, :] = result
-        stores.append(pltpu.make_async_copy(radial.at[field], radial_out.at[field], sems.at[field]))
-        stores[-1].start()
-    for store in stores:
-        store.wait()
+            spot = (field, pl.ds(start, BLOCK))
+            store(radial.at[spot], radial_out.at[spot])
+    for copy in stores:
+        copy.wait()
 
 
 def on_device(fields, whole_shift, frac_shift, inv_spacing):
@@ -402,7 +407,7 @@
         scratch_shapes=[
             pltpu.VMEM(whole_shape, jnp.float32),
             pltpu.VMEM(whole_shape, jnp.float32),
-            pltpu.SemaphoreType.DMA((sets + 1,)),
+            pltpu.SemaphoreType.DMA((sets + sets * row_count // BLOCK,)),
         ],
         compiler_params=PARAMS,
     )(signal, matrix)

time: 41.6 us -> 41.6 us (level)
  no operation moved by 1% of the time
where the time goes in v9:
time: 41.6 us; the launch traced here: 41.4 us
  blocking collectives  16.8 us (40%)
  starting transfers between devices  16 us (38%)
  waiting for transfers between devices  4.12 us (10%)
  Pallas kernels  2.99 us (7%)
  between operations  0.72 us (2%)
  local copies, waits for them, and re-layouts  0.7 us (2%)
    all_to_all x1, blocking collectives, on_device(): lax.all_to_all(signal, 'az', 0, 0, axis_index_groups=[listed(BACK, groups...  16.8 us
    all_to_all x1, starting transfers between devices, on_device(): lax.all_to_all(fields.reshape(groups, rows, width), 'az', 0, 0, axis_inde...  14.2 us
    all_to_all x1, waiting for transfers between devices, on_device(): lax.all_to_all(fields.reshape(groups, rows, width), 'az', 0, 0, axis_inde...  2.5 us
    ppermute x1, waiting for transfers between devices, on_device(): lax.ppermute(far, ('rad', 'az'), [(place, other ^ groups // 4) for place,...  1.61 us
    ppermute x1, starting transfers between devices, on_device(): near = lax.ppermute(near, ('rad', 'az'), turns)  1.33 us
    pallas_call x1, Pallas kernels, on_device(): pl.pallas_call(functools.partial(shear_kernel, groups=groups, rows=rows),...  1.04 us
    pallas_call x1, Pallas kernels, on_device(): pl.pallas_call(functools.partial(derivative_kernel, groups=groups, rows=r...  0.99 us
  transfers between devices with their start and end apart: 4, of which 2 were waited for; matrix products, arithmetic and copies ran while one was open for 0% of the time, Pallas kernels for 2%

profile of v9, /device:TPU:1, one launch (start us, length us, event | category | flops | bytes accessed | tf_op | source)
XLA Modules:
  0.0 41.4 jit_solution(17617169942123784932)
XLA Ops:
  0.6 0.0 copy-start
  0.6 14.2 %all-to-all-start = ((f32[64,8,128]{2,1,0:T(8,128)}), f32[64,8,128]{2,1,0:T(8,128)S(1)}, u32[]{:S(2)}, u32[]{:S(2)}) async-start(f32[64,8,128]{2,1,0:T(8,128)} %bitcast.17), calls=%async_computation | async-start | bytes 524288 | tf_op jit(solution)/shard_map/all_to_all | solution.py:328
  14.9 0.0 copy-done
  14.9 0.0 copy-start.2
  14.9 0.0 copy-start.3
  14.9 0.0 copy-start.5
  14.9 0.1 shard_map.79
  15.0 0.4 collective-permute-start
  15.4 0.2 copy-done.2
  15.5 0.0 copy-done.3
  15.6 0.5 %copy-done.1 = s32[256]{0:T(256)S(1)} copy-done((s32[256]{0:T(256)S(1)}, s32[256]{0:T(256)}, u32[]{:S(2)}) %copy-start.1) | copy-done | bytes 1048
  16.1 0.1 shard_map.78.shift_ref
  16.2 0.0 collective-permute-done.got_ref
  16.2 0.1 collective-permute-start.2
  16.3 1.3 %collective-permute-start.1 = (f32[4,128]{1,0:T(4,128)S(1)}, f32[4,128]{1,0:T(4,128)S(1)}, u32[]{:S(2)}, u32[]{:S(2)}) collective-permute-start(f32[4,128]{1,0:T(4,128)S(1)} %get-tuple-element.17), channel_id=1, source_target_pairs={{0,64},{1,0},{2,66},{3,2},{4,68},{5,4},{6,70},{7,6},{8,72},{9,8},{... | collective-permute-start | bytes 6152 | tf_op jit(solution)/shard_map/ppermute | solution.py:378
  17.7 0.0 copy-done.5
  17.7 0.6 %shard_map.77 = (bf16[640,256]{1,0:T(8,128)(2,1)S(1)}, f32[2,40,128]{2,1,0:T(8,128)S(1)}, f32[2,264,128]{2,1,0:T(8,128)S(1)}, bf16[256,256]{1,0:T(8,128)(2,1)S(1)}) custom-call(s32[1]{0:T(128)S(6)} %and.5.part_ref, s32[1,256]{1,0:T(1,128)S(1)} %bitcast.22, f32[1,256]{1,0:T(1,128)S(1)} %bitcast.24, f32[1,256]{1,0:T(1,128)S(1)} %bitcast.26, ...), custom_call_target="tpu_custom_call" | custom-call | flops 1000000000 | bytes 2097152 | tf_op jit(solution)/shard_map/pallas_call | solution.py:331
  18.3 1.6 %collective-permute-done.2.far_ref = f32[2,128]{1,0:T(2,128)S(1)} collective-permute-done((f32[2,128]{1,0:T(2,128)S(1)}, f32[2,128]{1,0:T(2,128)S(1)}, u32[]{:S(2)}, u32[]{:S(2)}) %collective-permute-start.2) | collective-permute-done | bytes 1056 | tf_op jit(solution)/shard_map/ppermute | solution.py:379
  19.9 0.0 collective-permute-done.1.near_ref
  19.9 0.1 shard_map.81
  20.0 2.5 %all-to-all-done = f32[64,8,128]{2,1,0:T(8,128)S(1)} async-done(((f32[64,8,128]{2,1,0:T(8,128)}), f32[64,8,128]{2,1,0:T(8,128)S(1)}, u32[]{:S(2)}, u32[]{:S(2)}) %all-to-all-start) | async-done | bytes 262176 | tf_op jit(solution)/shard_map/all_to_all | solution.py:328
  22.5 1.0 %shard_map.82 = f32[576,128]{1,0:T(8,128)S(1)} custom-call(s32[1]{0:T(128)} %bitcast.position_ref, f32[512,128]{1,0:T(8,128)S(1)} %bitcast.20, f32[2,264,128]{2,1,0:T(8,128)S(1)} %get-tuple-element.14.phase_ref, f32[4,128]{1,0:T(4,128)S(1)} %get-tuple-element.19.halo_ref, f32[2,40,128]{2,1,0:T(8,128)S(1)} %get-tuple-element.20.halo_phase_ref, ...), custom_call_target="tpu_custom_call" | custom-call | flops 1000000000 | bytes 2097152 | tf_op jit(solution)/shard_map/pallas_call | solution.py:389
  23.6 16.8 %all_to_all.10 = f32[64,9,1,128]{3,2,1,0:T(1,128)S(1)} all-to-all(f32[64,9,1,128]{3,2,1,0:T(1,128)S(1)} %bitcast.19), channel_id=1, replica_groups={{43,38,33,28,23,18,13,8,3,62,57,52,47,42,37,32,27,22,17,12,7,2,61,56,51..., dimensions={0} | all-to-all | bytes 589824 | tf_op jit(solution)/shard_map/all_to_all | solution.py:399
  40.4 1.0 %shard_map.83 = (f32[2,256,128]{2,1,0:T(8,128)}, f32[2,256,128]{2,1,0:T(8,128)}) custom-call(f32[576,128]{1,0:T(8,128)S(1)} %bitcast.16, bf16[256,256]{1,0:T(8,128)(2,1)S(1)} %get-tuple-element.23.matrix_ref), custom_call_target="tpu_custom_call" | custom-call | tf_op jit(solution)/shard_map/pallas_call | solution.py:402
  (4 shorter events, 0.0 us)
Async XLA Ops:
  0.6 14.2 %copy-start = (f32[2,1,256,128]{3,2,1,0:T(8,128)S(1)}, f32[2,1,256,128]{3,2,1,0:T(8,128)}, u32[]{:S(2)}) copy-start(f32[2,1,256,128]{3,2,1,0:T(8,128)} %param.6) | copy-start | bytes 786436
  0.6 21.9 %all-to-all-start = ((f32[64,8,128]{2,1,0:T(8,128)}), f32[64,8,128]{2,1,0:T(8,128)S(1)}, u32[]{:S(2)}, u32[]{:S(2)}) async-start(f32[64,8,128]{2,1,0:T(8,128)} %bitcast.17), calls=%async_computation | async-start | bytes 524288 | tf_op jit(solution)/shard_map/all_to_all | solution.py:328
  14.9 0.7 %copy-start.2 = (f32[256]{0:T(256)S(1)}, f32[256]{0:T(256)}, u32[]{:S(2)}) copy-start(f32[256]{0:T(256)} %param.8) | copy-start | bytes 3076
  14.9 0.7 %copy-start.3 = (f32[256]{0:T(256)S(1)}, f32[256]{0:T(256)}, u32[]{:S(2)}) copy-start(f32[256]{0:T(256)} %param.9) | copy-start | bytes 3076
  14.9 2.8 %copy-start.5 = (f32[128,128]{1,0:T(8,128)S(1)}, f32[128,128]{1,0:T(8,128)}, u32[]{:S(2)}) copy-start(f32[128,128]{1,0:T(8,128)} %constant.20.clone.compact_ref) | copy-start | bytes 196612
  15.0 1.2 %collective-permute-start = (f32[2,128]{1,0:T(2,128)S(1)}, f32[2,128]{1,0:T(2,128)S(1)}, u32[]{:S(2)}, u32[]{:S(2)}) collective-permute-start(f32[2,128]{1,0:T(2,128)S(1)} %get-tuple-element.16), channel_id=1, source_target_pairs={{0,1},{1,0},{2,3},{3,2},{4,5},{5,4},{6,7},{7,6},{8,9},{9,8},{10,11... | collective-permute-start | bytes 3080 | tf_op jit(solution)/shard_map/ppermute | solution.py:358
  15.4 0.7 %copy-start.1 = (s32[256]{0:T(256)S(1)}, s32[256]{0:T(256)}, u32[]{:S(2)}) copy-start(s32[256]{0:T(256)} %param.7) | copy-start | bytes 3076
  15.4 2.3 %copy-start.4 = (bf16[640,256]{1,0:T(8,128)(2,1)S(1)}, bf16[640,256]{1,0:T(8,128)(2,1)}, u32[]{:S(2)}) copy-start(bf16[640,256]{1,0:T(8,128)(2,1)} %constant.21.clone.table_ref) | copy-start | bytes 983044
  16.2 3.7 %collective-permute-start.2 = (f32[2,128]{1,0:T(2,128)S(1)}, f32[2,128]{1,0:T(2,128)S(1)}, u32[]{:S(2)}, u32[]{:S(2)}) collective-permute-start(f32[2,128]{1,0:T(2,128)S(1)} %get-tuple-element.18), channel_id=1, source_target_pairs={{0,80},{1,16},{2,82},{3,18},{4,84},{5,20},{6,86},{7,22},{8,88},{9,... | collective-permute-start | bytes 3080 | tf_op jit(solution)/shard_map/ppermute | solution.py:379
  16.3 3.6 %collective-permute-start.1 = (f32[4,128]{1,0:T(4,128)S(1)}, f32[4,128]{1,0:T(4,128)S(1)}, u32[]{:S(2)}, u32[]{:S(2)}) collective-permute-start(f32[4,128]{1,0:T(4,128)S(1)} %get-tuple-element.17), channel_id=1, source_target_pairs={{0,64},{1,0},{2,66},{3,2},{4,68},{5,4},{6,70},{7,6},{8,72},{9,8},{... | collective-permute-start | bytes 6152 | tf_op jit(solution)/shard_map/ppermute | solution.py:378

commit v10 on v9

--- a/solution.py
+++ b/solution.py
@@ -12,7 +12,7 @@
 BLOCK = 128
 QUAD = 4
 THERE = (43, 5)
-BACK = (43, 59)
+BACK = (41, 59)
 VMEM = pl.BlockSpec(memory_space=pltpu.VMEM)
 SMEM = pl.BlockSpec(memory_space=pltpu.SMEM)
 HBM = pl.BlockSpec(memory_space=pltpu.HBM)

time: 41.6 us -> 41.7 us (level)
  no operation moved by 1% of the time
where the time goes in v10:
time: 41.7 us; the launch traced here: 41.4 us
  blocking collectives  16.9 us (41%)
  starting transfers between devices  16 us (38%)
  waiting for transfers between devices  4.12 us (10%)
  Pallas kernels  2.99 us (7%)
  between operations  0.72 us (2%)
  local copies, waits for them, and re-layouts  0.7 us (2%)
    all_to_all x1, blocking collectives, on_device(): lax.all_to_all(signal, 'az', 0, 0, axis_index_groups=[listed(BACK, groups...  16.9 us
    all_to_all x1, starting transfers between devices, on_device(): lax.all_to_all(fields.reshape(groups, rows, width), 'az', 0, 0, axis_inde...  14.2 us
    all_to_all x1, waiting for transfers between devices, on_device(): lax.all_to_all(fields.reshape(groups, rows, width), 'az', 0, 0, axis_inde...  2.5 us
    ppermute x1, waiting for transfers between devices, on_device(): lax.ppermute(far, ('rad', 'az'), [(place, other ^ groups // 4) for place,...  1.61 us
    ppermute x1, starting transfers between devices, on_device(): near = lax.ppermute(near, ('rad', 'az'), turns)  1.33 us
    pallas_call x1, Pallas kernels, on_device(): pl.pallas_call(functools.partial(shear_kernel, groups=groups, rows=rows),...  1.04 us
    pallas_call x1, Pallas kernels, on_device(): pl.pallas_call(functools.partial(derivative_kernel, groups=groups, rows=r...  0.99 us
  transfers between devices with their start and end apart: 4, of which 2 were waited for; matrix products, arithmetic and copies ran while one was open for 0% of the time, Pallas kernels for 2%

profile of v10, /device:TPU:1, one launch (start us, length us, event | category | flops | bytes accessed | tf_op | source)
XLA Modules:
  0.0 41.4 jit_solution(8755123955992023633)
XLA Ops:
  0.6 0.0 copy-start
  0.6 14.2 %all-to-all-start = ((f32[64,8,128]{2,1,0:T(8,128)}), f32[64,8,128]{2,1,0:T(8,128)S(1)}, u32[]{:S(2)}, u32[]{:S(2)}) async-start(f32[64,8,128]{2,1,0:T(8,128)} %bitcast.17), calls=%async_computation | async-start | bytes 524288 | tf_op jit(solution)/shard_map/all_to_all | solution.py:328
  14.9 0.0 copy-done
  14.9 0.0 copy-start.2
  14.9 0.0 copy-start.3
  14.9 0.0 copy-start.5
  14.9 0.1 shard_map.79
  15.0 0.4 collective-permute-start
  15.4 0.2 copy-done.2
  15.5 0.0 copy-done.3
  15.6 0.5 %copy-done.1 = s32[256]{0:T(256)S(1)} copy-done((s32[256]{0:T(256)S(1)}, s32[256]{0:T(256)}, u32[]{:S(2)}) %copy-start.1) | copy-done | bytes 1048
  16.1 0.1 shard_map.78.shift_ref
  16.2 0.0 collective-permute-done.got_ref
  16.2 0.1 collective-permute-start.2
  16.3 1.3 %collective-permute-start.1 = (f32[4,128]{1,0:T(4,128)S(1)}, f32[4,128]{1,0:T(4,128)S(1)}, u32[]{:S(2)}, u32[]{:S(2)}) collective-permute-start(f32[4,128]{1,0:T(4,128)S(1)} %get-tuple-element.17), channel_id=1, source_target_pairs={{0,64},{1,0},{2,66},{3,2},{4,68},{5,4},{6,70},{7,6},{8,72},{9,8},{... | collective-permute-start | bytes 6152 | tf_op jit(solution)/shard_map/ppermute | solution.py:378
  17.7 0.0 copy-done.4
  17.7 0.6 %shard_map.77 = (bf16[640,256]{1,0:T(8,128)(2,1)S(1)}, f32[2,40,128]{2,1,0:T(8,128)S(1)}, f32[2,264,128]{2,1,0:T(8,128)S(1)}, bf16[256,256]{1,0:T(8,128)(2,1)S(1)}) custom-call(s32[1]{0:T(128)S(6)} %and.5.part_ref, s32[1,256]{1,0:T(1,128)S(1)} %bitcast.22, f32[1,256]{1,0:T(1,128)S(1)} %bitcast.24, f32[1,256]{1,0:T(1,128)S(1)} %bitcast.26, ...), custom_call_target="tpu_custom_call" | custom-call | flops 1000000000 | bytes 2097152 | tf_op jit(solution)/shard_map/pallas_call | solution.py:331
  18.3 1.6 %collective-permute-done.2.far_ref = f32[2,128]{1,0:T(2,128)S(1)} collective-permute-done((f32[2,128]{1,0:T(2,128)S(1)}, f32[2,128]{1,0:T(2,128)S(1)}, u32[]{:S(2)}, u32[]{:S(2)}) %collective-permute-start.2) | collective-permute-done | bytes 1056 | tf_op jit(solution)/shard_map/ppermute | solution.py:379
  19.9 0.0 collective-permute-done.1.near_ref
  19.9 0.1 shard_map.81
  20.0 2.5 %all-to-all-done = f32[64,8,128]{2,1,0:T(8,128)S(1)} async-done(((f32[64,8,128]{2,1,0:T(8,128)}), f32[64,8,128]{2,1,0:T(8,128)S(1)}, u32[]{:S(2)}, u32[]{:S(2)}) %all-to-all-start) | async-done | bytes 262176 | tf_op jit(solution)/shard_map/all_to_all | solution.py:328
  22.5 1.0 %shard_map.82 = f32[576,128]{1,0:T(8,128)S(1)} custom-call(s32[1]{0:T(128)} %bitcast.position_ref, f32[512,128]{1,0:T(8,128)S(1)} %bitcast.20, f32[2,264,128]{2,1,0:T(8,128)S(1)} %get-tuple-element.14.phase_ref, f32[4,128]{1,0:T(4,128)S(1)} %get-tuple-element.19.halo_ref, f32[2,40,128]{2,1,0:T(8,128)S(1)} %get-tuple-element.20.halo_phase_ref, ...), custom_call_target="tpu_custom_call" | custom-call | flops 1000000000 | bytes 2097152 | tf_op jit(solution)/shard_map/pallas_call | solution.py:389
  23.6 16.9 %all_to_all.10 = f32[64,9,1,128]{3,2,1,0:T(1,128)S(1)} all-to-all(f32[64,9,1,128]{3,2,1,0:T(1,128)S(1)} %bitcast.19), channel_id=1, replica_groups={{41,36,31,26,21,16,11,6,1,60,55,50,45,40,35,30,25,20,15,10,5,0,59,54,49..., dimensions={0} | all-to-all | bytes 589824 | tf_op jit(solution)/shard_map/all_to_all | solution.py:399
  40.5 1.0 %shard_map.83 = (f32[2,256,128]{2,1,0:T(8,128)}, f32[2,256,128]{2,1,0:T(8,128)}) custom-call(f32[576,128]{1,0:T(8,128)S(1)} %bitcast.16, bf16[256,256]{1,0:T(8,128)(2,1)S(1)} %get-tuple-element.23.matrix_ref), custom_call_target="tpu_custom_call" | custom-call | tf_op jit(solution)/shard_map/pallas_call | solution.py:402
  (4 shorter events, 0.0 us)
Async XLA Ops:
  0.6 14.2 %copy-start = (f32[2,1,256,128]{3,2,1,0:T(8,128)S(1)}, f32[2,1,256,128]{3,2,1,0:T(8,128)}, u32[]{:S(2)}) copy-start(f32[2,1,256,128]{3,2,1,0:T(8,128)} %param.6) | copy-start | bytes 786436
  0.6 21.9 %all-to-all-start = ((f32[64,8,128]{2,1,0:T(8,128)}), f32[64,8,128]{2,1,0:T(8,128)S(1)}, u32[]{:S(2)}, u32[]{:S(2)}) async-start(f32[64,8,128]{2,1,0:T(8,128)} %bitcast.17), calls=%async_computation | async-start | bytes 524288 | tf_op jit(solution)/shard_map/all_to_all | solution.py:328
  14.9 0.7 %copy-start.2 = (f32[256]{0:T(256)S(1)}, f32[256]{0:T(256)}, u32[]{:S(2)}) copy-start(f32[256]{0:T(256)} %param.8) | copy-start | bytes 3076
  14.9 0.7 %copy-start.3 = (f32[256]{0:T(256)S(1)}, f32[256]{0:T(256)}, u32[]{:S(2)}) copy-start(f32[256]{0:T(256)} %param.9) | copy-start | bytes 3076
  14.9 2.8 %copy-start.5 = (f32[128,128]{1,0:T(8,128)S(1)}, f32[128,128]{1,0:T(8,128)}, u32[]{:S(2)}) copy-start(f32[128,128]{1,0:T(8,128)} %constant.20.clone.compact_ref) | copy-start | bytes 196612
  15.0 1.2 %collective-permute-start = (f32[2,128]{1,0:T(2,128)S(1)}, f32[2,128]{1,0:T(2,128)S(1)}, u32[]{:S(2)}, u32[]{:S(2)}) collective-permute-start(f32[2,128]{1,0:T(2,128)S(1)} %get-tuple-element.16), channel_id=1, source_target_pairs={{0,1},{1,0},{2,3},{3,2},{4,5},{5,4},{6,7},{7,6},{8,9},{9,8},{10,11... | collective-permute-start | bytes 3080 | tf_op jit(solution)/shard_map/ppermute | solution.py:358
  15.4 0.7 %copy-start.1 = (s32[256]{0:T(256)S(1)}, s32[256]{0:T(256)}, u32[]{:S(2)}) copy-start(s32[256]{0:T(256)} %param.7) | copy-start | bytes 3076
  15.4 2.3 %copy-start.4 = (bf16[640,256]{1,0:T(8,128)(2,1)S(1)}, bf16[640,256]{1,0:T(8,128)(2,1)}, u32[]{:S(2)}) copy-start(bf16[640,256]{1,0:T(8,128)(2,1)} %constant.21.clone.table_ref) | copy-start | bytes 983044
  16.2 3.7 %collective-permute-start.2 = (f32[2,128]{1,0:T(2,128)S(1)}, f32[2,128]{1,0:T(2,128)S(1)}, u32[]{:S(2)}, u32[]{:S(2)}) collective-permute-start(f32[2,128]{1,0:T(2,128)S(1)} %get-tuple-element.18), channel_id=1, source_target_pairs={{0,80},{1,16},{2,82},{3,18},{4,84},{5,20},{6,86},{7,22},{8,88},{9,... | collective-permute-start | bytes 3080 | tf_op jit(solution)/shard_map/ppermute | solution.py:379
  16.3 3.6 %collective-permute-start.1 = (f32[4,128]{1,0:T(4,128)S(1)}, f32[4,128]{1,0:T(4,128)S(1)}, u32[]{:S(2)}, u32[]{:S(2)}) collective-permute-start(f32[4,128]{1,0:T(4,128)S(1)} %get-tuple-element.17), channel_id=1, source_target_pairs={{0,64},{1,0},{2,66},{3,2},{4,68},{5,4},{6,70},{7,6},{8,72},{9,8},{... | collective-permute-start | bytes 6152 | tf_op jit(solution)/shard_map/ppermute | solution.py:378
